TPU v7x, 1024 devices: a whole 8x8x8 slice. The times are simulated.
1024 devices in a mesh: dom: 128 (over x, y, core), col: 8 (over z).
Axes of the slice: x: 8, y: 8, z: 8, core: 2. Of those that a mesh axis runs over, the one named last changes fastest.
Arguments:
- states: bfloat16 [256, 131072], P('col', 'dom'), may hold values from -6 to 6
- diag_blocks: bfloat16 [131072, 1024], P('dom'), may hold values from -0.1875 to 0.1875
- coupling: bfloat16 [131072, 1024], P('dom'), may hold values from -0.1875 to 0.1875
- counts: int32 [128], P('dom'), may hold values from 512 to 1024, as said below
Outputs:
- basis: float32 [256, 131072], P('col', 'dom')
- reduced: float32 [256, 256], replicated
Inputs may be any that keep to these rules, and one draw needn't show every extreme that they name: `counts`: each domain uses between 512 and 1024 slots; one domain uses all 1024.
All inputs are finite; a program needn't handle non-finite values.
Results may differ from a plain program's by a relative error of at most 0.0046.
Values may be sent and summed in bfloat16 or wider, within the bound.
No kernel may reach another device: no remote copies, remote signals or barrier semaphores. Data moves between devices by JAX's collectives and lax.ppermute only.
A program may use at most 32 MiB of HBM per device.

v0:
```python
import math

import jax
import jax.numpy as jnp
from jax import lax
from jax.sharding import PartitionSpec as P

DEGREE = 3


HIGH = lax.Precision.HIGHEST
CENTER = 0.5
HALF = 2.0
TRANSPOSED = (((1,), (1,)), ((), ()))


def passed_along(array, axis, by):
    count = lax.axis_size(axis)
    pairs = [(i, i + by) for i in range(count) if 0 <= i + by < count]
    return lax.ppermute(array, axis, pairs)


def body(states, diag_blocks, coupling, counts):
    rows = diag_blocks.shape[1]
    local_states = states.shape[0]
    live = (lax.iota(jnp.int32, rows) < counts[0]).astype(jnp.float32)[None, :]

    def apply_op(block):
        own = jnp.dot(block, diag_blocks, preferred_element_type=jnp.float32)
        own_t = lax.dot_general(block, diag_blocks, TRANSPOSED, preferred_element_type=jnp.float32)
        onward = jnp.dot(block, coupling, preferred_element_type=jnp.float32)
        from_prev = passed_along(onward, "dom", 1)
        next_block = passed_along(block, "dom", -1)
        from_next = lax.dot_general(
            next_block, coupling, TRANSPOSED, preferred_element_type=jnp.float32
        )
        return live * (0.5 * (own + own_t) + from_prev + from_next)

    first = live * states.astype(jnp.float32)
    prev = first
    cur = (apply_op(first.astype(jnp.bfloat16)) - CENTER * first) / HALF
    for step in range(DEGREE - 1):
        nxt = 2.0 * (apply_op(cur.astype(jnp.bfloat16)) - CENTER * cur) / HALF - prev
        prev = cur
        cur = nxt
    filtered = cur.astype(jnp.bfloat16)
    image = apply_op(filtered).astype(jnp.bfloat16)
    all_states, all_image = (
        lax.all_gather(filtered, "col", axis=0, tiled=True),
        lax.all_gather(image, "col", axis=0, tiled=True),
    )
    gram_term = lax.dot_general(
        all_states, all_states, TRANSPOSED, preferred_element_type=jnp.float32
    )
    proj_term = lax.dot_general(
        all_states, all_image, TRANSPOSED, preferred_element_type=jnp.float32
    )
    gram, proj = lax.psum((gram_term, proj_term), "dom")
    total = gram.shape[0]
    lower = jnp.linalg.cholesky(gram)
    inverse = lax.linalg.triangular_solve(
        lower, jnp.eye(total, dtype=jnp.float32), left_side=True, lower=True
    )
    reduced = jnp.dot(jnp.dot(inverse, proj, precision=HIGH), inverse.T, precision=HIGH)
    start = lax.axis_index("col") * local_states
    inverse_rows = lax.dynamic_slice_in_dim(inverse, start, local_states, 0)
    scale = math.sqrt(lax.axis_size("dom") * rows)
    basis = scale * jnp.dot(inverse_rows, all_states.astype(jnp.float32), precision=HIGH)
    return (basis, reduced)


def solution(mesh):
    placed = (P("col", "dom"), P("dom", None), P("dom", None), P("dom"))
    return jax.shard_map(
        body, mesh=mesh, in_specs=placed, out_specs=(P("col", "dom"), P()), check_vma=False
    )
```

profile of v0, /device:TPU:1, one launch (start us, length us, event | category | flops | bytes accessed | tf_op | source)
XLA Modules:
  0.0 403.5 jit_solution(13311612794290132068)
XLA Ops:
  8.0 2.2 fusion.36
  10.3 4.7 %collective-permute-start = (f32[32,1024]{1,0:T(8,128)S(1)}, f32[32,1024]{1,0:T(8,128)S(1)}, u32[]{:S(2)}, u32[]{:S(2)}) collective-permute-start(f32[32,1024]{1,0:T(8,128)S(1)} %fusion.36), channel_id=1, source_target_pairs={{0,8},{8,16},{16,24},{24,32},{32,40},{40,48},{48,56},{56,64},{64,7... | collective-permute-start | bytes 393224 | tf_op jit(solution)/shard_map/ppermute | solution.py:20
  15.0 12.7 %collective-permute-start.1 = (bf16[32,1024]{1,0:T(8,128)(2,1)S(1)}, bf16[32,1024]{1,0:T(8,128)(2,1)S(1)}, u32[]{:S(2)}, u32[]{:S(2)}) collective-permute-start(bf16[32,1024]{1,0:T(8,128)(2,1)S(1)} %fusion.26), channel_id=1, source_target_pairs={{8,0},{16,8},{24,16},{32,24},{40,32},{48,40},{56,48},{64,56},{72,6... | collective-permute-start | bytes 196616 | tf_op jit(solution)/shard_map/ppermute | solution.py:20
  27.7 0.5 fusion.39
  28.2 0.4 collective-permute-done.1
  28.6 0.7 fusion.48
  29.3 0.8 multiply_convert_fusion
  30.1 0.5 fusion.50
  30.5 2.3 collective-permute-start.3
  32.8 0.5 fusion.49
  33.3 3.3 collective-permute-start.2
  36.6 0.7 fusion.51
  37.3 1.2 collective-permute-done.2
  38.5 0.7 fusion.47
  39.2 0.5 fusion.53
  39.7 1.9 collective-permute-start.5
  41.6 0.5 fusion.52
  42.1 4.4 %collective-permute-start.4 = (f32[32,1024]{1,0:T(8,128)S(1)}, f32[32,1024]{1,0:T(8,128)S(1)}, u32[]{:S(2)}, u32[]{:S(2)}) collective-permute-start(f32[32,1024]{1,0:T(8,128)S(1)} %fusion.53), channel_id=1, source_target_pairs={{0,8},{8,16},{16,24},{24,32},{32,40},{40,48},{48,56},{56,64},{64,7... | collective-permute-start | bytes 393224 | tf_op jit(solution)/shard_map/ppermute | solution.py:20
  46.5 0.7 fusion.54
  47.2 1.2 collective-permute-done.4
  48.4 0.8 fusion.21
  49.1 0.5 fusion.57
  49.6 1.9 collective-permute-start.7
  51.5 0.5 fusion.56
  52.0 24.1 %all_gather.6 = bf16[256,1024]{1,0:T(8,128)(2,1)S(1)} all-gather(bf16[32,1024]{1,0:T(8,128)(2,1)S(1)} %fusion.21), channel_id=1, replica_groups=mesh['dom'=128,'col'=8] {'col'}, dimensions={0}, use_global_device_ids=true | all-gather | bytes 589824 | tf_op jit(solution)/shard_map/all_gather | solution.py:49
  76.1 10.1 %collective-permute-start.6 = (f32[32,1024]{1,0:T(8,128)S(1)}, f32[32,1024]{1,0:T(8,128)S(1)}, u32[]{:S(2)}, u32[]{:S(2)}) collective-permute-start(f32[32,1024]{1,0:T(8,128)S(1)} %fusion.57), channel_id=1, source_target_pairs={{0,8},{8,16},{16,24},{24,32},{32,40},{40,48},{48,56},{56,64},{64,7... | collective-permute-start | bytes 393224 | tf_op jit(solution)/shard_map/ppermute | solution.py:20
  86.2 1.0 fusion.55
  87.2 0.7 fusion.58
  88.1 0.7 fusion.22
  88.9 20.2 %all_gather.7 = bf16[256,1024]{1,0:T(8,128)(2,1)S(1)} all-gather(bf16[32,1024]{1,0:T(8,128)(2,1)S(1)} %fusion.22), channel_id=1, replica_groups=mesh['dom'=128,'col'=8] {'col'}, dimensions={0}, use_global_device_ids=true | all-gather | bytes 589824 | tf_op jit(solution)/shard_map/all_gather | solution.py:50
  109.1 1.0 fusion.59
  110.2 217.9 %all-reduce.4.cloned.1.call-done = (f32[256,256]{0,1:T(8,128)}, f32[256,256]{1,0:T(8,128)}) async-done(((f32[256,256]{0,1:T(8,128)}, f32[256,256]{1,0:T(8,128)}), (f32[256,256]{0,1:T(8,128)}, f32[256,256]{1,0:T(8,128)})) %all-reduce.4.cloned.1.call-update) | async-done | bytes 524304 | tf_op jit(solution)/shard_map/psum | solution.py:58
  328.1 1.1 copy.7
  329.2 1.0 fusion.23
  330.2 11.7 %cholesky.50 = f32[128,128]{1,0:T(8,128)S(1)} custom-call(f32[128,128]{1,0:T(8,128)S(1)} %cholesky.118), custom_call_target="Cholesky" | custom-call | tf_op jit(solution)/shard_map/jit(cholesky)/cholesky | solution.py:60
  341.9 0.7 select_reduce_fusion.1
  342.6 10.6 %custom-call.14 = f32[1,128,128]{1,2,0:T(8,128)S(1)} custom-call(f32[1,128,128]{2,1,0:T(8,128)} %get-tuple-element.25), custom_call_target="InvertDiagBlocksLowerTriangular" | custom-call | tf_op jit(solution)/shard_map/jit(cholesky)/cholesky | solution.py:60
  353.8 11.7 %cholesky.105 = f32[128,128]{1,0:T(8,128)S(1)} custom-call(f32[128,128]{1,0:T(8,128)S(1)} %convolution_subtract_fusion.1), custom_call_target="Cholesky" | custom-call | tf_op jit(solution)/shard_map/jit(cholesky)/cholesky | solution.py:60
  365.5 0.6 compare_reduce_fusion
  367.5 5.2 %while.1 = (s32[]{:T(128)}, f32[256,256]{1,0:T(8,128)S(1)}, s32[2,2]{1,0:T(2,128)S(1)}, f32[2,128,128]{2,1,0:T(8,128)}, s32[]{:T(128)}) while((s32[]{:T(128)}, f32[256,256]{1,0:T(8,128)S(1)}, s32[2,2]{1,0:T(2,128)S(1)}, f32[2,128,128]{2,1,0:T(8,128)}, s32[]{:T(128)}) %tuple.29), condition=%wide.while_cond, body=%wide.while_body.sunk | while | flops 2 | bytes 132705 | solution.py:61
  367.7 0.6 fusion.101
  368.3 1.9 bitcast_dynamic-update-slice_fusion.2
  370.2 0.6 fusion.101
  370.8 1.9 bitcast_dynamic-update-slice_fusion.2
  372.7 20.5 %custom-call.15 = f32[2,128,128]{1,2,0:T(8,128)S(1)} custom-call(f32[2,128,128]{2,1,0:T(8,128)} %get-tuple-element.9), custom_call_target="InvertDiagBlocksLowerTriangular" | custom-call | tf_op jit(solution)/shard_map/triangular_solve | solution.py:61
  394.1 0.4 fusion.24
  394.5 1.1 fusion.25
  395.6 1.0 convolution_multiply_fusion
  (32 shorter events, 1.8 us)
Async XLA Ops:
  7.2 20.5 %copy-start = (bf16[1024,1024]{1,0:T(8,128)(2,1)S(1)}, bf16[1024,1024]{1,0:T(8,128)(2,1)}, u32[]{:S(2)}) copy-start(bf16[1024,1024]{1,0:T(8,128)(2,1)} %param.5) | copy-start | bytes 6291460
  7.2 7.8 %copy-start.2 = (bf16[32,1024]{1,0:T(8,128)(2,1)S(1)}, bf16[32,1024]{1,0:T(8,128)(2,1)}, u32[]{:S(2)}) copy-start(bf16[32,1024]{1,0:T(8,128)(2,1)} %param.4) | copy-start | bytes 196612
  7.2 320.9 %all-reduce.4.cloned.1.call-start = ((), (), s32[]{:S(2)}) async-start(), calls=%async_computation | async-start | bytes 1048576 | tf_op jit(solution)/shard_map/psum | solution.py:58
  8.0 20.5 %copy-start.1 = (bf16[1024,1024]{1,0:T(8,128)(2,1)S(1)}, bf16[1024,1024]{1,0:T(8,128)(2,1)}, u32[]{:S(2)}) copy-start(bf16[1024,1024]{1,0:T(8,128)(2,1)} %param.6) | copy-start | bytes 6291460
  10.3 19.0 %collective-permute-start = (f32[32,1024]{1,0:T(8,128)S(1)}, f32[32,1024]{1,0:T(8,128)S(1)}, u32[]{:S(2)}, u32[]{:S(2)}) collective-permute-start(f32[32,1024]{1,0:T(8,128)S(1)} %fusion.36), channel_id=1, source_target_pairs={{0,8},{8,16},{16,24},{24,32},{32,40},{40,48},{48,56},{56,64},{64,7... | collective-permute-start | bytes 393224 | tf_op jit(solution)/shard_map/ppermute | solution.py:20
  15.0 13.5 %collective-permute-start.1 = (bf16[32,1024]{1,0:T(8,128)(2,1)S(1)}, bf16[32,1024]{1,0:T(8,128)(2,1)S(1)}, u32[]{:S(2)}, u32[]{:S(2)}) collective-permute-start(bf16[32,1024]{1,0:T(8,128)(2,1)S(1)} %fusion.26), channel_id=1, source_target_pairs={{8,0},{16,8},{24,16},{32,24},{40,32},{48,40},{56,48},{64,56},{72,6... | collective-permute-start | bytes 196616 | tf_op jit(solution)/shard_map/ppermute | solution.py:20
  30.5 6.0 %collective-permute-start.3 = (bf16[32,1024]{1,0:T(8,128)(2,1)S(1)}, bf16[32,1024]{1,0:T(8,128)(2,1)S(1)}, u32[]{:S(2)}, u32[]{:S(2)}) collective-permute-start(bf16[32,1024]{1,0:T(8,128)(2,1)S(1)} %get-tuple-element.26), channel_id=1, source_target_pairs={{8,0},{16,8},{24,16},{32,24},{40,32},{48,40},{56,48},{64,56},{72,6... | collective-permute-start | bytes 196616 | tf_op jit(solution)/shard_map/ppermute | solution.py:20
  33.3 5.2 %collective-permute-start.2 = (f32[32,1024]{1,0:T(8,128)S(1)}, f32[32,1024]{1,0:T(8,128)S(1)}, u32[]{:S(2)}, u32[]{:S(2)}) collective-permute-start(f32[32,1024]{1,0:T(8,128)S(1)} %fusion.50), channel_id=1, source_target_pairs={{0,8},{8,16},{16,24},{24,32},{32,40},{40,48},{48,56},{56,64},{64,7... | collective-permute-start | bytes 393224 | tf_op jit(solution)/shard_map/ppermute | solution.py:20
  39.7 6.8 %collective-permute-start.5 = (bf16[32,1024]{1,0:T(8,128)(2,1)S(1)}, bf16[32,1024]{1,0:T(8,128)(2,1)S(1)}, u32[]{:S(2)}, u32[]{:S(2)}) collective-permute-start(bf16[32,1024]{1,0:T(8,128)(2,1)S(1)} %get-tuple-element.28), channel_id=1, source_target_pairs={{8,0},{16,8},{24,16},{32,24},{40,32},{48,40},{56,48},{64,56},{72,6... | collective-permute-start | bytes 196616 | tf_op jit(solution)/shard_map/ppermute | solution.py:20
  42.1 6.3 %collective-permute-start.4 = (f32[32,1024]{1,0:T(8,128)S(1)}, f32[32,1024]{1,0:T(8,128)S(1)}, u32[]{:S(2)}, u32[]{:S(2)}) collective-permute-start(f32[32,1024]{1,0:T(8,128)S(1)} %fusion.53), channel_id=1, source_target_pairs={{0,8},{8,16},{16,24},{24,32},{32,40},{40,48},{48,56},{56,64},{64,7... | collective-permute-start | bytes 393224 | tf_op jit(solution)/shard_map/ppermute | solution.py:20
  49.6 37.6 %collective-permute-start.7 = (bf16[32,1024]{1,0:T(8,128)(2,1)S(1)}, bf16[32,1024]{1,0:T(8,128)(2,1)S(1)}, u32[]{:S(2)}, u32[]{:S(2)}) collective-permute-start(bf16[32,1024]{1,0:T(8,128)(2,1)S(1)} %fusion.21), channel_id=1, source_target_pairs={{8,0},{16,8},{24,16},{32,24},{40,32},{48,40},{56,48},{64,56},{72,6... | collective-permute-start | bytes 196616 | tf_op jit(solution)/shard_map/ppermute | solution.py:20
  76.1 12.0 %collective-permute-start.6 = (f32[32,1024]{1,0:T(8,128)S(1)}, f32[32,1024]{1,0:T(8,128)S(1)}, u32[]{:S(2)}, u32[]{:S(2)}) collective-permute-start(f32[32,1024]{1,0:T(8,128)S(1)} %fusion.57), channel_id=1, source_target_pairs={{0,8},{8,16},{16,24},{24,32},{32,40},{40,48},{48,56},{56,64},{64,7... | collective-permute-start | bytes 393224 | tf_op jit(solution)/shard_map/ppermute | solution.py:20
  329.2 64.9 %copy-start.3 = (f32[256,256]{1,0:T(8,128)S(1)}, f32[256,256]{1,0:T(8,128)}, u32[]{:S(2)}) copy-start(f32[256,256]{1,0:T(8,128)} %get-tuple-element.19) | copy-start | bytes 786436
Sparse Core Ops, SparseCore 0:
  110.3 217.7 all-reduce.3
where the time goes:
time: 405 us; the launch traced here: 403 us
  waiting for transfers between devices  221 us (55%)
  other arithmetic  57 us (14%)
  blocking collectives  44.3 us (11%)
  starting transfers between devices  41.2 us (10%)
  matrix products  17.2 us (4%)
  between operations  16.4 us (4%)
  local copies, waits for them, and re-layouts  6.26 us (2%)
    psum x1, waiting for transfers between devices, body(): gram, proj = lax.psum((gram_term, proj_term), 'dom')  218 us
    ppermute x8, starting transfers between devices, passed_along(): return lax.ppermute(array, axis, pairs)  41.2 us
    another operation x6, other arithmetic, body(): lower = jnp.linalg.cholesky(gram)  35.4 us
    all_gather x1, blocking collectives, body(): lax.all_gather(filtered, 'col', axis=0, tiled=True)  24.1 us
    another operation x3, other arithmetic, body(): lax.linalg.triangular_solve(lower, jnp.eye(total, dtype=jnp.float32), lef...  20.5 us
    all_gather x1, blocking collectives, body(): lax.all_gather(image, 'col', axis=0, tiled=True)  20.2 us
  transfers between devices with their start and end apart: 9, of which 5 were waited for; matrix products, arithmetic and copies ran while one was open for 1% of the time, Pallas kernels for 0%

commit v1 on v0

v1 whole, which is shorter than its diff:
```python
import math

import jax
import jax.numpy as jnp
from jax import lax
from jax.experimental import pallas as pl
from jax.experimental.pallas import tpu as pltpu
from jax.sharding import Mesh
from jax.sharding import PartitionSpec as P

DEGREE = 3
HIGH = lax.Precision.HIGHEST
CENTER = 0.5
HALF = 2.0
TRANSPOSED = (((1,), (1,)), ((), ()))
FIRST_WITH_FIRST = (((0,), (0,)), ((), ()))
ALONG_X, ALONG_Y, CORES = 8, 8, 2
DOM = ("x", "y", "core")
WIDE = 64
F32 = jnp.float32
BF16 = jnp.bfloat16


def factor_rows(block, wide):
    done = []
    rest = block
    for start in range(0, wide, 8):
        cols = [
            jnp.broadcast_to(rest[:, start + q : start + q + 1], rest.shape) for q in range(8)
        ]
        rows = [rest[q : q + 1, :] for q in range(8)]
        scaled = []
        for p in range(8):
            pivot = cols[p][p : p + 1, :]
            inv = 1.0 / pivot
            scaled.append(rows[p] * inv)
            for q in range(p + 1, 8):
                link = cols[p][q : q + 1, :]
                rows[q] = rows[q] - link * scaled[p]
                cols[q] = cols[q] - cols[p] * (link * inv)
            done.append(rows[p] * lax.rsqrt(pivot))
        if start + 8 < wide:
            change = cols[0][8:, :] * scaled[0]
            for p in range(1, 8):
                change = change + cols[p][8:, :] * scaled[p]
            rest = rest[8:, :] - change
    return jnp.concatenate(done, axis=0)


def cholesky_inverse(a_ref, x_ref, inv_ref):
    n, w = a_ref.shape[0], WIDE
    i = lax.broadcasted_iota(jnp.int32, (n, n), 0)
    j = lax.broadcasted_iota(jnp.int32, (n, n), 1)
    x_ref[...] = (i == j).astype(F32)
    eye = x_ref[:w, :w]
    for s in range(0, n, w):
        here = slice(s, s + w)
        block = factor_rows(jnp.concatenate([a_ref[here, here], eye], axis=1), w)
        both = jnp.concatenate([a_ref[here, :], x_ref[here, :]], axis=1)
        out = jnp.dot(block[:, w:], both, precision=HIGH, preferred_element_type=F32)
        inv_ref[here, :] = out[:, n:]
        if s + w < n:
            change = lax.dot_general(
                out[:, s + w : n], out, FIRST_WITH_FIRST, precision=HIGH, preferred_element_type=F32
            )
            a_ref[s + w :, :] = a_ref[s + w :, :] - change[:, :n]
            x_ref[s + w :, :] = x_ref[s + w :, :] - change[:, n:]


def finish_kernel(col_ref, sums_ref, all_ref, basis_ref, reduced_ref, a_ref, q_ref, x_ref, inv_ref):
    tiles, cols, eight, lanes = sums_ref.shape
    local = basis_ref.shape[0]
    per_matrix = tiles // 2
    halves = a_ref.shape[1] // lanes
    for t in range(tiles):
        target = a_ref if t < per_matrix else q_ref
        block, half = divmod(t % per_matrix, halves)
        for z in range(cols):
            top = z * local + block * eight
            target[top : top + eight, half * lanes : (half + 1) * lanes] = sums_ref[t, z]
    cholesky_inverse(a_ref, x_ref, inv_ref)
    proj = q_ref[...]
    proj = 0.5 * (proj + proj.T)
    inverse = inv_ref[...]
    left = jnp.dot(inverse, proj, precision=HIGH, preferred_element_type=F32)
    reduced_ref[...] = lax.dot_general(
        left, inverse, TRANSPOSED, precision=HIGH, preferred_element_type=F32
    )
    scale = math.sqrt(ALONG_X * ALONG_Y * CORES * basis_ref.shape[1])
    mine = scale * inv_ref[pl.ds(pl.multiple_of(col_ref[0] * local, local), local), :]
    high = mine.astype(BF16)
    low = (mine - high.astype(F32)).astype(BF16)
    states = all_ref[...]
    basis_ref[...] = jnp.dot(high, states, preferred_element_type=F32) + jnp.dot(
        low, states, preferred_element_type=F32
    )


def finish(col, sums, all_states, local):
    total, rows = all_states.shape
    vmem = pl.BlockSpec(memory_space=pltpu.VMEM)
    square = pltpu.VMEM((total, total), F32)
    return pl.pallas_call(
        finish_kernel,
        out_shape=(
            jax.ShapeDtypeStruct((local, rows), F32),
            jax.ShapeDtypeStruct((total, total), F32),
        ),
        in_specs=[pl.BlockSpec(memory_space=pltpu.SMEM), vmem, vmem],
        out_specs=(vmem, vmem),
        scratch_shapes=[square] * 4,
        compiler_params=pltpu.CompilerParams(vmem_limit_bytes=32 * 2**20),
        cost_estimate=pl.CostEstimate(flops=2 * 10**8, bytes_accessed=2**21, transcendentals=0),
    )(col, sums, all_states)


def across_pairs(count):
    pairs = [(i, i + 1 if i % 2 else i - 1) for i in range(count)]
    return [(i, j) for i, j in pairs if 0 <= j < count]


def body(states, diag_blocks, coupling, counts):
    rows = diag_blocks.shape[1]
    local = states.shape[0]
    domains = lax.axis_size(DOM)
    live = (lax.iota(jnp.int32, rows) < counts[0]).astype(F32)[None, :]
    even = lax.axis_index("core") == 0

    def trade(block, onward):
        over = lax.ppermute(jnp.where(even, block, onward), DOM, across_pairs(domains))
        both = lax.all_gather(jnp.where(even, onward, block), "core")
        beside = jnp.where(even, both[1], both[0])
        return jnp.where(even, over, beside), jnp.where(even, beside, over)

    def apply_op(block):
        low = block.astype(BF16)
        onward = jnp.dot(low, coupling, preferred_element_type=F32)
        from_prev, next_block = trade(block, onward)
        own = jnp.dot(low, diag_blocks, preferred_element_type=F32)
        own_t = lax.dot_general(low, diag_blocks, TRANSPOSED, preferred_element_type=F32)
        from_next = lax.dot_general(
            next_block.astype(BF16), coupling, TRANSPOSED, preferred_element_type=F32
        )
        return live * (0.5 * (own + own_t) + from_prev + from_next)

    first = live * states.astype(F32)
    prev = first
    cur = (apply_op(first) - CENTER * first) / HALF
    for step in range(DEGREE - 1):
        prev, cur = cur, 2.0 * (apply_op(cur) - CENTER * cur) / HALF - prev
    filtered = cur.astype(BF16)

    onward = jnp.dot(filtered, coupling, preferred_element_type=F32).astype(BF16)
    arrived = lax.ppermute(onward, DOM, [(i, i + 1) for i in range(domains - 1)])
    cols = lax.axis_size("col")
    all_states = lax.all_to_all(
        jnp.broadcast_to(filtered[None], (cols, local, rows)), "col", 0, 0
    ).reshape(cols * local, rows)
    half_image = jnp.dot(filtered, diag_blocks, preferred_element_type=F32)
    half_image = (half_image + 2.0 * arrived.astype(F32)).astype(BF16)

    total = cols * local
    pair = jnp.concatenate([filtered, half_image], axis=0)
    terms = lax.dot_general(pair, all_states, TRANSPOSED, preferred_element_type=F32)
    peers = ALONG_Y * CORES
    tiles = terms.reshape(2 * local // 8, 8, total // 128, 128)
    tiles = tiles.transpose(0, 2, 1, 3).reshape(peers, -1, 8, 128)
    share = lax.all_to_all(tiles, ("y", "core"), 0, 0).sum(0)
    shares = jnp.broadcast_to(share[None], (ALONG_X * cols,) + share.shape)
    shares = lax.all_to_all(shares, ("x", "col"), 0, 0)
    share = shares.reshape((ALONG_X, cols) + share.shape).sum(0)
    spread = jnp.broadcast_to(share[None], (peers,) + share.shape)
    sums = lax.all_to_all(spread, ("y", "core"), 0, 0)
    sums = sums.reshape(peers, cols, 8, 128)
    col = lax.axis_index("col").astype(jnp.int32).reshape(1)
    return finish(col, sums, all_states, local)


def solution(mesh):
    shape = (ALONG_X, ALONG_Y, CORES, mesh.shape["col"])
    fine = Mesh(mesh.devices.reshape(shape), DOM + ("col",))
    placed = (P("col", DOM), P(DOM, None), P(DOM, None), P(DOM))
    return jax.shard_map(
        body, mesh=fine, in_specs=placed, out_specs=(P("col", DOM), P()), check_vma=False
    )
```

time: 405 us -> 138 us (0.34)
  waiting for transfers between devices: 221 us -> 33 us
  other arithmetic: 57 us -> 0.04 us
  starting transfers between devices: 41.2 us -> 25.7 us
  between operations: 16.4 us -> 1.59 us
  blocking collectives: 44.3 us -> 55.2 us
  Pallas kernels: 0 us -> 10.4 us
  matrix products: 17.2 us -> 9.4 us
    psum x1 -> x0, waiting for transfers between devices: 218 us -> none  [body(): gram, proj = lax.psum((gram_term, proj_term), 'dom')]
    another operation x9 -> x0, other arithmetic: 55.9 us -> none  [the longest x6 35.4 us: body(): lower = jnp.linalg.cholesky(gram)]
    all_to_all x0 -> x2, blocking collectives: none -> 39.4 us  [the longest x1 22.5 us: body(): shares = lax.all_to_all(shares, ('x', 'col'), 0, 0)]
    all_gather x2 -> x3, blocking collectives: 44.3 us -> 15.7 us  [trade(): both = lax.all_gather(jnp.where(even, onward, block), 'core')]
    all_to_all x0 -> x2, waiting for transfers between devices: none -> 28.5 us  [the longest x1 17.3 us: body(): sums = lax.all_to_all(spread, ('y', 'core'), 0, 0)]
    ppermute x8 -> x4, starting transfers between devices: 41.2 us -> 13.3 us  [the longest x3 8.65 us: trade(): lax.ppermute(jnp.where(even, block, onward), DOM, across_pairs(domains))]
    all_to_all x0 -> x2, starting transfers between devices: none -> 12.4 us  [the longest x1 6.65 us: body(): lax.all_to_all(jnp.broadcast_to(filtered[None], (cols, local, rows)), 'co...]
    pallas_call x0 -> x1, Pallas kernels: none -> 10.4 us  [finish(): pl.pallas_call(finish_kernel, out_shape=(jax.ShapeDtypeStruct((local, row...]
  transfers between devices with their start and end apart: 9 -> 6, of which waited for: 5 -> 5; matrix products, arithmetic and copies ran while one was open for 1% -> 3% of each run, Pallas kernels for 0% -> 0%
where the time goes in v1:
time: 138 us
  blocking collectives  55.2 us (40%)
  waiting for transfers between devices  33 us (24%)
  starting transfers between devices  25.7 us (19%)
  Pallas kernels  10.4 us (8%)
  matrix products  9.4 us (7%)
  local copies, waits for them, and re-layouts  2.51 us (2%)
  between operations  1.59 us (1%)
    all_to_all x1, blocking collectives, body(): shares = lax.all_to_all(shares, ('x', 'col'), 0, 0)  22.5 us
    all_to_all x1, waiting for transfers between devices, body(): sums = lax.all_to_all(spread, ('y', 'core'), 0, 0)  17.3 us
    all_to_all x1, blocking collectives, body(): share = lax.all_to_all(tiles, ('y', 'core'), 0, 0).sum(0)  16.9 us
    all_gather x3, blocking collectives, trade(): both = lax.all_gather(jnp.where(even, onward, block), 'core')  15.7 us
    all_to_all x1, waiting for transfers between devices, body(): lax.all_to_all(jnp.broadcast_to(filtered[None], (cols, local, rows)), 'co...  11.2 us
    pallas_call x1, Pallas kernels, finish(): pl.pallas_call(finish_kernel, out_shape=(jax.ShapeDtypeStruct((local, row...  10.4 us
    ppermute x3, starting transfers between devices, trade(): lax.ppermute(jnp.where(even, block, onward), DOM, across_pairs(domains))  8.65 us
    all_to_all x1, starting transfers between devices, body(): lax.all_to_all(jnp.broadcast_to(filtered[None], (cols, local, rows)), 'co...  6.65 us
  transfers between devices with their start and end apart: 6, of which 5 were waited for; matrix products, arithmetic and copies ran while one was open for 3% of the time, Pallas kernels for 0%

profile of v1, /device:TPU:1, one launch (start us, length us, event | category | flops | bytes accessed | tf_op | source)
XLA Modules:
  0.0 137.9 jit_solution(2555001446373291356)
XLA Ops:
  0.6 0.0 copy-start
  0.6 0.0 copy-start.3
  1.5 0.8 copy-done
  2.2 0.0 copy-start.1
  2.2 1.5 %fusion.7 = (f32[32,1024]{1,0:T(8,128)S(1)}, f32[32,1024]{1,0:T(8,128)S(1)}) fusion(bf16[32,1024]{1,0:T(8,128)(2,1)} %param.4, f32[1024]{0:T(1024)S(1)} %fusion.27, pred[]{:T(512)S(6)} %eq.3, bf16[1024,1024]{1,0:T(8,128)(2,1)S(1)} %copy-done), kind=kOutput, calls=%fused_computation.24 | convolution fusion | flops 67338240 | bytes 2428929 | tf_op jit(solution)/shard_map/dot_general | solution.py:137
  3.7 4.7 %collective-permute-start = (f32[32,1024]{1,0:T(8,128)S(1)}, f32[32,1024]{1,0:T(8,128)S(1)}, u32[]{:S(2)}, u32[]{:S(2)}) collective-permute-start(f32[32,1024]{1,0:T(8,128)S(1)} %get-tuple-element.9), channel_id=1, source_target_pairs={{8,16},{16,8},{24,32},{32,24},{40,48},{48,40},{56,64},{64,56},{72,... | collective-permute-start | bytes 393224 | tf_op jit(solution)/shard_map/ppermute | solution.py:130
  8.5 0.0 copy-done.3
  8.5 0.0 copy-done.1
  8.5 0.5 fusion.25
  8.9 0.7 fusion.2
  9.7 11.7 %all-gather = f32[64,1024]{1,0:T(8,128)S(1)} all-gather(f32[32,1024]{1,0:T(8,128)S(1)} %get-tuple-element.8), channel_id=2, replica_groups=mesh['x'=8,'y'=8,'core'=2,'col'=8] {'core'}, dimensions={0}, use_global_device_ids=true | all-gather | bytes 393216 | tf_op jit(solution)/shard_map/all_gather | solution.py:131
  21.4 0.0 collective-permute-done
  21.4 0.7 multiply_subtract_fusion
  22.2 0.5 fusion.37
  22.7 0.5 multiply_select_fusion
  23.1 1.9 %collective-permute-start.1 = (f32[32,1024]{1,0:T(8,128)S(1)}, f32[32,1024]{1,0:T(8,128)S(1)}, u32[]{:S(2)}, u32[]{:S(2)}) collective-permute-start(f32[32,1024]{1,0:T(8,128)S(1)} %get-tuple-element.7), channel_id=1, source_target_pairs={{8,16},{16,8},{24,32},{32,24},{40,48},{48,40},{56,64},{64,56},{72,... | collective-permute-start | bytes 393224 | tf_op jit(solution)/shard_map/ppermute | solution.py:130
  25.1 0.7 fusion.1
  25.8 2.0 %all-gather.1 = f32[64,1024]{1,0:T(8,128)S(1)} all-gather(f32[32,1024]{1,0:T(8,128)S(1)} %get-tuple-element.6), channel_id=3, replica_groups=mesh['x'=8,'y'=8,'core'=2,'col'=8] {'core'}, dimensions={0}, use_global_device_ids=true | all-gather | bytes 393216 | tf_op jit(solution)/shard_map/all_gather | solution.py:131
  27.8 1.6 %collective-permute-done.1 = f32[32,1024]{1,0:T(8,128)S(1)} collective-permute-done((f32[32,1024]{1,0:T(8,128)S(1)}, f32[32,1024]{1,0:T(8,128)S(1)}, u32[]{:S(2)}, u32[]{:S(2)}) %collective-permute-start.1) | collective-permute-done | bytes 131104 | tf_op jit(solution)/shard_map/ppermute | solution.py:130
  29.4 0.7 subtract_subtract_fusion
  30.2 0.5 fusion.32
  30.6 0.5 broadcast_select_fusion.1
  31.1 2.0 %collective-permute-start.2 = (f32[32,1024]{1,0:T(8,128)S(1)}, f32[32,1024]{1,0:T(8,128)S(1)}, u32[]{:S(2)}, u32[]{:S(2)}) collective-permute-start(f32[32,1024]{1,0:T(8,128)S(1)} %get-tuple-element.5), channel_id=1, source_target_pairs={{8,16},{16,8},{24,32},{32,24},{40,48},{48,40},{56,64},{64,56},{72,... | collective-permute-start | bytes 393224 | tf_op jit(solution)/shard_map/ppermute | solution.py:130
  33.1 0.7 fusion
  33.9 2.0 %all-gather.2 = f32[64,1024]{1,0:T(8,128)S(1)} all-gather(f32[32,1024]{1,0:T(8,128)S(1)} %get-tuple-element.4), channel_id=4, replica_groups=mesh['x'=8,'y'=8,'core'=2,'col'=8] {'core'}, dimensions={0}, use_global_device_ids=true | all-gather | bytes 393216 | tf_op jit(solution)/shard_map/all_gather | solution.py:131
  35.9 1.5 %collective-permute-done.2 = f32[32,1024]{1,0:T(8,128)S(1)} collective-permute-done((f32[32,1024]{1,0:T(8,128)S(1)}, f32[32,1024]{1,0:T(8,128)S(1)}, u32[]{:S(2)}, u32[]{:S(2)}) %collective-permute-start.2) | collective-permute-done | bytes 131104 | tf_op jit(solution)/shard_map/ppermute | solution.py:130
  37.4 0.7 subtract_convert_fusion
  38.2 0.9 broadcast_in_dim.6
  39.0 6.6 %all-to-all-start = ((bf16[8,32,1024]{2,1,0:T(8,128)(2,1)}), bf16[8,32,1024]{2,1,0:T(8,128)(2,1)S(1)}, u32[]{:S(2)}, u32[]{:S(2)}) async-start(bf16[8,32,1024]{2,1,0:T(8,128)(2,1)} %broadcast_in_dim.6), calls=%async_computation | async-start | bytes 1048576 | tf_op jit(solution)/shard_map/all_to_all | solution.py:156
  45.7 0.0 copy-start.2
  45.7 0.4 convolution_convert_fusion
  46.1 4.6 %collective-permute-start.3 = (bf16[32,1024]{1,0:T(8,128)(2,1)S(1)}, bf16[32,1024]{1,0:T(8,128)(2,1)S(1)}, u32[]{:S(2)}, u32[]{:S(2)}) collective-permute-start(bf16[32,1024]{1,0:T(8,128)(2,1)S(1)} %convolution_convert_fusion), channel_id=1, source_target_pairs={{0,8},{8,16},{16,24},{24,32},{32,40},{40,48},{48,56},{56,64},{64,7... | collective-permute-start | bytes 196616 | tf_op jit(solution)/shard_map/ppermute | solution.py:154
  50.7 1.3 collective-permute-done.3
  52.0 0.0 copy-done.2
  52.0 0.4 add_convert_fusion
  52.4 11.2 %all-to-all-done = bf16[8,32,1024]{2,1,0:T(8,128)(2,1)S(1)} async-done(((bf16[8,32,1024]{2,1,0:T(8,128)(2,1)}), bf16[8,32,1024]{2,1,0:T(8,128)(2,1)S(1)}, u32[]{:S(2)}, u32[]{:S(2)}) %all-to-all-start) | async-done | bytes 524320 | tf_op jit(solution)/shard_map/all_to_all | solution.py:156
  63.7 0.3 fusion.3
  64.0 16.9 %all_to_all.20 = f32[16,1,8,128]{3,2,1,0:T(8,128)S(1)} all-to-all(f32[16,1,8,128]{3,2,1,0:T(8,128)S(1)} %bitcast.42), channel_id=1, replica_groups=mesh['x'=8,'y'=8,'core'=2,'col'=8] {'y','core'}, dimensions={0} | all-to-all | bytes 131072 | tf_op jit(solution)/shard_map/all_to_all | solution.py:168
  80.9 22.5 %all_to_all.21 = f32[64,1,8,128]{3,2,1,0:T(8,128)S(1)} all-to-all(f32[64,1,8,128]{3,2,1,0:T(8,128)S(1)} %broadcast_in_dim.7), channel_id=1, replica_groups=mesh['x'=8,'y'=8,'core'=2,'col'=8] {'x','col'}, dimensions={0} | all-to-all | bytes 524288 | tf_op jit(solution)/shard_map/all_to_all | solution.py:170
  103.5 0.8 broadcast_in_dim.8
  104.3 5.8 %all-to-all-start.3 = ((f32[16,8,1,8,128]{4,3,1,2,0:T(8,128)}), f32[16,8,1,8,128]{4,3,1,2,0:T(8,128)S(1)}, u32[]{:S(2)}, u32[]{:S(2)}) async-start(f32[16,8,1,8,128]{4,3,1,2,0:T(8,128)} %broadcast_in_dim.8), calls=%async_computation.3 | async-start | bytes 1048576 | tf_op jit(solution)/shard_map/all_to_all | solution.py:173
  110.1 17.3 %all-to-all-done.3 = f32[16,8,1,8,128]{4,3,1,2,0:T(8,128)S(1)} async-done(((f32[16,8,1,8,128]{4,3,1,2,0:T(8,128)}), f32[16,8,1,8,128]{4,3,1,2,0:T(8,128)S(1)}, u32[]{:S(2)}, u32[]{:S(2)}) %all-to-all-start.3) | async-done | bytes 524320 | tf_op jit(solution)/shard_map/all_to_all | solution.py:173
  127.4 10.4 %shard_map.59 = (f32[32,1024]{1,0:T(8,128)}, f32[256,256]{1,0:T(8,128)}) custom-call(s32[1]{0:T(128)} %bitcast.col_ref, f32[16,8,8,128]{3,2,1,0:T(8,128)S(1)} %bitcast.40, bf16[256,1024]{1,0:T(8,128)(2,1)S(1)} %bitcast.39), custom_call_target="tpu_custom_call" | custom-call | flops 200000000 | bytes 2097152 | tf_op jit(solution)/shard_map/pallas_call | solution.py:103
  (4 shorter events, 0.1 us)
Async XLA Ops:
  0.6 1.6 %copy-start = (bf16[1024,1024]{1,0:T(8,128)(2,1)S(1)}, bf16[1024,1024]{1,0:T(8,128)(2,1)}, u32[]{:S(2)}) copy-start(bf16[1024,1024]{1,0:T(8,128)(2,1)} %param.6) | copy-start | bytes 6291460
  0.6 7.8 %copy-start.3 = (bf16[32,1024]{1,0:T(8,128)(2,1)S(1)}, bf16[32,1024]{1,0:T(8,128)(2,1)}, u32[]{:S(2)}) copy-start(bf16[32,1024]{1,0:T(8,128)(2,1)} %param.4) | copy-start | bytes 196612
  2.2 6.2 %copy-start.1 = (bf16[1024,1024]{1,0:T(8,128)(2,1)S(1)}, bf16[1024,1024]{1,0:T(8,128)(2,1)}, u32[]{:S(2)}) copy-start(bf16[1024,1024]{1,0:T(8,128)(2,1)} %param.5) | copy-start | bytes 6291460
  3.7 17.7 %collective-permute-start = (f32[32,1024]{1,0:T(8,128)S(1)}, f32[32,1024]{1,0:T(8,128)S(1)}, u32[]{:S(2)}, u32[]{:S(2)}) collective-permute-start(f32[32,1024]{1,0:T(8,128)S(1)} %get-tuple-element.9), channel_id=1, source_target_pairs={{8,16},{16,8},{24,32},{32,24},{40,48},{48,40},{56,64},{64,56},{72,... | collective-permute-start | bytes 393224 | tf_op jit(solution)/shard_map/ppermute | solution.py:130
  23.1 6.3 %collective-permute-start.1 = (f32[32,1024]{1,0:T(8,128)S(1)}, f32[32,1024]{1,0:T(8,128)S(1)}, u32[]{:S(2)}, u32[]{:S(2)}) collective-permute-start(f32[32,1024]{1,0:T(8,128)S(1)} %get-tuple-element.7), channel_id=1, source_target_pairs={{8,16},{16,8},{24,32},{32,24},{40,48},{48,40},{56,64},{64,56},{72,... | collective-permute-start | bytes 393224 | tf_op jit(solution)/shard_map/ppermute | solution.py:130
  31.1 6.3 %collective-permute-start.2 = (f32[32,1024]{1,0:T(8,128)S(1)}, f32[32,1024]{1,0:T(8,128)S(1)}, u32[]{:S(2)}, u32[]{:S(2)}) collective-permute-start(f32[32,1024]{1,0:T(8,128)S(1)} %get-tuple-element.5), channel_id=1, source_target_pairs={{8,16},{16,8},{24,32},{32,24},{40,48},{48,40},{56,64},{64,56},{72,... | collective-permute-start | bytes 393224 | tf_op jit(solution)/shard_map/ppermute | solution.py:130
  39.0 24.7 %all-to-all-start = ((bf16[8,32,1024]{2,1,0:T(8,128)(2,1)}), bf16[8,32,1024]{2,1,0:T(8,128)(2,1)S(1)}, u32[]{:S(2)}, u32[]{:S(2)}) async-start(bf16[8,32,1024]{2,1,0:T(8,128)(2,1)} %broadcast_in_dim.6), calls=%async_computation | async-start | bytes 1048576 | tf_op jit(solution)/shard_map/all_to_all | solution.py:156
  45.7 6.4 %copy-start.2 = (bf16[1024,1024]{1,0:T(8,128)(2,1)S(1)}, bf16[1024,1024]{1,0:T(8,128)(2,1)}, u32[]{:S(2)}) copy-start(bf16[1024,1024]{1,0:T(8,128)(2,1)} %param.5) | copy-start | bytes 6291460
  46.1 5.9 %collective-permute-start.3 = (bf16[32,1024]{1,0:T(8,128)(2,1)S(1)}, bf16[32,1024]{1,0:T(8,128)(2,1)S(1)}, u32[]{:S(2)}, u32[]{:S(2)}) collective-permute-start(bf16[32,1024]{1,0:T(8,128)(2,1)S(1)} %convolution_convert_fusion), channel_id=1, source_target_pairs={{0,8},{8,16},{16,24},{24,32},{32,40},{40,48},{48,56},{56,64},{64,7... | collective-permute-start | bytes 196616 | tf_op jit(solution)/shard_map/ppermute | solution.py:154
  104.3 23.1 %all-to-all-start.3 = ((f32[16,8,1,8,128]{4,3,1,2,0:T(8,128)}), f32[16,8,1,8,128]{4,3,1,2,0:T(8,128)S(1)}, u32[]{:S(2)}, u32[]{:S(2)}) async-start(f32[16,8,1,8,128]{4,3,1,2,0:T(8,128)} %broadcast_in_dim.8), calls=%async_computation.3 | async-start | bytes 1048576 | tf_op jit(solution)/shard_map/all_to_all | solution.py:173

commit v2 on v1

--- a/solution.py
+++ b/solution.py
@@ -129,13 +129,15 @@
     def trade(block, onward):
         over = lax.ppermute(jnp.where(even, block, onward), DOM, across_pairs(domains))
         both = lax.all_gather(jnp.where(even, onward, block), "core")
-        beside = jnp.where(even, both[1], both[0])
-        return jnp.where(even, over, beside), jnp.where(even, beside, over)
+        return over, both
 
     def apply_op(block):
         low = block.astype(BF16)
         onward = jnp.dot(low, coupling, preferred_element_type=F32)
-        from_prev, next_block = trade(block, onward)
+        over, both = trade(block, onward)
+        low, both = lax.optimization_barrier((low, both))
+        beside = jnp.where(even, both[1], both[0])
+        from_prev, next_block = jnp.where(even, over, beside), jnp.where(even, beside, over)
         own = jnp.dot(low, diag_blocks, preferred_element_type=F32)
         own_t = lax.dot_general(low, diag_blocks, TRANSPOSED, preferred_element_type=F32)
         from_next = lax.dot_general(
@@ -162,16 +164,15 @@
     total = cols * local
     pair = jnp.concatenate([filtered, half_image], axis=0)
     terms = lax.dot_general(pair, all_states, TRANSPOSED, preferred_element_type=F32)
-    peers = ALONG_Y * CORES
-    tiles = terms.reshape(2 * local // 8, 8, total // 128, 128)
-    tiles = tiles.transpose(0, 2, 1, 3).reshape(peers, -1, 8, 128)
-    share = lax.all_to_all(tiles, ("y", "core"), 0, 0).sum(0)
-    shares = jnp.broadcast_to(share[None], (ALONG_X * cols,) + share.shape)
-    shares = lax.all_to_all(shares, ("x", "col"), 0, 0)
-    share = shares.reshape((ALONG_X, cols) + share.shape).sum(0)
-    spread = jnp.broadcast_to(share[None], (peers,) + share.shape)
-    sums = lax.all_to_all(spread, ("y", "core"), 0, 0)
-    sums = sums.reshape(peers, cols, 8, 128)
+    tiles = terms.reshape(2 * local // 8, 8, total // 128, 128).transpose(0, 2, 1, 3)
+    tiles = tiles.reshape(CORES, ALONG_Y, 8, 128)
+    pairs = lax.all_gather(tiles, "core")
+    half = lax.dynamic_index_in_dim(pairs, lax.axis_index("core"), 1, keepdims=False).sum(0)
+    share = lax.all_to_all(half, "y", 0, 0).sum(0)
+    share = lax.all_to_all(jnp.broadcast_to(share, (ALONG_X, 8, 128)), "x", 0, 0).sum(0)
+    shares = jnp.broadcast_to(share, (ALONG_Y * cols, 8, 128))
+    shares = lax.all_to_all(shares, ("y", "col"), 0, 0)
+    sums = lax.all_gather(shares, "core").reshape(CORES * ALONG_Y, cols, 8, 128)
     col = lax.axis_index("col").astype(jnp.int32).reshape(1)
     return finish(col, sums, all_states, local)
 

time: 138 us -> 134 us (0.971)
  waiting for transfers between devices: 33 us -> 23.1 us
  matrix products: 9.4 us -> 13.2 us
  blocking collectives: 55.2 us -> 56.9 us
    all_gather x0 -> x2, blocking collectives: none -> 7.87 us  [the longest x1 5.97 us: body(): sums = lax.all_gather(shares, 'core').reshape(CORES * ALONG_Y, cols, 8, 128)]
    all_to_all x1, waiting for transfers between devices: 11.2 us -> 4.75 us  [body(): lax.all_to_all(jnp.broadcast_to(filtered[None], (cols, local, rows)), 'co...]
    all_to_all x2, blocking collectives: 39.4 us -> 33.3 us  [the longest x1 20.2 us: body(): share = lax.all_to_all(half, 'y', 0, 0).sum(0)]
    all_to_all x1, waiting for transfers between devices: 17.3 us -> 12.5 us  [body(): shares = lax.all_to_all(shares, ('y', 'col'), 0, 0)]
    dot_general x1, matrix products: 0.43 us -> 2.69 us  [body(): half_image = jnp.dot(filtered, diag_blocks, preferred_element_type=F32)]
  transfers between devices with their start and end apart: 6 -> 6, of which waited for: 5 -> 5; matrix products, arithmetic and copies ran while one was open for 3% -> 5% of each run, Pallas kernels for 0% -> 0%
where the time goes in v2:
time: 134 us; the launch traced here: 133 us
  blocking collectives  56.9 us (42%)
  starting transfers between devices  25.6 us (19%)
  waiting for transfers between devices  23.1 us (17%)
  matrix products  13.2 us (10%)
  Pallas kernels  10.5 us (8%)
  local copies, waits for them, and re-layouts  2.38 us (2%)
  between operations  1.61 us (1%)
    all_to_all x1, blocking collectives, body(): share = lax.all_to_all(half, 'y', 0, 0).sum(0)  20.2 us
    all_gather x3, blocking collectives, trade(): both = lax.all_gather(jnp.where(even, onward, block), 'core')  15.7 us
    all_to_all x1, blocking collectives, body(): lax.all_to_all(jnp.broadcast_to(share, (ALONG_X, 8, 128)), 'x', 0, 0).sum(0)  13.1 us
    all_to_all x1, waiting for transfers between devices, body(): shares = lax.all_to_all(shares, ('y', 'col'), 0, 0)  12.5 us
    pallas_call x1, Pallas kernels, finish(): pl.pallas_call(finish_kernel, out_shape=(jax.ShapeDtypeStruct((local, row...  10.5 us
    ppermute x3, starting transfers between devices, trade(): lax.ppermute(jnp.where(even, block, onward), DOM, across_pairs(domains))  9.12 us
    all_to_all x1, starting transfers between devices, body(): lax.all_to_all(jnp.broadcast_to(filtered[None], (cols, local, rows)), 'co...  6.94 us
    all_gather x1, blocking collectives, body(): sums = lax.all_gather(shares, 'core').reshape(CORES * ALONG_Y, cols, 8, 128)  5.97 us
  transfers between devices with their start and end apart: 6, of which 5 were waited for; matrix products, arithmetic and copies ran while one was open for 5% of the time, Pallas kernels for 0%

profile of v2, /device:TPU:1, one launch (start us, length us, event | category | flops | bytes accessed | tf_op | source)
XLA Modules:
  0.0 133.3 jit_solution(17238602133131398426)
XLA Ops:
  0.6 0.0 copy-start
  0.6 0.0 copy-start.2
  1.5 0.8 copy-done
  2.2 0.0 copy-start.1
  2.2 1.5 %fusion.33 = (f32[32,1024]{1,0:T(8,128)S(1)}, f32[32,1024]{1,0:T(8,128)S(1)}) fusion(bf16[32,1024]{1,0:T(8,128)(2,1)} %param.4, f32[1024]{0:T(1024)S(1)} %fusion.61, pred[]{:T(512)S(6)} %eq.3, bf16[1024,1024]{1,0:T(8,128)(2,1)S(1)} %copy-done), kind=kOutput, calls=%fused_computation.42 | convolution fusion | flops 67338240 | bytes 2428929 | tf_op jit(solution)/shard_map/dot_general | solution.py:136
  3.7 4.7 %collective-permute-start = (f32[32,1024]{1,0:T(8,128)S(1)}, f32[32,1024]{1,0:T(8,128)S(1)}, u32[]{:S(2)}, u32[]{:S(2)}) collective-permute-start(f32[32,1024]{1,0:T(8,128)S(1)} %get-tuple-element.18), channel_id=1, source_target_pairs={{8,16},{16,8},{24,32},{32,24},{40,48},{48,40},{56,64},{64,56},{72,... | collective-permute-start | bytes 393224 | tf_op jit(solution)/shard_map/ppermute | solution.py:130
  8.5 0.0 copy-done.2
  8.5 11.7 %all-gather = f32[64,1024]{1,0:T(8,128)S(1)} all-gather(f32[32,1024]{1,0:T(8,128)S(1)} %get-tuple-element.19), channel_id=2, replica_groups=mesh['x'=8,'y'=8,'core'=2,'col'=8] {'core'}, dimensions={0}, use_global_device_ids=true | all-gather | bytes 393216 | tf_op jit(solution)/shard_map/all_gather | solution.py:131
  20.2 0.0 copy-done.1
  20.2 0.5 fusion.67
  20.7 0.7 fusion.2
  21.4 0.0 collective-permute-done
  21.5 0.8 multiply_convert_fusion
  22.2 0.5 multiply_select_fusion
  22.7 1.9 %collective-permute-start.1 = (f32[32,1024]{1,0:T(8,128)S(1)}, f32[32,1024]{1,0:T(8,128)S(1)}, u32[]{:S(2)}, u32[]{:S(2)}) collective-permute-start(f32[32,1024]{1,0:T(8,128)S(1)} %get-tuple-element.16), channel_id=1, source_target_pairs={{8,16},{16,8},{24,32},{32,24},{40,48},{48,40},{56,64},{64,56},{72,... | collective-permute-start | bytes 393224 | tf_op jit(solution)/shard_map/ppermute | solution.py:130
  24.6 2.0 %all-gather.1 = f32[64,1024]{1,0:T(8,128)S(1)} all-gather(f32[32,1024]{1,0:T(8,128)S(1)} %get-tuple-element.17), channel_id=3, replica_groups=mesh['x'=8,'y'=8,'core'=2,'col'=8] {'core'}, dimensions={0}, use_global_device_ids=true | all-gather | bytes 393216 | tf_op jit(solution)/shard_map/all_gather | solution.py:131
  26.6 0.5 fusion.68
  27.1 0.7 fusion.1
  27.8 1.2 collective-permute-done.1
  29.0 0.8 fusion.65
  29.7 0.5 broadcast_select_fusion.1
  30.2 2.0 %all-gather.2 = f32[64,1024]{1,0:T(8,128)S(1)} all-gather(f32[32,1024]{1,0:T(8,128)S(1)} %get-tuple-element.14), channel_id=4, replica_groups=mesh['x'=8,'y'=8,'core'=2,'col'=8] {'core'}, dimensions={0}, use_global_device_ids=true | all-gather | bytes 393216 | tf_op jit(solution)/shard_map/all_gather | solution.py:131
  32.2 0.5 fusion.69
  32.7 2.5 %collective-permute-start.2 = (f32[32,1024]{1,0:T(8,128)S(1)}, f32[32,1024]{1,0:T(8,128)S(1)}, u32[]{:S(2)}, u32[]{:S(2)}) collective-permute-start(f32[32,1024]{1,0:T(8,128)S(1)} %get-tuple-element.15), channel_id=1, source_target_pairs={{8,16},{16,8},{24,32},{32,24},{40,48},{48,40},{56,64},{64,56},{72,... | collective-permute-start | bytes 393224 | tf_op jit(solution)/shard_map/ppermute | solution.py:130
  35.2 0.7 fusion
  35.9 3.0 %collective-permute-done.2 = f32[32,1024]{1,0:T(8,128)S(1)} collective-permute-done((f32[32,1024]{1,0:T(8,128)S(1)}, f32[32,1024]{1,0:T(8,128)S(1)}, u32[]{:S(2)}, u32[]{:S(2)}) %collective-permute-start.2) | collective-permute-done | bytes 131104 | tf_op jit(solution)/shard_map/ppermute | solution.py:130
  39.0 0.7 fusion.11
  39.7 0.0 copy-start.3
  39.7 0.9 broadcast_in_dim.6
  40.6 0.0 copy-done.3
  40.6 6.9 %all-to-all-start = ((bf16[8,32,1024]{2,1,0:T(8,128)(2,1)}), bf16[8,32,1024]{2,1,0:T(8,128)(2,1)S(1)}, u32[]{:S(2)}, u32[]{:S(2)}) async-start(bf16[8,32,1024]{2,1,0:T(8,128)(2,1)} %broadcast_in_dim.6), calls=%async_computation | async-start | bytes 1048576 | tf_op jit(solution)/shard_map/all_to_all | solution.py:158
  47.5 1.1 convolution_convert_fusion
  48.6 3.6 %collective-permute-start.3 = (bf16[32,1024]{1,0:T(8,128)(2,1)}, bf16[32,1024]{1,0:T(8,128)(2,1)}, u32[]{:S(2)}, u32[]{:S(2)}) collective-permute-start(bf16[32,1024]{1,0:T(8,128)(2,1)} %convolution_convert_fusion), channel_id=1, source_target_pairs={{0,8},{8,16},{16,24},{24,32},{32,40},{40,48},{48,56},{56,64},{64,7... | collective-permute-start | bytes 196616 | tf_op jit(solution)/shard_map/ppermute | solution.py:156
  52.3 1.6 %collective-permute-done.3 = bf16[32,1024]{1,0:T(8,128)(2,1)} collective-permute-done((bf16[32,1024]{1,0:T(8,128)(2,1)}, bf16[32,1024]{1,0:T(8,128)(2,1)}, u32[]{:S(2)}, u32[]{:S(2)}) %collective-permute-start.3) | collective-permute-done | bytes 65568 | tf_op jit(solution)/shard_map/ppermute | solution.py:156
  53.9 2.7 %fusion.18 = bf16[32,1024]{1,0:T(8,128)(2,1)} fusion(bf16[1024,1024]{1,0:T(8,128)(2,1)} %param.5, f32[32,1024]{1,0:T(8,128)S(1)} %get-tuple-element.25, f32[32,1024]{1,0:T(8,128)S(1)} %fusion, f32[32,1024]{1,0:T(8,128)S(1)} %collective-permute-done.2, bf16[32,1024]{1,0:T(8,128)(2,1)} %collective-permute-done.3, f32[32,1024]{1,0:T(8,128)S(1)} %get-tuple-element.23, ...), kind=kOutput, calls=%fused_computation.21 | convolution fusion | flops 67567616 | bytes 3150848 | tf_op jit(solution)/shard_map/dot_general | solution.py:161
  56.6 4.7 %all-to-all-done = bf16[8,32,1024]{2,1,0:T(8,128)(2,1)S(1)} async-done(((bf16[8,32,1024]{2,1,0:T(8,128)(2,1)}), bf16[8,32,1024]{2,1,0:T(8,128)(2,1)S(1)}, u32[]{:S(2)}, u32[]{:S(2)}) %all-to-all-start) | async-done | bytes 524320 | tf_op jit(solution)/shard_map/all_to_all | solution.py:158
  61.3 1.2 fusion.3
  62.5 1.9 %all_gather.33 = f32[2,2,8,8,128]{4,3,2,1,0:T(8,128)S(1)} all-gather(f32[1,2,8,8,128]{4,3,2,1,0:T(8,128)S(1)} %bitcast.116), channel_id=1, replica_groups=mesh['x'=8,'y'=8,'core'=2,'col'=8] {'core'}, dimensions={0}, use_global_device_ids=true | all-gather | bytes 196608 | tf_op jit(solution)/shard_map/all_gather | solution.py:169
  64.4 20.2 %all_to_all.20 = f32[8,8,128]{2,1,0:T(8,128)S(1)} all-to-all(f32[8,8,128]{2,1,0:T(8,128)S(1)} %dynamic-slice_reduce_fusion), channel_id=1, replica_groups=mesh['x'=8,'y'=8,'core'=2,'col'=8] {'y'}, dimensions={0} | all-to-all | bytes 65536 | tf_op jit(solution)/shard_map/all_to_all | solution.py:171
  84.6 13.1 %all_to_all.21 = f32[8,8,128]{2,1,0:T(8,128)S(1)} all-to-all(f32[8,8,128]{2,1,0:T(8,128)S(1)} %broadcast_in_dim.14), channel_id=1, replica_groups=mesh['x'=8,'y'=8,'core'=2,'col'=8] {'x'}, dimensions={0} | all-to-all | bytes 65536 | tf_op jit(solution)/shard_map/all_to_all | solution.py:172
  97.7 0.7 broadcast_in_dim.15
  98.5 5.9 %all-to-all-start.3 = ((f32[64,8,128]{2,1,0:T(8,128)}), f32[64,8,128]{2,1,0:T(8,128)S(1)}, u32[]{:S(2)}, u32[]{:S(2)}) async-start(f32[64,8,128]{2,1,0:T(8,128)} %broadcast_in_dim.15), calls=%async_computation.3 | async-start | bytes 524288 | tf_op jit(solution)/shard_map/all_to_all | solution.py:174
  104.3 12.5 %all-to-all-done.3 = f32[64,8,128]{2,1,0:T(8,128)S(1)} async-done(((f32[64,8,128]{2,1,0:T(8,128)}), f32[64,8,128]{2,1,0:T(8,128)S(1)}, u32[]{:S(2)}, u32[]{:S(2)}) %all-to-all-start.3) | async-done | bytes 262176 | tf_op jit(solution)/shard_map/all_to_all | solution.py:174
  116.9 6.0 %all-gather.3 = f32[128,8,128]{2,1,0:T(8,128)S(1)} all-gather(f32[64,8,128]{2,1,0:T(8,128)S(1)} %all-to-all-done.3), channel_id=5, replica_groups=mesh['x'=8,'y'=8,'core'=2,'col'=8] {'core'}, dimensions={0}, use_global_device_ids=true | all-gather | bytes 786432 | tf_op jit(solution)/shard_map/all_gather | solution.py:175
  122.8 10.5 %shard_map.59 = (f32[32,1024]{1,0:T(8,128)}, f32[256,256]{1,0:T(8,128)}) custom-call(s32[1]{0:T(128)} %bitcast.col_ref, f32[16,8,8,128]{3,2,1,0:T(8,128)S(1)} %bitcast.110, bf16[256,1024]{1,0:T(8,128)(2,1)S(1)} %bitcast.109), custom_call_target="tpu_custom_call" | custom-call | flops 200000000 | bytes 2097152 | tf_op jit(solution)/shard_map/pallas_call | solution.py:103
  (6 shorter events, 0.1 us)
Async XLA Ops:
  0.6 1.6 %copy-start = (bf16[1024,1024]{1,0:T(8,128)(2,1)S(1)}, bf16[1024,1024]{1,0:T(8,128)(2,1)}, u32[]{:S(2)}) copy-start(bf16[1024,1024]{1,0:T(8,128)(2,1)} %param.6) | copy-start | bytes 6291460
  0.6 7.8 %copy-start.2 = (bf16[32,1024]{1,0:T(8,128)(2,1)S(1)}, bf16[32,1024]{1,0:T(8,128)(2,1)}, u32[]{:S(2)}) copy-start(bf16[32,1024]{1,0:T(8,128)(2,1)} %param.4) | copy-start | bytes 196612
  2.2 18.0 %copy-start.1 = (bf16[1024,1024]{1,0:T(8,128)(2,1)S(1)}, bf16[1024,1024]{1,0:T(8,128)(2,1)}, u32[]{:S(2)}) copy-start(bf16[1024,1024]{1,0:T(8,128)(2,1)} %param.5) | copy-start | bytes 6291460
  3.7 17.7 %collective-permute-start = (f32[32,1024]{1,0:T(8,128)S(1)}, f32[32,1024]{1,0:T(8,128)S(1)}, u32[]{:S(2)}, u32[]{:S(2)}) collective-permute-start(f32[32,1024]{1,0:T(8,128)S(1)} %get-tuple-element.18), channel_id=1, source_target_pairs={{8,16},{16,8},{24,32},{32,24},{40,48},{48,40},{56,64},{64,56},{72,... | collective-permute-start | bytes 393224 | tf_op jit(solution)/shard_map/ppermute | solution.py:130
  22.7 6.3 %collective-permute-start.1 = (f32[32,1024]{1,0:T(8,128)S(1)}, f32[32,1024]{1,0:T(8,128)S(1)}, u32[]{:S(2)}, u32[]{:S(2)}) collective-permute-start(f32[32,1024]{1,0:T(8,128)S(1)} %get-tuple-element.16), channel_id=1, source_target_pairs={{8,16},{16,8},{24,32},{32,24},{40,48},{48,40},{56,64},{64,56},{72,... | collective-permute-start | bytes 393224 | tf_op jit(solution)/shard_map/ppermute | solution.py:130
  32.7 6.3 %collective-permute-start.2 = (f32[32,1024]{1,0:T(8,128)S(1)}, f32[32,1024]{1,0:T(8,128)S(1)}, u32[]{:S(2)}, u32[]{:S(2)}) collective-permute-start(f32[32,1024]{1,0:T(8,128)S(1)} %get-tuple-element.15), channel_id=1, source_target_pairs={{8,16},{16,8},{24,32},{32,24},{40,48},{48,40},{56,64},{64,56},{72,... | collective-permute-start | bytes 393224 | tf_op jit(solution)/shard_map/ppermute | solution.py:130
  39.7 0.9 copy-start.3
  40.6 20.7 %all-to-all-start = ((bf16[8,32,1024]{2,1,0:T(8,128)(2,1)}), bf16[8,32,1024]{2,1,0:T(8,128)(2,1)S(1)}, u32[]{:S(2)}, u32[]{:S(2)}) async-start(bf16[8,32,1024]{2,1,0:T(8,128)(2,1)} %broadcast_in_dim.6), calls=%async_computation | async-start | bytes 1048576 | tf_op jit(solution)/shard_map/all_to_all | solution.py:158
  48.6 5.3 %collective-permute-start.3 = (bf16[32,1024]{1,0:T(8,128)(2,1)}, bf16[32,1024]{1,0:T(8,128)(2,1)}, u32[]{:S(2)}, u32[]{:S(2)}) collective-permute-start(bf16[32,1024]{1,0:T(8,128)(2,1)} %convolution_convert_fusion), channel_id=1, source_target_pairs={{0,8},{8,16},{16,24},{24,32},{32,40},{40,48},{48,56},{56,64},{64,7... | collective-permute-start | bytes 196616 | tf_op jit(solution)/shard_map/ppermute | solution.py:156
  98.5 18.4 %all-to-all-start.3 = ((f32[64,8,128]{2,1,0:T(8,128)}), f32[64,8,128]{2,1,0:T(8,128)S(1)}, u32[]{:S(2)}, u32[]{:S(2)}) async-start(f32[64,8,128]{2,1,0:T(8,128)} %broadcast_in_dim.15), calls=%async_computation.3 | async-start | bytes 524288 | tf_op jit(solution)/shard_map/all_to_all | solution.py:174

commit v3 on v1

--- a/solution.py
+++ b/solution.py
@@ -68,8 +68,9 @@
 
 
 def finish_kernel(col_ref, sums_ref, all_ref, basis_ref, reduced_ref, a_ref, q_ref, x_ref, inv_ref):
-    tiles, cols, eight, lanes = sums_ref.shape
+    cores, along, cols, eight, lanes = sums_ref.shape
     local = basis_ref.shape[0]
+    tiles = cores * along
     per_matrix = tiles // 2
     halves = a_ref.shape[1] // lanes
     for t in range(tiles):
@@ -77,7 +78,7 @@
         block, half = divmod(t % per_matrix, halves)
         for z in range(cols):
             top = z * local + block * eight
-            target[top : top + eight, half * lanes : (half + 1) * lanes] = sums_ref[t, z]
+            target[top : top + eight, half * lanes : (half + 1) * lanes] = sums_ref[t % cores, t // cores, z]
     cholesky_inverse(a_ref, x_ref, inv_ref)
     proj = q_ref[...]
     proj = 0.5 * (proj + proj.T)
@@ -119,59 +120,148 @@
     return [(i, j) for i, j in pairs if 0 <= j < count]
 
 
+def local_kernel(kernel, outs, *operands, scalars=0):
+    vmem = pl.BlockSpec(memory_space=pltpu.VMEM)
+    smem = pl.BlockSpec(memory_space=pltpu.SMEM)
+    return pl.pallas_call(
+        kernel,
+        out_shape=tuple(jax.ShapeDtypeStruct(shape, dtype) for shape, dtype in outs),
+        in_specs=[smem] * scalars + [vmem] * (len(operands) - scalars),
+        out_specs=(vmem,) * len(outs),
+        compiler_params=pltpu.CompilerParams(vmem_limit_bytes=12 * 2**20),
+        cost_estimate=pl.CostEstimate(flops=2**16, bytes_accessed=2**16, transcendentals=0),
+    )(*operands)
+
+
+def live_row(counts_ref, shape):
+    return lax.broadcasted_iota(jnp.int32, (1, shape[1]), 1) < counts_ref[0]
+
+
+def send_off(even, block, low, coupling_ref, over_ref, on_ref):
+    onward = jnp.dot(low, coupling_ref[...], preferred_element_type=F32)
+    over_ref[...] = jnp.where(even, block, onward)
+    on_ref[...] = jnp.where(even, onward, block)
+
+
+def first_kernel(counts_ref, core_ref, states_ref, coupling_ref, low_ref, over_ref, on_ref):
+    live = live_row(counts_ref, states_ref.shape)
+    block = jnp.where(live, states_ref[...].astype(F32), 0.0)
+    low = block.astype(BF16)
+    low_ref[...] = low
+    send_off(core_ref[0] == 0, block, low, coupling_ref, over_ref, on_ref)
+
+
+def own_kernel(low_ref, diag_ref, own_ref):
+    low, diag = low_ref[...], diag_ref[...]
+    own = jnp.dot(low, diag, preferred_element_type=F32)
+    own_t = lax.dot_general(low, diag, TRANSPOSED, preferred_element_type=F32)
+    own_ref[...] = 0.5 * (own + own_t)
+
+
+def recur(counts_ref, even, over_ref, both_ref, own_ref, cur_ref, prev_ref, coupling_ref):
+    over = over_ref[...]
+    beside = jnp.where(even, both_ref[1], both_ref[0])
+    from_prev = jnp.where(even, over, beside)
+    next_block = jnp.where(even, beside, over).astype(BF16)
+    from_next = lax.dot_general(
+        next_block, coupling_ref[...], TRANSPOSED, preferred_element_type=F32
+    )
+    live = live_row(counts_ref, over.shape)
+    image = jnp.where(live, own_ref[...] + from_prev + from_next, 0.0)
+    shifted = (image - CENTER * cur_ref[...].astype(F32)) / HALF
+    if prev_ref is None:
+        return shifted
+    return 2.0 * shifted - prev_ref[...].astype(F32)
+
+
+def step_kernel(counts_ref, core_ref, over_ref, both_ref, own_ref, coupling_ref, cur_ref, *rest):
+    prev_ref = rest[0] if len(rest) == 5 else None
+    next_ref, low_ref, over_out, on_out = rest[-4:]
+    even = core_ref[0] == 0
+    block = recur(counts_ref, even, over_ref, both_ref, own_ref, cur_ref, prev_ref, coupling_ref)
+    low = block.astype(BF16)
+    next_ref[...] = block
+    low_ref[...] = low
+    send_off(even, block, low, coupling_ref, over_out, on_out)
+
+
+def last_kernel(
+    counts_ref, core_ref, over_ref, both_ref, own_ref, coupling_ref, cur_ref, prev_ref,
+    filtered_ref, copies_ref, onward_ref,
+):
+    even = core_ref[0] == 0
+    block = recur(counts_ref, even, over_ref, both_ref, own_ref, cur_ref, prev_ref, coupling_ref)
+    low = block.astype(BF16)
+    filtered_ref[...] = low
+    for z in range(copies_ref.shape[0]):
+        copies_ref[z] = low
+    onward_ref[...] = jnp.dot(low, coupling_ref[...], preferred_element_type=F32).astype(BF16)
+
+
+def diag_kernel(filtered_ref, diag_ref, out_ref):
+    out_ref[...] = jnp.dot(filtered_ref[...], diag_ref[...], preferred_element_type=F32)
+
+
+def terms_kernel(filtered_ref, product_ref, arrived_ref, all_ref, tiles_ref):
+    half_image = (product_ref[...] + 2.0 * arrived_ref[...].astype(F32)).astype(BF16)
+    pair = jnp.concatenate([filtered_ref[...], half_image], axis=0)
+    terms = lax.dot_general(pair, all_ref[...], TRANSPOSED, preferred_element_type=F32)
+    across = terms.shape[1] // 128
+    for t in range(tiles_ref.shape[0]):
+        k, half = divmod(t, across)
+        tiles_ref[t] = terms[8 * k : 8 * k + 8, 128 * half : 128 * half + 128]
+
+
+def sum_kernel(parts_ref, copies_ref):
+    total = parts_ref[0]
+    for i in range(1, parts_ref.shape[0]):
+        total = total + parts_ref[i]
+    for i in range(copies_ref.shape[0]):
+        copies_ref[i] = total
+
+
 def body(states, diag_blocks, coupling, counts):
-    rows = diag_blocks.shape[1]
-    local = states.shape[0]
-    domains = lax.axis_size(DOM)
-    live = (lax.iota(jnp.int32, rows) < counts[0]).astype(F32)[None, :]
-    even = lax.axis_index("core") == 0
-
-    def trade(block, onward):
-        over = lax.ppermute(jnp.where(even, block, onward), DOM, across_pairs(domains))
-        both = lax.all_gather(jnp.where(even, onward, block), "core")
-        beside = jnp.where(even, both[1], both[0])
-        return jnp.where(even, over, beside), jnp.where(even, beside, over)
-
-    def apply_op(block):
-        low = block.astype(BF16)
-        onward = jnp.dot(low, coupling, preferred_element_type=F32)
-        from_prev, next_block = trade(block, onward)
-        own = jnp.dot(low, diag_blocks, preferred_element_type=F32)
-        own_t = lax.dot_general(low, diag_blocks, TRANSPOSED, preferred_element_type=F32)
-        from_next = lax.dot_general(
-            next_block.astype(BF16), coupling, TRANSPOSED, preferred_element_type=F32
-        )
-        return live * (0.5 * (own + own_t) + from_prev + from_next)
-
-    first = live * states.astype(F32)
-    prev = first
-    cur = (apply_op(first) - CENTER * first) / HALF
-    for step in range(DEGREE - 1):
-        prev, cur = cur, 2.0 * (apply_op(cur) - CENTER * cur) / HALF - prev
-    filtered = cur.astype(BF16)
-
-    onward = jnp.dot(filtered, coupling, preferred_element_type=F32).astype(BF16)
+    local, rows = states.shape
+    block = (local, rows)
+    domains, cols = lax.axis_size(DOM), lax.axis_size("col")
+    core = lax.axis_index("core").astype(jnp.int32).reshape(1)
+    trade = [(block, F32), (block, F32)]
+
+    low, over, on = local_kernel(
+        first_kernel, [(block, BF16)] + trade, counts, core, states, coupling, scalars=2
+    )
+    history = [low]
+    for step in range(DEGREE):
+        over = lax.ppermute(over, DOM, across_pairs(domains))
+        both = lax.all_gather(on, "core")
+        low, both = lax.optimization_barrier((low, both))
+        (own,) = local_kernel(own_kernel, [(block, F32)], low, diag_blocks)
+        args = (counts, core, over, both, own, coupling, *history[:-3:-1])
+        if step < DEGREE - 1:
+            cur, low, over, on = local_kernel(
+                step_kernel, [(block, F32), (block, BF16)] + trade, *args, scalars=2
+            )
+            history.append(cur)
+    filtered, copies, onward = local_kernel(
+        last_kernel,
+        [(block, BF16), ((cols,) + block, BF16), (block, BF16)],
+        *args,
+        scalars=2,
+    )
+
     arrived = lax.ppermute(onward, DOM, [(i, i + 1) for i in range(domains - 1)])
-    cols = lax.axis_size("col")
-    all_states = lax.all_to_all(
-        jnp.broadcast_to(filtered[None], (cols, local, rows)), "col", 0, 0
-    ).reshape(cols * local, rows)
-    half_image = jnp.dot(filtered, diag_blocks, preferred_element_type=F32)
-    half_image = (half_image + 2.0 * arrived.astype(F32)).astype(BF16)
-
-    total = cols * local
-    pair = jnp.concatenate([filtered, half_image], axis=0)
-    terms = lax.dot_general(pair, all_states, TRANSPOSED, preferred_element_type=F32)
+    all_states = lax.all_to_all(copies, "col", 0, 0).reshape(cols * local, rows)
+    (product,) = local_kernel(diag_kernel, [(block, F32)], filtered, diag_blocks)
     peers = ALONG_Y * CORES
-    tiles = terms.reshape(2 * local // 8, 8, total // 128, 128)
-    tiles = tiles.transpose(0, 2, 1, 3).reshape(peers, -1, 8, 128)
-    share = lax.all_to_all(tiles, ("y", "core"), 0, 0).sum(0)
-    shares = jnp.broadcast_to(share[None], (ALONG_X * cols,) + share.shape)
-    shares = lax.all_to_all(shares, ("x", "col"), 0, 0)
-    share = shares.reshape((ALONG_X, cols) + share.shape).sum(0)
-    spread = jnp.broadcast_to(share[None], (peers,) + share.shape)
-    sums = lax.all_to_all(spread, ("y", "core"), 0, 0)
-    sums = sums.reshape(peers, cols, 8, 128)
+    (tiles,) = local_kernel(
+        terms_kernel, [((peers, 8, 128), F32)], filtered, product, arrived, all_states
+    )
+    parts = lax.all_to_all(tiles, ("y", "core"), 0, 0)
+    (copies,) = local_kernel(sum_kernel, [((ALONG_X, 8, 128), F32)], parts)
+    parts = lax.all_to_all(copies, "x", 0, 0)
+    (copies,) = local_kernel(sum_kernel, [((ALONG_Y * cols, 8, 128), F32)], parts)
+    shares = lax.all_to_all(copies, ("y", "col"), 0, 0)
+    sums = lax.all_gather(shares, "core").reshape(CORES, ALONG_Y, cols, 8, 128)
     col = lax.axis_index("col").astype(jnp.int32).reshape(1)
     return finish(col, sums, all_states, local)
 

time: 138 us -> 130 us (0.942)
  matrix products: 9.4 us -> 0 us
  Pallas kernels: 10.4 us -> 19.6 us
  waiting for transfers between devices: 33 us -> 27.3 us
  blocking collectives: 55.2 us -> 51.8 us
  local copies, waits for them, and re-layouts: 2.51 us -> 4.03 us
    dot_general x15 -> x0, matrix products: 9.4 us -> none  [the longest x3 2.44 us: apply_op(): onward = jnp.dot(low, coupling, preferred_element_type=F32)]
    pallas_call x0 -> x11, Pallas kernels: none -> 9.19 us  [local_kernel(): pl.pallas_call(kernel, out_shape=tuple((jax.ShapeDtypeStruct(shape, dtype...]
    all_to_all x2, blocking collectives: 39.4 us -> 30.6 us  [the longest x1 16.9 us: body(): parts = lax.all_to_all(tiles, ('y', 'core'), 0, 0)]
    all_gather x3 -> x4, blocking collectives: 15.7 us -> 21.2 us  [the longest x3 15.7 us: body(): both = lax.all_gather(on, 'core')]
    all_to_all x2, waiting for transfers between devices: 28.5 us -> 24.3 us  [the longest x1 12.5 us: body(): shares = lax.all_to_all(copies, ('y', 'col'), 0, 0)]
    unnamed x8 -> x10, local copies, waits for them, and re-layouts: 0.79 us -> 4.03 us
    broadcast_in_dim x3 -> x0, local copies, waits for them, and re-layouts: 1.72 us -> none  [the longest x1 0.85 us: body(): jnp.broadcast_to(filtered[None], (cols, local, rows))]
  transfers between devices with their start and end apart: 6 -> 6, of which waited for: 5 -> 5; matrix products, arithmetic and copies ran while one was open for 3% -> 0% of each run, Pallas kernels for 0% -> 3%
where the time goes in v3:
time: 130 us
  blocking collectives  51.8 us (40%)
  waiting for transfers between devices  27.3 us (21%)
  starting transfers between devices  25.6 us (20%)
  Pallas kernels  19.6 us (15%)
  local copies, waits for them, and re-layouts  4.03 us (3%)
  between operations  1.38 us (1%)
    all_to_all x1, blocking collectives, body(): parts = lax.all_to_all(tiles, ('y', 'core'), 0, 0)  16.9 us
    all_gather x3, blocking collectives, body(): both = lax.all_gather(on, 'core')  15.7 us
    all_to_all x1, blocking collectives, body(): parts = lax.all_to_all(copies, 'x', 0, 0)  13.7 us
    all_to_all x1, waiting for transfers between devices, body(): shares = lax.all_to_all(copies, ('y', 'col'), 0, 0)  12.5 us
    all_to_all x1, waiting for transfers between devices, body(): all_states = lax.all_to_all(copies, 'col', 0, 0).reshape(cols * local, rows)  11.8 us
    pallas_call x1, Pallas kernels, finish(): pl.pallas_call(finish_kernel, out_shape=(jax.ShapeDtypeStruct((local, row...  10.4 us
    pallas_call x11, Pallas kernels, local_kernel(): pl.pallas_call(kernel, out_shape=tuple((jax.ShapeDtypeStruct(shape, dtype...  9.19 us
    ppermute x3, starting transfers between devices, body(): over = lax.ppermute(over, DOM, across_pairs(domains))  9.14 us
  transfers between devices with their start and end apart: 6, of which 5 were waited for; matrix products, arithmetic and copies ran while one was open for 0% of the time, Pallas kernels for 3%

profile of v3, /device:TPU:1, one launch (start us, length us, event | category | flops | bytes accessed | tf_op | source)
XLA Modules:
  0.0 129.7 jit_solution(11394680441881297203)
XLA Ops:
  1.3 0.0 copy-start
  1.3 1.6 %copy-done = bf16[1024,1024]{1,0:T(8,128)(2,1)S(1)} copy-done((bf16[1024,1024]{1,0:T(8,128)(2,1)S(1)}, bf16[1024,1024]{1,0:T(8,128)(2,1)}, u32[]{:S(2)}) %copy-start) | copy-done | bytes 2097176
  2.9 0.0 copy-start.4
  2.9 0.8 copy-done.4
  3.7 0.0 copy-start.1
  3.7 0.5 shard_map.59
  4.2 4.8 %collective-permute-start = (f32[32,1024]{1,0:T(8,128)S(1)}, f32[32,1024]{1,0:T(8,128)S(1)}, u32[]{:S(2)}, u32[]{:S(2)}) collective-permute-start(f32[32,1024]{1,0:T(8,128)S(1)} %get-tuple-element.22), channel_id=1, source_target_pairs={{8,16},{16,8},{24,32},{32,24},{40,48},{48,40},{56,64},{64,56},{72,... | collective-permute-start | bytes 393224 | tf_op jit(solution)/shard_map/ppermute | solution.py:235
  9.0 11.7 %all-gather = f32[64,1024]{1,0:T(8,128)S(1)} all-gather(f32[32,1024]{1,0:T(8,128)S(1)} %get-tuple-element.24), channel_id=2, replica_groups=mesh['x'=8,'y'=8,'core'=2,'col'=8] {'core'}, dimensions={0}, use_global_device_ids=true | all-gather | bytes 393216 | tf_op jit(solution)/shard_map/all_gather | solution.py:236
  20.8 0.0 copy-start.2
  20.8 1.6 %copy-done.2 = bf16[1024,1024]{1,0:T(8,128)(2,1)S(1)} copy-done((bf16[1024,1024]{1,0:T(8,128)(2,1)S(1)}, bf16[1024,1024]{1,0:T(8,128)(2,1)}, u32[]{:S(2)}) %copy-start.2) | copy-done | bytes 2097176
  22.4 1.1 shard_map.60.own_ref
  23.4 0.0 copy-start.3
  23.5 0.0 collective-permute-done.over_ref
  23.5 0.0 copy-done.1
  23.5 1.1 shard_map.61
  24.6 1.9 %collective-permute-start.1 = (f32[32,1024]{1,0:T(8,128)S(1)}, f32[32,1024]{1,0:T(8,128)S(1)}, u32[]{:S(2)}, u32[]{:S(2)}) collective-permute-start(f32[32,1024]{1,0:T(8,128)S(1)} %get-tuple-element.27), channel_id=1, source_target_pairs={{8,16},{16,8},{24,32},{32,24},{40,48},{48,40},{56,64},{64,56},{72,... | collective-permute-start | bytes 393224 | tf_op jit(solution)/shard_map/ppermute | solution.py:235
  26.5 2.0 %all-gather.1 = f32[64,1024]{1,0:T(8,128)S(1)} all-gather(f32[32,1024]{1,0:T(8,128)S(1)} %get-tuple-element.29), channel_id=3, replica_groups=mesh['x'=8,'y'=8,'core'=2,'col'=8] {'core'}, dimensions={0}, use_global_device_ids=true | all-gather | bytes 393216 | tf_op jit(solution)/shard_map/all_gather | solution.py:236
  28.5 0.0 copy-done.3
  28.5 1.1 shard_map.62.own_ref
  29.6 1.3 collective-permute-done.1.over_ref
  30.9 1.1 shard_map.63
  32.0 2.4 %collective-permute-start.2 = (f32[32,1024]{1,0:T(8,128)S(1)}, f32[32,1024]{1,0:T(8,128)S(1)}, u32[]{:S(2)}, u32[]{:S(2)}) collective-permute-start(f32[32,1024]{1,0:T(8,128)S(1)} %get-tuple-element.33), channel_id=1, source_target_pairs={{8,16},{16,8},{24,32},{32,24},{40,48},{48,40},{56,64},{64,56},{72,... | collective-permute-start | bytes 393224 | tf_op jit(solution)/shard_map/ppermute | solution.py:235
  34.4 2.0 %all-gather.2 = f32[64,1024]{1,0:T(8,128)S(1)} all-gather(f32[32,1024]{1,0:T(8,128)S(1)} %get-tuple-element.35), channel_id=4, replica_groups=mesh['x'=8,'y'=8,'core'=2,'col'=8] {'core'}, dimensions={0}, use_global_device_ids=true | all-gather | bytes 393216 | tf_op jit(solution)/shard_map/all_gather | solution.py:236
  36.4 1.1 shard_map.64.own_ref
  37.5 0.8 collective-permute-done.2.over_ref
  38.3 1.8 %shard_map.65 = (bf16[32,1024]{1,0:T(8,128)(2,1)S(1)}, bf16[8,32,1024]{2,1,0:T(8,128)(2,1)}, bf16[32,1024]{1,0:T(8,128)(2,1)S(1)}) custom-call(s32[1]{0:T(128)S(6)} %copy.6.counts_ref, s32[1]{0:T(128)} %bitcast.1.core_ref, f32[32,1024]{1,0:T(8,128)S(1)} %collective-permute-done.2.over_ref, f32[2,32,1024]{2,1,0:T(8,128)S(1)} %bitcast.12, ...), custom_call_target="tpu_custom_call" | custom-call | flops 65536 | bytes 65536 | tf_op jit(solution)/shard_map/pallas_call | solution.py:126
  40.1 7.0 %all-to-all-start = ((bf16[8,32,1024]{2,1,0:T(8,128)(2,1)}), bf16[8,32,1024]{2,1,0:T(8,128)(2,1)S(1)}, u32[]{:S(2)}, u32[]{:S(2)}) async-start(bf16[8,32,1024]{2,1,0:T(8,128)(2,1)} %get-tuple-element.41), calls=%async_computation | async-start | bytes 1048576 | tf_op jit(solution)/shard_map/all_to_all | solution.py:253
  47.1 4.8 %collective-permute-start.3 = (bf16[32,1024]{1,0:T(8,128)(2,1)S(1)}, bf16[32,1024]{1,0:T(8,128)(2,1)S(1)}, u32[]{:S(2)}, u32[]{:S(2)}) collective-permute-start(bf16[32,1024]{1,0:T(8,128)(2,1)S(1)} %get-tuple-element.40), channel_id=1, source_target_pairs={{0,8},{8,16},{16,24},{24,32},{32,40},{40,48},{48,56},{56,64},{64,7... | collective-permute-start | bytes 196616 | tf_op jit(solution)/shard_map/ppermute | solution.py:252
  51.9 0.5 shard_map.66.product_ref
  52.4 0.9 collective-permute-done.3.arrived_ref
  53.2 11.8 %all-to-all-done = bf16[8,32,1024]{2,1,0:T(8,128)(2,1)S(1)} async-done(((bf16[8,32,1024]{2,1,0:T(8,128)(2,1)}), bf16[8,32,1024]{2,1,0:T(8,128)(2,1)S(1)}, u32[]{:S(2)}, u32[]{:S(2)}) %all-to-all-start) | async-done | bytes 524320 | tf_op jit(solution)/shard_map/all_to_all | solution.py:253
  65.0 0.3 shard_map.67
  65.3 16.9 %all_to_all.20.parts_ref = f32[16,8,128]{2,1,0:T(8,128)S(1)} all-to-all(f32[16,8,128]{2,1,0:T(8,128)S(1)} %shard_map.67), channel_id=1, replica_groups=mesh['x'=8,'y'=8,'core'=2,'col'=8] {'y','core'}, dimensions={0} | all-to-all | bytes 131072 | tf_op jit(solution)/shard_map/all_to_all | solution.py:259
  82.2 13.7 %all_to_all.21.parts_ref = f32[8,8,128]{2,1,0:T(8,128)S(1)} all-to-all(f32[8,8,128]{2,1,0:T(8,128)S(1)} %shard_map.68), channel_id=1, replica_groups=mesh['x'=8,'y'=8,'core'=2,'col'=8] {'x'}, dimensions={0} | all-to-all | bytes 65536 | tf_op jit(solution)/shard_map/all_to_all | solution.py:261
  95.9 0.7 shard_map.69
  96.6 4.6 %all-to-all-start.3 = ((f32[64,8,128]{2,1,0:T(8,128)}), f32[64,8,128]{2,1,0:T(8,128)S(1)}, u32[]{:S(2)}, u32[]{:S(2)}) async-start(f32[64,8,128]{2,1,0:T(8,128)} %shard_map.69), calls=%async_computation.3 | async-start | bytes 524288 | tf_op jit(solution)/shard_map/all_to_all | solution.py:263
  101.3 12.5 %all-to-all-done.3 = f32[64,8,128]{2,1,0:T(8,128)S(1)} async-done(((f32[64,8,128]{2,1,0:T(8,128)}), f32[64,8,128]{2,1,0:T(8,128)S(1)}, u32[]{:S(2)}, u32[]{:S(2)}) %all-to-all-start.3) | async-done | bytes 262176 | tf_op jit(solution)/shard_map/all_to_all | solution.py:263
  113.8 5.4 %all-gather.3 = f32[128,8,128]{2,1,0:T(8,128)S(1)} all-gather(f32[64,8,128]{2,1,0:T(8,128)S(1)} %all-to-all-done.3), channel_id=5, replica_groups=mesh['x'=8,'y'=8,'core'=2,'col'=8] {'core'}, dimensions={0}, use_global_device_ids=true | all-gather | bytes 786432 | tf_op jit(solution)/shard_map/all_gather | solution.py:264
  119.2 10.4 %shard_map.70 = (f32[32,1024]{1,0:T(8,128)}, f32[256,256]{1,0:T(8,128)}) custom-call(s32[1]{0:T(128)} %bitcast.col_ref, f32[2,8,8,8,128]{4,3,2,1,0:T(8,128)S(1)} %bitcast.9, bf16[256,1024]{1,0:T(8,128)(2,1)S(1)} %bitcast.8), custom_call_target="tpu_custom_call" | custom-call | flops 200000000 | bytes 2097152 | tf_op jit(solution)/shard_map/pallas_call | solution.py:104
  (1 shorter events, 0.0 us)
Async XLA Ops:
  1.3 1.6 %copy-start = (bf16[1024,1024]{1,0:T(8,128)(2,1)S(1)}, bf16[1024,1024]{1,0:T(8,128)(2,1)}, u32[]{:S(2)}) copy-start(bf16[1024,1024]{1,0:T(8,128)(2,1)} %coupling_ref.7) | copy-start | bytes 6291460
  2.9 0.8 copy-start.4
  3.7 19.8 %copy-start.1 = (bf16[1024,1024]{1,0:T(8,128)(2,1)S(1)}, bf16[1024,1024]{1,0:T(8,128)(2,1)}, u32[]{:S(2)}) copy-start(bf16[1024,1024]{1,0:T(8,128)(2,1)} %coupling_ref.7) | copy-start | bytes 6291460
  4.2 19.3 %collective-permute-start = (f32[32,1024]{1,0:T(8,128)S(1)}, f32[32,1024]{1,0:T(8,128)S(1)}, u32[]{:S(2)}, u32[]{:S(2)}) collective-permute-start(f32[32,1024]{1,0:T(8,128)S(1)} %get-tuple-element.22), channel_id=1, source_target_pairs={{8,16},{16,8},{24,32},{32,24},{40,48},{48,40},{56,64},{64,56},{72,... | collective-permute-start | bytes 393224 | tf_op jit(solution)/shard_map/ppermute | solution.py:235
  20.8 1.6 %copy-start.2 = (bf16[1024,1024]{1,0:T(8,128)(2,1)S(1)}, bf16[1024,1024]{1,0:T(8,128)(2,1)}, u32[]{:S(2)}) copy-start(bf16[1024,1024]{1,0:T(8,128)(2,1)} %diag_ref.7) | copy-start | bytes 6291460
  23.4 5.1 %copy-start.3 = (bf16[1024,1024]{1,0:T(8,128)(2,1)S(1)}, bf16[1024,1024]{1,0:T(8,128)(2,1)}, u32[]{:S(2)}) copy-start(bf16[1024,1024]{1,0:T(8,128)(2,1)} %diag_ref.7) | copy-start | bytes 6291460
  24.6 6.3 %collective-permute-start.1 = (f32[32,1024]{1,0:T(8,128)S(1)}, f32[32,1024]{1,0:T(8,128)S(1)}, u32[]{:S(2)}, u32[]{:S(2)}) collective-permute-start(f32[32,1024]{1,0:T(8,128)S(1)} %get-tuple-element.27), channel_id=1, source_target_pairs={{8,16},{16,8},{24,32},{32,24},{40,48},{48,40},{56,64},{64,56},{72,... | collective-permute-start | bytes 393224 | tf_op jit(solution)/shard_map/ppermute | solution.py:235
  32.0 6.3 %collective-permute-start.2 = (f32[32,1024]{1,0:T(8,128)S(1)}, f32[32,1024]{1,0:T(8,128)S(1)}, u32[]{:S(2)}, u32[]{:S(2)}) collective-permute-start(f32[32,1024]{1,0:T(8,128)S(1)} %get-tuple-element.33), channel_id=1, source_target_pairs={{8,16},{16,8},{24,32},{32,24},{40,48},{48,40},{56,64},{64,56},{72,... | collective-permute-start | bytes 393224 | tf_op jit(solution)/shard_map/ppermute | solution.py:235
  40.1 24.9 %all-to-all-start = ((bf16[8,32,1024]{2,1,0:T(8,128)(2,1)}), bf16[8,32,1024]{2,1,0:T(8,128)(2,1)S(1)}, u32[]{:S(2)}, u32[]{:S(2)}) async-start(bf16[8,32,1024]{2,1,0:T(8,128)(2,1)} %get-tuple-element.41), calls=%async_computation | async-start | bytes 1048576 | tf_op jit(solution)/shard_map/all_to_all | solution.py:253
  47.1 6.2 %collective-permute-start.3 = (bf16[32,1024]{1,0:T(8,128)(2,1)S(1)}, bf16[32,1024]{1,0:T(8,128)(2,1)S(1)}, u32[]{:S(2)}, u32[]{:S(2)}) collective-permute-start(bf16[32,1024]{1,0:T(8,128)(2,1)S(1)} %get-tuple-element.40), channel_id=1, source_target_pairs={{0,8},{8,16},{16,24},{24,32},{32,40},{40,48},{48,56},{56,64},{64,7... | collective-permute-start | bytes 196616 | tf_op jit(solution)/shard_map/ppermute | solution.py:252
  96.6 17.2 %all-to-all-start.3 = ((f32[64,8,128]{2,1,0:T(8,128)}), f32[64,8,128]{2,1,0:T(8,128)S(1)}, u32[]{:S(2)}, u32[]{:S(2)}) async-start(f32[64,8,128]{2,1,0:T(8,128)} %shard_map.69), calls=%async_computation.3 | async-start | bytes 524288 | tf_op jit(solution)/shard_map/all_to_all | solution.py:263

commit v4 on v3

--- a/solution.py
+++ b/solution.py
@@ -12,11 +12,15 @@
 HIGH = lax.Precision.HIGHEST
 CENTER = 0.5
 HALF = 2.0
+PLAIN = (((1,), (0,)), ((), ()))
 TRANSPOSED = (((1,), (1,)), ((), ()))
 FIRST_WITH_FIRST = (((0,), (0,)), ((), ()))
 ALONG_X, ALONG_Y, CORES = 8, 8, 2
 DOM = ("x", "y", "core")
 WIDE = 64
+EVALUATIONS = 3
+CLOSE = 1.6e-5
+CHUNKS = 4
 F32 = jnp.float32
 BF16 = jnp.bfloat16
 
@@ -67,37 +71,77 @@
             x_ref[s + w :, :] = x_ref[s + w :, :] - change[:, n:]
 
 
-def finish_kernel(col_ref, sums_ref, all_ref, basis_ref, reduced_ref, a_ref, q_ref, x_ref, inv_ref):
+def halves(array):
+    high = array.astype(BF16)
+    return high, (array - high.astype(F32)).astype(BF16)
+
+
+def product(left, right, dims):
+    return lax.dot_general(left, right, dims, preferred_element_type=F32)
+
+
+def product_of_halves(left, right, dims):
+    small = product(left[0], right[1], dims) + product(left[1], right[0], dims)
+    return product(left[0], right[0], dims) + small
+
+
+def newton_inverse(gram, inv_ref):
+    n = gram.shape[0]
+    i = lax.broadcasted_iota(jnp.int32, (n, n), 0)
+    j = lax.broadcasted_iota(jnp.int32, (n, n), 1)
+    diagonal = jnp.where(i == j, gram, 0.0)
+    down = lax.rsqrt(jnp.sum(diagonal, axis=1, keepdims=True))
+    along = lax.rsqrt(jnp.sum(diagonal, axis=0, keepdims=True))
+    ident = jnp.where(i == j, 1.0, 0.0)
+    weight = jnp.where(i > j, 1.0, 0.5 * ident)
+    scaled = jnp.where(i == j, 1.0, gram * down * along)
+    parts = halves(scaled)
+    x = jnp.where(i > j, -scaled, ident)
+    for step in range(EVALUATIONS):
+        xs = halves(x)
+        if step == 0:
+            moved = product(xs[0], parts[0], PLAIN).astype(BF16)
+            error = product(moved, xs[0], TRANSPOSED) - ident
+        else:
+            moved = halves(product_of_halves(xs, parts, PLAIN))
+            error = product_of_halves(moved, xs, TRANSPOSED) - ident
+        x = x - product((error * weight).astype(BF16), xs[0], PLAIN)
+    inv_ref[...] = x * along
+    return jnp.sum(error * error)
+
+
+def finish_kernel(place_ref, sums_ref, all_ref, basis_ref, reduced_ref, a_ref, q_ref, x_ref, inv_ref):
     cores, along, cols, eight, lanes = sums_ref.shape
     local = basis_ref.shape[0]
     tiles = cores * along
     per_matrix = tiles // 2
-    halves = a_ref.shape[1] // lanes
+    across = a_ref.shape[1] // lanes
     for t in range(tiles):
         target = a_ref if t < per_matrix else q_ref
-        block, half = divmod(t % per_matrix, halves)
+        block, half = divmod(t % per_matrix, across)
         for z in range(cols):
             top = z * local + block * eight
             target[top : top + eight, half * lanes : (half + 1) * lanes] = sums_ref[t % cores, t // cores, z]
-    cholesky_inverse(a_ref, x_ref, inv_ref)
+    residual = newton_inverse(a_ref[...], inv_ref)
+
+    @pl.when(jnp.logical_not(residual < CLOSE))
+    def _():
+        cholesky_inverse(a_ref, x_ref, inv_ref)
+
     proj = q_ref[...]
-    proj = 0.5 * (proj + proj.T)
-    inverse = inv_ref[...]
-    left = jnp.dot(inverse, proj, precision=HIGH, preferred_element_type=F32)
-    reduced_ref[...] = lax.dot_general(
-        left, inverse, TRANSPOSED, precision=HIGH, preferred_element_type=F32
-    )
+    inverse = halves(inv_ref[...])
+    left = product_of_halves(inverse, halves(0.5 * (proj + proj.T)), PLAIN)
+    reduced_ref[...] = product_of_halves(halves(left), inverse, TRANSPOSED)
     scale = math.sqrt(ALONG_X * ALONG_Y * CORES * basis_ref.shape[1])
-    mine = scale * inv_ref[pl.ds(pl.multiple_of(col_ref[0] * local, local), local), :]
-    high = mine.astype(BF16)
-    low = (mine - high.astype(F32)).astype(BF16)
+    mine = scale * inv_ref[pl.ds(pl.multiple_of(place_ref[1] * local, local), local), :]
+    high, low = halves(mine)
     states = all_ref[...]
     basis_ref[...] = jnp.dot(high, states, preferred_element_type=F32) + jnp.dot(
         low, states, preferred_element_type=F32
     )
 
 
-def finish(col, sums, all_states, local):
+def finish(place, sums, all_states, local):
     total, rows = all_states.shape
     vmem = pl.BlockSpec(memory_space=pltpu.VMEM)
     square = pltpu.VMEM((total, total), F32)
@@ -112,7 +156,7 @@
         scratch_shapes=[square] * 4,
         compiler_params=pltpu.CompilerParams(vmem_limit_bytes=32 * 2**20),
         cost_estimate=pl.CostEstimate(flops=2 * 10**8, bytes_accessed=2**21, transcendentals=0),
-    )(col, sums, all_states)
+    )(place, sums, all_states)
 
 
 def across_pairs(count):
@@ -137,18 +181,59 @@
     return lax.broadcasted_iota(jnp.int32, (1, shape[1]), 1) < counts_ref[0]
 
 
-def send_off(even, block, low, coupling_ref, over_ref, on_ref):
-    onward = jnp.dot(low, coupling_ref[...], preferred_element_type=F32)
+def send_off(even, block, onward, over_ref, on_ref):
     over_ref[...] = jnp.where(even, block, onward)
     on_ref[...] = jnp.where(even, onward, block)
 
 
-def first_kernel(counts_ref, core_ref, states_ref, coupling_ref, low_ref, over_ref, on_ref):
+def first_kernel(
+    counts_ref, place_ref, states_any, coupling_any, low_ref, over_ref, on_ref,
+    states_ref, coupling_ref, sems,
+):
+    depth = coupling_ref.shape[0] // CHUNKS
+    chunks = [pl.ds(k * depth, depth) for k in range(CHUNKS)]
+    whole = pltpu.make_async_copy(states_any, states_ref, sems.at[CHUNKS])
+    whole.start()
+    copies = [
+        pltpu.make_async_copy(coupling_any.at[rows], coupling_ref.at[rows], sems.at[k])
+        for k, rows in enumerate(chunks)
+    ]
+    for copy in copies:
+        copy.start()
+    whole.wait()
     live = live_row(counts_ref, states_ref.shape)
     block = jnp.where(live, states_ref[...].astype(F32), 0.0)
     low = block.astype(BF16)
     low_ref[...] = low
-    send_off(core_ref[0] == 0, block, low, coupling_ref, over_ref, on_ref)
+    onward = jnp.zeros_like(block)
+    for k, copy in enumerate(copies):
+        copy.wait()
+        onward = onward + jnp.dot(
+            low[:, k * depth : (k + 1) * depth],
+            coupling_ref[k * depth : (k + 1) * depth, :],
+            preferred_element_type=F32,
+        )
+    send_off(place_ref[0] == 0, block, onward, over_ref, on_ref)
+
+
+def first(counts, place, states, coupling):
+    block = states.shape
+    vmem = pl.BlockSpec(memory_space=pltpu.VMEM)
+    smem = pl.BlockSpec(memory_space=pltpu.SMEM)
+    left = pl.BlockSpec(memory_space=pltpu.HBM)
+    return pl.pallas_call(
+        first_kernel,
+        out_shape=tuple(jax.ShapeDtypeStruct(block, dtype) for dtype in (BF16, F32, F32)),
+        in_specs=[smem, smem, left, left],
+        out_specs=(vmem,) * 3,
+        scratch_shapes=[
+            pltpu.VMEM(block, BF16),
+            pltpu.VMEM(coupling.shape, BF16),
+            pltpu.SemaphoreType.DMA((CHUNKS + 1,)),
+        ],
+        compiler_params=pltpu.CompilerParams(vmem_limit_bytes=59 * 2**20),
+        cost_estimate=pl.CostEstimate(flops=2**16, bytes_accessed=2**16, transcendentals=0),
+    )(counts, place, states, coupling)
 
 
 def own_kernel(low_ref, diag_ref, own_ref):
@@ -174,22 +259,23 @@
     return 2.0 * shifted - prev_ref[...].astype(F32)
 
 
-def step_kernel(counts_ref, core_ref, over_ref, both_ref, own_ref, coupling_ref, cur_ref, *rest):
+def step_kernel(counts_ref, place_ref, over_ref, both_ref, own_ref, coupling_ref, cur_ref, *rest):
     prev_ref = rest[0] if len(rest) == 5 else None
     next_ref, low_ref, over_out, on_out = rest[-4:]
-    even = core_ref[0] == 0
+    even = place_ref[0] == 0
     block = recur(counts_ref, even, over_ref, both_ref, own_ref, cur_ref, prev_ref, coupling_ref)
     low = block.astype(BF16)
     next_ref[...] = block
     low_ref[...] = low
-    send_off(even, block, low, coupling_ref, over_out, on_out)
+    onward = jnp.dot(low, coupling_ref[...], preferred_element_type=F32)
+    send_off(even, block, onward, over_out, on_out)
 
 
 def last_kernel(
-    counts_ref, core_ref, over_ref, both_ref, own_ref, coupling_ref, cur_ref, prev_ref,
+    counts_ref, place_ref, over_ref, both_ref, own_ref, coupling_ref, cur_ref, prev_ref,
     filtered_ref, copies_ref, onward_ref,
 ):
-    even = core_ref[0] == 0
+    even = place_ref[0] == 0
     block = recur(counts_ref, even, over_ref, both_ref, own_ref, cur_ref, prev_ref, coupling_ref)
     low = block.astype(BF16)
     filtered_ref[...] = low
@@ -224,19 +310,17 @@
     local, rows = states.shape
     block = (local, rows)
     domains, cols = lax.axis_size(DOM), lax.axis_size("col")
-    core = lax.axis_index("core").astype(jnp.int32).reshape(1)
+    place = jnp.stack([lax.axis_index("core"), lax.axis_index("col")]).astype(jnp.int32)
     trade = [(block, F32), (block, F32)]
 
-    low, over, on = local_kernel(
-        first_kernel, [(block, BF16)] + trade, counts, core, states, coupling, scalars=2
-    )
+    low, over, on = first(counts, place, states, coupling)
     history = [low]
     for step in range(DEGREE):
         over = lax.ppermute(over, DOM, across_pairs(domains))
         both = lax.all_gather(on, "core")
         low, both = lax.optimization_barrier((low, both))
         (own,) = local_kernel(own_kernel, [(block, F32)], low, diag_blocks)
-        args = (counts, core, over, both, own, coupling, *history[:-3:-1])
+        args = (counts, place, over, both, own, coupling, *history[:-3:-1])
         if step < DEGREE - 1:
             cur, low, over, on = local_kernel(
                 step_kernel, [(block, F32), (block, BF16)] + trade, *args, scalars=2
@@ -262,8 +346,7 @@
     (copies,) = local_kernel(sum_kernel, [((ALONG_Y * cols, 8, 128), F32)], parts)
     shares = lax.all_to_all(copies, ("y", "col"), 0, 0)
     sums = lax.all_gather(shares, "core").reshape(CORES, ALONG_Y, cols, 8, 128)
-    col = lax.axis_index("col").astype(jnp.int32).reshape(1)
-    return finish(col, sums, all_states, local)
+    return finish(place, sums, all_states, local)
 
 
 def solution(mesh):

time: 130 us -> 134 us (1.031)
  blocking collectives: 51.8 us -> 68.9 us
  waiting for transfers between devices: 27.3 us -> 14.8 us
  Pallas kernels: 19.6 us -> 25.7 us
  starting transfers between devices: 25.6 us -> 20.8 us
  local copies, waits for them, and re-layouts: 4.03 us -> 0.86 us
    all_to_all x0 -> x1, blocking collectives: none -> 16.3 us  [body(): shares = lax.all_to_all(copies, ('y', 'col'), 0, 0)]
    all_to_all x1 -> x0, waiting for transfers between devices: 12.5 us -> none  [body(): shares = lax.all_to_all(copies, ('y', 'col'), 0, 0)]
    all_to_all x1 -> x0, starting transfers between devices: 4.62 us -> none  [body(): shares = lax.all_to_all(copies, ('y', 'col'), 0, 0)]
    pallas_call x0 -> x1, Pallas kernels: none -> 3.29 us  [first(): pl.pallas_call(first_kernel, out_shape=tuple((jax.ShapeDtypeStruct(block,...]
    unnamed x10, local copies, waits for them, and re-layouts: 4.03 us -> 0.86 us
    pallas_call x1, Pallas kernels: 10.4 us -> 12.7 us  [finish(): pl.pallas_call(finish_kernel, out_shape=(jax.ShapeDtypeStruct((local, row...]
    pallas_call x11 -> x10, Pallas kernels: 9.19 us -> 9.64 us  [local_kernel(): pl.pallas_call(kernel, out_shape=tuple((jax.ShapeDtypeStruct(shape, dtype...]
  transfers between devices with their start and end apart: 6 -> 5, of which waited for: 5 -> 4; matrix products, arithmetic and copies ran while one was open for 0% -> 0% of each run, Pallas kernels for 3% -> 3%
where the time goes in v4:
time: 134 us; the launch traced here: 133 us
  blocking collectives  68.9 us (51%)
  Pallas kernels  25.7 us (19%)
  starting transfers between devices  20.8 us (16%)
  waiting for transfers between devices  14.8 us (11%)
  between operations  1.54 us (1%)
    all_to_all x1, blocking collectives, body(): parts = lax.all_to_all(tiles, ('y', 'core'), 0, 0)  16.7 us
    all_to_all x1, blocking collectives, body(): shares = lax.all_to_all(copies, ('y', 'col'), 0, 0)  16.3 us
    all_gather x3, blocking collectives, body(): both = lax.all_gather(on, 'core')  15.9 us
    all_to_all x1, blocking collectives, body(): parts = lax.all_to_all(copies, 'x', 0, 0)  14.6 us
    pallas_call x1, Pallas kernels, finish(): pl.pallas_call(finish_kernel, out_shape=(jax.ShapeDtypeStruct((local, row...  12.7 us
    all_to_all x1, waiting for transfers between devices, body(): all_states = lax.all_to_all(copies, 'col', 0, 0).reshape(cols * local, rows)  11.8 us
    pallas_call x10, Pallas kernels, local_kernel(): pl.pallas_call(kernel, out_shape=tuple((jax.ShapeDtypeStruct(shape, dtype...  9.64 us
    ppermute x3, starting transfers between devices, body(): over = lax.ppermute(over, DOM, across_pairs(domains))  9 us
  transfers between devices with their start and end apart: 5, of which 4 were waited for; matrix products, arithmetic and copies ran while one was open for 0% of the time, Pallas kernels for 3%

profile of v4, /device:TPU:1, one launch (start us, length us, event | category | flops | bytes accessed | tf_op | source)
XLA Modules:
  0.0 133.2 jit_solution(9435721756308840270)
XLA Ops:
  0.6 0.0 copy-start.1
  1.4 0.7 pad_add_fusion.place_ref
  2.1 0.0 copy-start
  2.1 3.3 %shard_map.59 = (bf16[32,1024]{1,0:T(8,128)(2,1)}, f32[32,1024]{1,0:T(8,128)}, f32[32,1024]{1,0:T(8,128)}) custom-call(s32[1]{0:T(128)S(6)} %copy.6.counts_ref, s32[2]{0:T(128)} %pad_add_fusion.place_ref, bf16[32,1024]{1,0:T(8,128)(2,1)} %states_any.1, bf16[1024,1024]{1,0:T(8,128)(2,1)} %coupling_ref.5), custom_call_target="tpu_custom_call" | custom-call | flops 65536 | bytes 65536 | tf_op jit(solution)/shard_map/pallas_call | solution.py:224
  5.4 4.7 %collective-permute-start = (f32[32,1024]{1,0:T(8,128)}, f32[32,1024]{1,0:T(8,128)S(1)}, u32[]{:S(2)}, u32[]{:S(2)}) collective-permute-start(f32[32,1024]{1,0:T(8,128)} %get-tuple-element.22), channel_id=1, source_target_pairs={{8,16},{16,8},{24,32},{32,24},{40,48},{48,40},{56,64},{64,56},{72,... | collective-permute-start | bytes 393224 | tf_op jit(solution)/shard_map/ppermute | solution.py:319
  10.1 12.0 %all-gather = f32[64,1024]{1,0:T(8,128)S(1)} all-gather(f32[32,1024]{1,0:T(8,128)} %get-tuple-element.24), channel_id=2, replica_groups=mesh['x'=8,'y'=8,'core'=2,'col'=8] {'core'}, dimensions={0}, use_global_device_ids=true | all-gather | bytes 393216 | tf_op jit(solution)/shard_map/all_gather | solution.py:320
  22.1 0.0 copy-done.1
  22.1 0.0 copy-start.2
  22.1 0.8 copy-done.2
  22.9 0.0 copy-start.3
  22.9 0.0 copy-start.4
  22.9 1.1 shard_map.60.own_ref
  24.0 0.0 collective-permute-done.over_ref
  24.0 0.0 copy-done
  24.0 0.0 copy-done.3
  24.0 0.0 copy-done.4
  24.0 1.6 %shard_map.61 = (f32[32,1024]{1,0:T(8,128)S(1)}, bf16[32,1024]{1,0:T(8,128)(2,1)S(1)}, f32[32,1024]{1,0:T(8,128)S(1)}, f32[32,1024]{1,0:T(8,128)S(1)}) custom-call(s32[1]{0:T(128)S(6)} %copy.6.counts_ref, s32[2]{0:T(128)S(1)} %copy-done.4, f32[32,1024]{1,0:T(8,128)S(1)} %collective-permute-done.over_ref, f32[2,32,1024]{2,1,0:T(8,128)S(1)} %bitcast.11, ...), custom_call_target="tpu_custom_call" | custom-call | flops 65536 | bytes 65536 | tf_op jit(solution)/shard_map/pallas_call | solution.py:170
  25.7 1.9 %collective-permute-start.1 = (f32[32,1024]{1,0:T(8,128)S(1)}, f32[32,1024]{1,0:T(8,128)S(1)}, u32[]{:S(2)}, u32[]{:S(2)}) collective-permute-start(f32[32,1024]{1,0:T(8,128)S(1)} %get-tuple-element.27), channel_id=1, source_target_pairs={{8,16},{16,8},{24,32},{32,24},{40,48},{48,40},{56,64},{64,56},{72,... | collective-permute-start | bytes 393224 | tf_op jit(solution)/shard_map/ppermute | solution.py:319
  27.6 2.0 %all-gather.1 = f32[64,1024]{1,0:T(8,128)S(1)} all-gather(f32[32,1024]{1,0:T(8,128)S(1)} %get-tuple-element.29), channel_id=3, replica_groups=mesh['x'=8,'y'=8,'core'=2,'col'=8] {'core'}, dimensions={0}, use_global_device_ids=true | all-gather | bytes 393216 | tf_op jit(solution)/shard_map/all_gather | solution.py:320
  29.6 1.1 shard_map.62.own_ref
  30.7 1.3 collective-permute-done.1.over_ref
  32.0 1.7 %shard_map.63 = (f32[32,1024]{1,0:T(8,128)S(1)}, bf16[32,1024]{1,0:T(8,128)(2,1)S(1)}, f32[32,1024]{1,0:T(8,128)S(1)}, f32[32,1024]{1,0:T(8,128)S(1)}) custom-call(s32[1]{0:T(128)S(6)} %copy.6.counts_ref, s32[2]{0:T(128)S(1)} %copy-done.4, f32[32,1024]{1,0:T(8,128)S(1)} %collective-permute-done.1.over_ref, f32[2,32,1024]{2,1,0:T(8,128)S(1)} %bitcast.10, ...), custom_call_target="tpu_custom_call" | custom-call | flops 65536 | bytes 65536 | tf_op jit(solution)/shard_map/pallas_call | solution.py:170
  33.7 2.4 %collective-permute-start.2 = (f32[32,1024]{1,0:T(8,128)S(1)}, f32[32,1024]{1,0:T(8,128)S(1)}, u32[]{:S(2)}, u32[]{:S(2)}) collective-permute-start(f32[32,1024]{1,0:T(8,128)S(1)} %get-tuple-element.33), channel_id=1, source_target_pairs={{8,16},{16,8},{24,32},{32,24},{40,48},{48,40},{56,64},{64,56},{72,... | collective-permute-start | bytes 393224 | tf_op jit(solution)/shard_map/ppermute | solution.py:319
  36.0 2.0 %all-gather.2 = f32[64,1024]{1,0:T(8,128)S(1)} all-gather(f32[32,1024]{1,0:T(8,128)S(1)} %get-tuple-element.35), channel_id=4, replica_groups=mesh['x'=8,'y'=8,'core'=2,'col'=8] {'core'}, dimensions={0}, use_global_device_ids=true | all-gather | bytes 393216 | tf_op jit(solution)/shard_map/all_gather | solution.py:320
  38.0 1.1 shard_map.64.own_ref
  39.1 0.8 collective-permute-done.2.over_ref
  39.9 2.3 %shard_map.65 = (bf16[32,1024]{1,0:T(8,128)(2,1)S(1)}, bf16[8,32,1024]{2,1,0:T(8,128)(2,1)}, bf16[32,1024]{1,0:T(8,128)(2,1)S(1)}) custom-call(s32[1]{0:T(128)S(6)} %copy.6.counts_ref, s32[2]{0:T(128)S(1)} %copy-done.4, f32[32,1024]{1,0:T(8,128)S(1)} %collective-permute-done.2.over_ref, f32[2,32,1024]{2,1,0:T(8,128)S(1)} %bitcast.12, ...), custom_call_target="tpu_custom_call" | custom-call | flops 65536 | bytes 65536 | tf_op jit(solution)/shard_map/pallas_call | solution.py:170
  42.3 7.0 %all-to-all-start = ((bf16[8,32,1024]{2,1,0:T(8,128)(2,1)}), bf16[8,32,1024]{2,1,0:T(8,128)(2,1)S(1)}, u32[]{:S(2)}, u32[]{:S(2)}) async-start(bf16[8,32,1024]{2,1,0:T(8,128)(2,1)} %get-tuple-element.41), calls=%async_computation | async-start | bytes 1048576 | tf_op jit(solution)/shard_map/all_to_all | solution.py:337
  49.2 4.8 %collective-permute-start.3 = (bf16[32,1024]{1,0:T(8,128)(2,1)S(1)}, bf16[32,1024]{1,0:T(8,128)(2,1)S(1)}, u32[]{:S(2)}, u32[]{:S(2)}) collective-permute-start(bf16[32,1024]{1,0:T(8,128)(2,1)S(1)} %get-tuple-element.40), channel_id=1, source_target_pairs={{0,8},{8,16},{16,24},{24,32},{32,40},{40,48},{48,56},{56,64},{64,7... | collective-permute-start | bytes 196616 | tf_op jit(solution)/shard_map/ppermute | solution.py:336
  54.1 0.5 shard_map.66.product_ref
  54.5 0.9 collective-permute-done.3.arrived_ref
  55.4 11.8 %all-to-all-done = bf16[8,32,1024]{2,1,0:T(8,128)(2,1)S(1)} async-done(((bf16[8,32,1024]{2,1,0:T(8,128)(2,1)}), bf16[8,32,1024]{2,1,0:T(8,128)(2,1)S(1)}, u32[]{:S(2)}, u32[]{:S(2)}) %all-to-all-start) | async-done | bytes 524320 | tf_op jit(solution)/shard_map/all_to_all | solution.py:337
  67.2 0.3 shard_map.67
  67.5 16.7 %all_to_all.20.parts_ref = f32[16,8,128]{2,1,0:T(8,128)S(1)} all-to-all(f32[16,8,128]{2,1,0:T(8,128)S(1)} %shard_map.67), channel_id=1, replica_groups=mesh['x'=8,'y'=8,'core'=2,'col'=8] {'y','core'}, dimensions={0} | all-to-all | bytes 131072 | tf_op jit(solution)/shard_map/all_to_all | solution.py:343
  84.2 14.6 %all_to_all.21.parts_ref = f32[8,8,128]{2,1,0:T(8,128)S(1)} all-to-all(f32[8,8,128]{2,1,0:T(8,128)S(1)} %shard_map.68), channel_id=1, replica_groups=mesh['x'=8,'y'=8,'core'=2,'col'=8] {'x'}, dimensions={0} | all-to-all | bytes 65536 | tf_op jit(solution)/shard_map/all_to_all | solution.py:345
  98.9 16.3 %all_to_all.22 = f32[64,8,128]{2,1,0:T(8,128)S(1)} all-to-all(f32[64,8,128]{2,1,0:T(8,128)S(1)} %shard_map.69), channel_id=1, replica_groups=mesh['x'=8,'y'=8,'core'=2,'col'=8] {'y','col'}, dimensions={0} | all-to-all | bytes 524288 | tf_op jit(solution)/shard_map/all_to_all | solution.py:347
  115.2 5.3 %all-gather.3 = f32[128,8,128]{2,1,0:T(8,128)S(1)} all-gather(f32[64,8,128]{2,1,0:T(8,128)S(1)} %all_to_all.22), channel_id=5, replica_groups=mesh['x'=8,'y'=8,'core'=2,'col'=8] {'core'}, dimensions={0}, use_global_device_ids=true | all-gather | bytes 786432 | tf_op jit(solution)/shard_map/all_gather | solution.py:348
  120.5 12.7 %shard_map.70 = (f32[32,1024]{1,0:T(8,128)}, f32[256,256]{1,0:T(8,128)}) custom-call(s32[2]{0:T(128)S(1)} %copy-done.4, f32[2,8,8,8,128]{4,3,2,1,0:T(8,128)S(1)} %bitcast.9, bf16[256,1024]{1,0:T(8,128)(2,1)S(1)} %bitcast.8), custom_call_target="tpu_custom_call" | custom-call | flops 200000000 | bytes 2097152 | tf_op jit(solution)/shard_map/pallas_call | solution.py:148
  (2 shorter events, 0.0 us)
Async XLA Ops:
  0.6 21.4 %copy-start.1 = (bf16[1024,1024]{1,0:T(8,128)(2,1)S(1)}, bf16[1024,1024]{1,0:T(8,128)(2,1)}, u32[]{:S(2)}) copy-start(bf16[1024,1024]{1,0:T(8,128)(2,1)} %diag_ref.7) | copy-start | bytes 6291460
  2.1 21.9 %copy-start = (bf16[1024,1024]{1,0:T(8,128)(2,1)S(1)}, bf16[1024,1024]{1,0:T(8,128)(2,1)}, u32[]{:S(2)}) copy-start(bf16[1024,1024]{1,0:T(8,128)(2,1)} %coupling_ref.5) | copy-start | bytes 6291460
  5.4 18.6 %collective-permute-start = (f32[32,1024]{1,0:T(8,128)}, f32[32,1024]{1,0:T(8,128)S(1)}, u32[]{:S(2)}, u32[]{:S(2)}) collective-permute-start(f32[32,1024]{1,0:T(8,128)} %get-tuple-element.22), channel_id=1, source_target_pairs={{8,16},{16,8},{24,32},{32,24},{40,48},{48,40},{56,64},{64,56},{72,... | collective-permute-start | bytes 393224 | tf_op jit(solution)/shard_map/ppermute | solution.py:319
  22.1 0.8 copy-start.2
  22.9 1.1 copy-start.3
  22.9 1.1 copy-start.4
  25.7 6.3 %collective-permute-start.1 = (f32[32,1024]{1,0:T(8,128)S(1)}, f32[32,1024]{1,0:T(8,128)S(1)}, u32[]{:S(2)}, u32[]{:S(2)}) collective-permute-start(f32[32,1024]{1,0:T(8,128)S(1)} %get-tuple-element.27), channel_id=1, source_target_pairs={{8,16},{16,8},{24,32},{32,24},{40,48},{48,40},{56,64},{64,56},{72,... | collective-permute-start | bytes 393224 | tf_op jit(solution)/shard_map/ppermute | solution.py:319
  33.7 6.3 %collective-permute-start.2 = (f32[32,1024]{1,0:T(8,128)S(1)}, f32[32,1024]{1,0:T(8,128)S(1)}, u32[]{:S(2)}, u32[]{:S(2)}) collective-permute-start(f32[32,1024]{1,0:T(8,128)S(1)} %get-tuple-element.33), channel_id=1, source_target_pairs={{8,16},{16,8},{24,32},{32,24},{40,48},{48,40},{56,64},{64,56},{72,... | collective-permute-start | bytes 393224 | tf_op jit(solution)/shard_map/ppermute | solution.py:319
  42.3 24.9 %all-to-all-start = ((bf16[8,32,1024]{2,1,0:T(8,128)(2,1)}), bf16[8,32,1024]{2,1,0:T(8,128)(2,1)S(1)}, u32[]{:S(2)}, u32[]{:S(2)}) async-start(bf16[8,32,1024]{2,1,0:T(8,128)(2,1)} %get-tuple-element.41), calls=%async_computation | async-start | bytes 1048576 | tf_op jit(solution)/shard_map/all_to_all | solution.py:337
  49.2 6.2 %collective-permute-start.3 = (bf16[32,1024]{1,0:T(8,128)(2,1)S(1)}, bf16[32,1024]{1,0:T(8,128)(2,1)S(1)}, u32[]{:S(2)}, u32[]{:S(2)}) collective-permute-start(bf16[32,1024]{1,0:T(8,128)(2,1)S(1)} %get-tuple-element.40), channel_id=1, source_target_pairs={{0,8},{8,16},{16,24},{24,32},{32,40},{40,48},{48,56},{56,64},{64,7... | collective-permute-start | bytes 196616 | tf_op jit(solution)/shard_map/ppermute | solution.py:336

commit v5 on v4

--- a/solution.py
+++ b/solution.py
@@ -20,7 +20,6 @@
 WIDE = 64
 EVALUATIONS = 3
 CLOSE = 1.6e-5
-CHUNKS = 4
 F32 = jnp.float32
 BF16 = jnp.bfloat16
 
@@ -110,7 +109,7 @@
     return jnp.sum(error * error)
 
 
-def finish_kernel(place_ref, sums_ref, all_ref, basis_ref, reduced_ref, a_ref, q_ref, x_ref, inv_ref):
+def finish_kernel(col_ref, sums_ref, all_ref, basis_ref, reduced_ref, a_ref, q_ref, x_ref, inv_ref):
     cores, along, cols, eight, lanes = sums_ref.shape
     local = basis_ref.shape[0]
     tiles = cores * along
@@ -133,7 +132,7 @@
     left = product_of_halves(inverse, halves(0.5 * (proj + proj.T)), PLAIN)
     reduced_ref[...] = product_of_halves(halves(left), inverse, TRANSPOSED)
     scale = math.sqrt(ALONG_X * ALONG_Y * CORES * basis_ref.shape[1])
-    mine = scale * inv_ref[pl.ds(pl.multiple_of(place_ref[1] * local, local), local), :]
+    mine = scale * inv_ref[pl.ds(pl.multiple_of(col_ref[0] * local, local), local), :]
     high, low = halves(mine)
     states = all_ref[...]
     basis_ref[...] = jnp.dot(high, states, preferred_element_type=F32) + jnp.dot(
@@ -141,7 +140,7 @@
     )
 
 
-def finish(place, sums, all_states, local):
+def finish(col, sums, all_states, local):
     total, rows = all_states.shape
     vmem = pl.BlockSpec(memory_space=pltpu.VMEM)
     square = pltpu.VMEM((total, total), F32)
@@ -156,7 +155,7 @@
         scratch_shapes=[square] * 4,
         compiler_params=pltpu.CompilerParams(vmem_limit_bytes=32 * 2**20),
         cost_estimate=pl.CostEstimate(flops=2 * 10**8, bytes_accessed=2**21, transcendentals=0),
-    )(place, sums, all_states)
+    )(col, sums, all_states)
 
 
 def across_pairs(count):
@@ -186,54 +185,10 @@
     on_ref[...] = jnp.where(even, onward, block)
 
 
-def first_kernel(
-    counts_ref, place_ref, states_any, coupling_any, low_ref, over_ref, on_ref,
-    states_ref, coupling_ref, sems,
-):
-    depth = coupling_ref.shape[0] // CHUNKS
-    chunks = [pl.ds(k * depth, depth) for k in range(CHUNKS)]
-    whole = pltpu.make_async_copy(states_any, states_ref, sems.at[CHUNKS])
-    whole.start()
-    copies = [
-        pltpu.make_async_copy(coupling_any.at[rows], coupling_ref.at[rows], sems.at[k])
-        for k, rows in enumerate(chunks)
-    ]
-    for copy in copies:
-        copy.start()
-    whole.wait()
-    live = live_row(counts_ref, states_ref.shape)
-    block = jnp.where(live, states_ref[...].astype(F32), 0.0)
-    low = block.astype(BF16)
-    low_ref[...] = low
-    onward = jnp.zeros_like(block)
-    for k, copy in enumerate(copies):
-        copy.wait()
-        onward = onward + jnp.dot(
-            low[:, k * depth : (k + 1) * depth],
-            coupling_ref[k * depth : (k + 1) * depth, :],
-            preferred_element_type=F32,
-        )
-    send_off(place_ref[0] == 0, block, onward, over_ref, on_ref)
-
-
-def first(counts, place, states, coupling):
-    block = states.shape
-    vmem = pl.BlockSpec(memory_space=pltpu.VMEM)
-    smem = pl.BlockSpec(memory_space=pltpu.SMEM)
-    left = pl.BlockSpec(memory_space=pltpu.HBM)
-    return pl.pallas_call(
-        first_kernel,
-        out_shape=tuple(jax.ShapeDtypeStruct(block, dtype) for dtype in (BF16, F32, F32)),
-        in_specs=[smem, smem, left, left],
-        out_specs=(vmem,) * 3,
-        scratch_shapes=[
-            pltpu.VMEM(block, BF16),
-            pltpu.VMEM(coupling.shape, BF16),
-            pltpu.SemaphoreType.DMA((CHUNKS + 1,)),
-        ],
-        compiler_params=pltpu.CompilerParams(vmem_limit_bytes=59 * 2**20),
-        cost_estimate=pl.CostEstimate(flops=2**16, bytes_accessed=2**16, transcendentals=0),
-    )(counts, place, states, coupling)
+def first_kernel(core_ref, low_ref, coupling_ref, over_ref, on_ref):
+    low = low_ref[...]
+    onward = jnp.dot(low, coupling_ref[...], preferred_element_type=F32)
+    send_off(core_ref[0] == 0, low.astype(F32), onward, over_ref, on_ref)
 
 
 def own_kernel(low_ref, diag_ref, own_ref):
@@ -259,10 +214,10 @@
     return 2.0 * shifted - prev_ref[...].astype(F32)
 
 
-def step_kernel(counts_ref, place_ref, over_ref, both_ref, own_ref, coupling_ref, cur_ref, *rest):
+def step_kernel(counts_ref, core_ref, over_ref, both_ref, own_ref, coupling_ref, cur_ref, *rest):
     prev_ref = rest[0] if len(rest) == 5 else None
     next_ref, low_ref, over_out, on_out = rest[-4:]
-    even = place_ref[0] == 0
+    even = core_ref[0] == 0
     block = recur(counts_ref, even, over_ref, both_ref, own_ref, cur_ref, prev_ref, coupling_ref)
     low = block.astype(BF16)
     next_ref[...] = block
@@ -272,10 +227,10 @@
 
 
 def last_kernel(
-    counts_ref, place_ref, over_ref, both_ref, own_ref, coupling_ref, cur_ref, prev_ref,
+    counts_ref, core_ref, over_ref, both_ref, own_ref, coupling_ref, cur_ref, prev_ref,
     filtered_ref, copies_ref, onward_ref,
 ):
-    even = place_ref[0] == 0
+    even = core_ref[0] == 0
     block = recur(counts_ref, even, over_ref, both_ref, own_ref, cur_ref, prev_ref, coupling_ref)
     low = block.astype(BF16)
     filtered_ref[...] = low
@@ -310,17 +265,20 @@
     local, rows = states.shape
     block = (local, rows)
     domains, cols = lax.axis_size(DOM), lax.axis_size("col")
-    place = jnp.stack([lax.axis_index("core"), lax.axis_index("col")]).astype(jnp.int32)
+    core = lax.axis_index("core").astype(jnp.int32).reshape(1)
+    col = lax.axis_index("col").astype(jnp.int32).reshape(1)
     trade = [(block, F32), (block, F32)]
 
-    low, over, on = first(counts, place, states, coupling)
+    live = lax.iota(jnp.int32, rows) < counts[0]
+    low = jnp.where(live[None, :], states, jnp.zeros_like(states))
+    over, on = local_kernel(first_kernel, trade, core, low, coupling, scalars=1)
     history = [low]
     for step in range(DEGREE):
         over = lax.ppermute(over, DOM, across_pairs(domains))
         both = lax.all_gather(on, "core")
-        low, both = lax.optimization_barrier((low, both))
+        low, both, col = lax.optimization_barrier((low, both, col))
         (own,) = local_kernel(own_kernel, [(block, F32)], low, diag_blocks)
-        args = (counts, place, over, both, own, coupling, *history[:-3:-1])
+        args = (counts, core, over, both, own, coupling, *history[:-3:-1])
         if step < DEGREE - 1:
             cur, low, over, on = local_kernel(
                 step_kernel, [(block, F32), (block, BF16)] + trade, *args, scalars=2
@@ -346,7 +304,7 @@
     (copies,) = local_kernel(sum_kernel, [((ALONG_Y * cols, 8, 128), F32)], parts)
     shares = lax.all_to_all(copies, ("y", "col"), 0, 0)
     sums = lax.all_gather(shares, "core").reshape(CORES, ALONG_Y, cols, 8, 128)
-    return finish(place, sums, all_states, local)
+    return finish(col, sums, all_states, local)
 
 
 def solution(mesh):

time: 134 us -> 130 us (0.970)
  Pallas kernels: 25.7 us -> 20.7 us
  local copies, waits for them, and re-layouts: 0.86 us -> 4.77 us
  waiting for transfers between devices: 14.8 us -> 13.2 us
    unnamed x10, local copies, waits for them, and re-layouts: 0.86 us -> 4.77 us
    pallas_call x1 -> x0, Pallas kernels: 3.29 us -> none  [first(): pl.pallas_call(first_kernel, out_shape=tuple((jax.ShapeDtypeStruct(block,...]
    pallas_call x10 -> x11, Pallas kernels: 9.64 us -> 8.49 us  [local_kernel(): pl.pallas_call(kernel, out_shape=tuple((jax.ShapeDtypeStruct(shape, dtype...]
  transfers between devices with their start and end apart: 5 -> 5, of which waited for: 4 -> 3; matrix products, arithmetic and copies ran while one was open for 0% -> 0% of each run, Pallas kernels for 3% -> 3%
where the time goes in v5:
time: 130 us
  blocking collectives  67.9 us (52%)
  starting transfers between devices  21 us (16%)
  Pallas kernels  20.7 us (16%)
  waiting for transfers between devices  13.2 us (10%)
  local copies, waits for them, and re-layouts  4.77 us (4%)
  between operations  1.39 us (1%)
    all_to_all x1, blocking collectives, body(): parts = lax.all_to_all(tiles, ('y', 'core'), 0, 0)  16.9 us
    all_to_all x1, blocking collectives, body(): shares = lax.all_to_all(copies, ('y', 'col'), 0, 0)  16.3 us
    all_gather x3, blocking collectives, body(): both = lax.all_gather(on, 'core')  15.7 us
    all_to_all x1, blocking collectives, body(): parts = lax.all_to_all(copies, 'x', 0, 0)  13.7 us
    pallas_call x1, Pallas kernels, finish(): pl.pallas_call(finish_kernel, out_shape=(jax.ShapeDtypeStruct((local, row...  12.2 us
    all_to_all x1, waiting for transfers between devices, body(): all_states = lax.all_to_all(copies, 'col', 0, 0).reshape(cols * local, rows)  11.1 us
    ppermute x3, starting transfers between devices, body(): over = lax.ppermute(over, DOM, across_pairs(domains))  9.14 us
    pallas_call x11, Pallas kernels, local_kernel(): pl.pallas_call(kernel, out_shape=tuple((jax.ShapeDtypeStruct(shape, dtype...  8.49 us
  transfers between devices with their start and end apart: 5, of which 3 were waited for; matrix products, arithmetic and copies ran while one was open for 0% of the time, Pallas kernels for 3%

profile of v5, /device:TPU:1, one launch (start us, length us, event | category | flops | bytes accessed | tf_op | source)
XLA Modules:
  0.0 129.8 jit_solution(14964382413734497329)
XLA Ops:
  1.3 0.9 broadcast_select_fusion.low_ref.cur_ref.rest_0_
  2.1 0.0 copy-start
  2.2 1.6 %copy-done = bf16[1024,1024]{1,0:T(8,128)(2,1)S(1)} copy-done((bf16[1024,1024]{1,0:T(8,128)(2,1)S(1)}, bf16[1024,1024]{1,0:T(8,128)(2,1)}, u32[]{:S(2)}) %copy-start) | copy-done | bytes 2097176
  3.7 0.0 copy-start.1
  3.7 0.5 shard_map.59
  4.2 4.8 %collective-permute-start = (f32[32,1024]{1,0:T(8,128)S(1)}, f32[32,1024]{1,0:T(8,128)S(1)}, u32[]{:S(2)}, u32[]{:S(2)}) collective-permute-start(f32[32,1024]{1,0:T(8,128)S(1)} %get-tuple-element.24), channel_id=1, source_target_pairs={{8,16},{16,8},{24,32},{32,24},{40,48},{48,40},{56,64},{64,56},{72,... | collective-permute-start | bytes 393224 | tf_op jit(solution)/shard_map/ppermute | solution.py:277
  9.1 11.7 %all-gather = f32[64,1024]{1,0:T(8,128)S(1)} all-gather(f32[32,1024]{1,0:T(8,128)S(1)} %get-tuple-element.25), channel_id=2, replica_groups=mesh['x'=8,'y'=8,'core'=2,'col'=8] {'core'}, dimensions={0}, use_global_device_ids=true | all-gather | bytes 393216 | tf_op jit(solution)/shard_map/all_gather | solution.py:278
  20.8 0.0 copy-start.2
  20.8 1.6 %copy-done.2 = bf16[1024,1024]{1,0:T(8,128)(2,1)S(1)} copy-done((bf16[1024,1024]{1,0:T(8,128)(2,1)S(1)}, bf16[1024,1024]{1,0:T(8,128)(2,1)}, u32[]{:S(2)}) %copy-start.2) | copy-done | bytes 2097176
  22.4 1.1 shard_map.60.own_ref
  23.5 0.0 copy-start.3
  23.5 0.0 collective-permute-done.over_ref
  23.5 0.0 copy-done.1
  23.5 1.1 shard_map.61
  24.6 1.9 %collective-permute-start.1 = (f32[32,1024]{1,0:T(8,128)S(1)}, f32[32,1024]{1,0:T(8,128)S(1)}, u32[]{:S(2)}, u32[]{:S(2)}) collective-permute-start(f32[32,1024]{1,0:T(8,128)S(1)} %get-tuple-element.28), channel_id=1, source_target_pairs={{8,16},{16,8},{24,32},{32,24},{40,48},{48,40},{56,64},{64,56},{72,... | collective-permute-start | bytes 393224 | tf_op jit(solution)/shard_map/ppermute | solution.py:277
  26.6 2.0 %all-gather.1 = f32[64,1024]{1,0:T(8,128)S(1)} all-gather(f32[32,1024]{1,0:T(8,128)S(1)} %get-tuple-element.30), channel_id=3, replica_groups=mesh['x'=8,'y'=8,'core'=2,'col'=8] {'core'}, dimensions={0}, use_global_device_ids=true | all-gather | bytes 393216 | tf_op jit(solution)/shard_map/all_gather | solution.py:278
  28.6 0.0 copy-done.3
  28.6 1.1 shard_map.62.own_ref
  29.6 1.3 collective-permute-done.1.over_ref
  30.9 1.1 shard_map.63
  32.0 2.4 %collective-permute-start.2 = (f32[32,1024]{1,0:T(8,128)S(1)}, f32[32,1024]{1,0:T(8,128)S(1)}, u32[]{:S(2)}, u32[]{:S(2)}) collective-permute-start(f32[32,1024]{1,0:T(8,128)S(1)} %get-tuple-element.39), channel_id=1, source_target_pairs={{8,16},{16,8},{24,32},{32,24},{40,48},{48,40},{56,64},{64,56},{72,... | collective-permute-start | bytes 393224 | tf_op jit(solution)/shard_map/ppermute | solution.py:277
  34.4 2.0 %all-gather.2 = f32[64,1024]{1,0:T(8,128)S(1)} all-gather(f32[32,1024]{1,0:T(8,128)S(1)} %get-tuple-element.36), channel_id=4, replica_groups=mesh['x'=8,'y'=8,'core'=2,'col'=8] {'core'}, dimensions={0}, use_global_device_ids=true | all-gather | bytes 393216 | tf_op jit(solution)/shard_map/all_gather | solution.py:278
  36.4 1.1 shard_map.64.own_ref
  37.5 0.8 collective-permute-done.2.over_ref
  38.3 1.8 %shard_map.65 = (bf16[32,1024]{1,0:T(8,128)(2,1)S(1)}, bf16[8,32,1024]{2,1,0:T(8,128)(2,1)}, bf16[32,1024]{1,0:T(8,128)(2,1)S(1)}) custom-call(s32[1]{0:T(128)} %copy.6.counts_ref, s32[1]{0:T(128)} %bitcast.core_ref, f32[32,1024]{1,0:T(8,128)S(1)} %collective-permute-done.2.over_ref, f32[2,32,1024]{2,1,0:T(8,128)S(1)} %bitcast.14, ...), custom_call_target="tpu_custom_call" | custom-call | flops 65536 | bytes 65536 | tf_op jit(solution)/shard_map/pallas_call | solution.py:169
  40.1 7.0 %all-to-all-start = ((bf16[8,32,1024]{2,1,0:T(8,128)(2,1)}), bf16[8,32,1024]{2,1,0:T(8,128)(2,1)S(1)}, u32[]{:S(2)}, u32[]{:S(2)}) async-start(bf16[8,32,1024]{2,1,0:T(8,128)(2,1)} %get-tuple-element.45), calls=%async_computation | async-start | bytes 1048576 | tf_op jit(solution)/shard_map/all_to_all | solution.py:295
  47.1 4.8 %collective-permute-start.3 = (bf16[32,1024]{1,0:T(8,128)(2,1)S(1)}, bf16[32,1024]{1,0:T(8,128)(2,1)S(1)}, u32[]{:S(2)}, u32[]{:S(2)}) collective-permute-start(bf16[32,1024]{1,0:T(8,128)(2,1)S(1)} %get-tuple-element.44), channel_id=1, source_target_pairs={{0,8},{8,16},{16,24},{24,32},{32,40},{40,48},{48,56},{56,64},{64,7... | collective-permute-start | bytes 196616 | tf_op jit(solution)/shard_map/ppermute | solution.py:294
  52.0 0.0 copy-start.4
  52.0 1.6 %copy-done.4 = bf16[1024,1024]{1,0:T(8,128)(2,1)S(1)} copy-done((bf16[1024,1024]{1,0:T(8,128)(2,1)S(1)}, bf16[1024,1024]{1,0:T(8,128)(2,1)}, u32[]{:S(2)}) %copy-start.4) | copy-done | bytes 2097176
  53.5 0.5 shard_map.66.product_ref
  54.0 0.0 collective-permute-done.3.arrived_ref
  54.0 11.1 %all-to-all-done = bf16[8,32,1024]{2,1,0:T(8,128)(2,1)S(1)} async-done(((bf16[8,32,1024]{2,1,0:T(8,128)(2,1)}), bf16[8,32,1024]{2,1,0:T(8,128)(2,1)S(1)}, u32[]{:S(2)}, u32[]{:S(2)}) %all-to-all-start) | async-done | bytes 524320 | tf_op jit(solution)/shard_map/all_to_all | solution.py:295
  65.1 0.3 shard_map.67
  65.3 16.9 %all_to_all.20.parts_ref = f32[16,8,128]{2,1,0:T(8,128)S(1)} all-to-all(f32[16,8,128]{2,1,0:T(8,128)S(1)} %shard_map.67), channel_id=1, replica_groups=mesh['x'=8,'y'=8,'core'=2,'col'=8] {'y','core'}, dimensions={0} | all-to-all | bytes 131072 | tf_op jit(solution)/shard_map/all_to_all | solution.py:301
  82.3 13.7 %all_to_all.21.parts_ref = f32[8,8,128]{2,1,0:T(8,128)S(1)} all-to-all(f32[8,8,128]{2,1,0:T(8,128)S(1)} %shard_map.68), channel_id=1, replica_groups=mesh['x'=8,'y'=8,'core'=2,'col'=8] {'x'}, dimensions={0} | all-to-all | bytes 65536 | tf_op jit(solution)/shard_map/all_to_all | solution.py:303
  96.0 16.3 %all_to_all.22 = f32[64,8,128]{2,1,0:T(8,128)S(1)} all-to-all(f32[64,8,128]{2,1,0:T(8,128)S(1)} %shard_map.69), channel_id=1, replica_groups=mesh['x'=8,'y'=8,'core'=2,'col'=8] {'y','col'}, dimensions={0} | all-to-all | bytes 524288 | tf_op jit(solution)/shard_map/all_to_all | solution.py:305
  112.3 5.3 %all-gather.3 = f32[128,8,128]{2,1,0:T(8,128)S(1)} all-gather(f32[64,8,128]{2,1,0:T(8,128)S(1)} %all_to_all.22), channel_id=5, replica_groups=mesh['x'=8,'y'=8,'core'=2,'col'=8] {'core'}, dimensions={0}, use_global_device_ids=true | all-gather | bytes 786432 | tf_op jit(solution)/shard_map/all_gather | solution.py:306
  117.6 12.2 %shard_map.70 = (f32[32,1024]{1,0:T(8,128)}, f32[256,256]{1,0:T(8,128)}) custom-call(s32[1]{0:T(128)} %bitcast.3.col_ref, f32[2,8,8,8,128]{4,3,2,1,0:T(8,128)S(1)} %bitcast.11, bf16[256,1024]{1,0:T(8,128)(2,1)S(1)} %bitcast.10), custom_call_target="tpu_custom_call" | custom-call | flops 200000000 | bytes 2097152 | tf_op jit(solution)/shard_map/pallas_call | solution.py:147
  (3 shorter events, 0.1 us)
Async XLA Ops:
  2.1 1.6 %copy-start = (bf16[1024,1024]{1,0:T(8,128)(2,1)S(1)}, bf16[1024,1024]{1,0:T(8,128)(2,1)}, u32[]{:S(2)}) copy-start(bf16[1024,1024]{1,0:T(8,128)(2,1)} %coupling_ref.7) | copy-start | bytes 6291460
  3.7 19.8 %copy-start.1 = (bf16[1024,1024]{1,0:T(8,128)(2,1)S(1)}, bf16[1024,1024]{1,0:T(8,128)(2,1)}, u32[]{:S(2)}) copy-start(bf16[1024,1024]{1,0:T(8,128)(2,1)} %coupling_ref.7) | copy-start | bytes 6291460
  4.2 19.3 %collective-permute-start = (f32[32,1024]{1,0:T(8,128)S(1)}, f32[32,1024]{1,0:T(8,128)S(1)}, u32[]{:S(2)}, u32[]{:S(2)}) collective-permute-start(f32[32,1024]{1,0:T(8,128)S(1)} %get-tuple-element.24), channel_id=1, source_target_pairs={{8,16},{16,8},{24,32},{32,24},{40,48},{48,40},{56,64},{64,56},{72,... | collective-permute-start | bytes 393224 | tf_op jit(solution)/shard_map/ppermute | solution.py:277
  20.8 1.6 %copy-start.2 = (bf16[1024,1024]{1,0:T(8,128)(2,1)S(1)}, bf16[1024,1024]{1,0:T(8,128)(2,1)}, u32[]{:S(2)}) copy-start(bf16[1024,1024]{1,0:T(8,128)(2,1)} %diag_ref.7) | copy-start | bytes 6291460
  23.5 5.1 %copy-start.3 = (bf16[1024,1024]{1,0:T(8,128)(2,1)S(1)}, bf16[1024,1024]{1,0:T(8,128)(2,1)}, u32[]{:S(2)}) copy-start(bf16[1024,1024]{1,0:T(8,128)(2,1)} %diag_ref.7) | copy-start | bytes 6291460
  24.6 6.3 %collective-permute-start.1 = (f32[32,1024]{1,0:T(8,128)S(1)}, f32[32,1024]{1,0:T(8,128)S(1)}, u32[]{:S(2)}, u32[]{:S(2)}) collective-permute-start(f32[32,1024]{1,0:T(8,128)S(1)} %get-tuple-element.28), channel_id=1, source_target_pairs={{8,16},{16,8},{24,32},{32,24},{40,48},{48,40},{56,64},{64,56},{72,... | collective-permute-start | bytes 393224 | tf_op jit(solution)/shard_map/ppermute | solution.py:277
  32.0 6.3 %collective-permute-start.2 = (f32[32,1024]{1,0:T(8,128)S(1)}, f32[32,1024]{1,0:T(8,128)S(1)}, u32[]{:S(2)}, u32[]{:S(2)}) collective-permute-start(f32[32,1024]{1,0:T(8,128)S(1)} %get-tuple-element.39), channel_id=1, source_target_pairs={{8,16},{16,8},{24,32},{32,24},{40,48},{48,40},{56,64},{64,56},{72,... | collective-permute-start | bytes 393224 | tf_op jit(solution)/shard_map/ppermute | solution.py:277
  40.1 24.9 %all-to-all-start = ((bf16[8,32,1024]{2,1,0:T(8,128)(2,1)}), bf16[8,32,1024]{2,1,0:T(8,128)(2,1)S(1)}, u32[]{:S(2)}, u32[]{:S(2)}) async-start(bf16[8,32,1024]{2,1,0:T(8,128)(2,1)} %get-tuple-element.45), calls=%async_computation | async-start | bytes 1048576 | tf_op jit(solution)/shard_map/all_to_all | solution.py:295
  47.1 6.9 %collective-permute-start.3 = (bf16[32,1024]{1,0:T(8,128)(2,1)S(1)}, bf16[32,1024]{1,0:T(8,128)(2,1)S(1)}, u32[]{:S(2)}, u32[]{:S(2)}) collective-permute-start(bf16[32,1024]{1,0:T(8,128)(2,1)S(1)} %get-tuple-element.44), channel_id=1, source_target_pairs={{0,8},{8,16},{16,24},{24,32},{32,40},{40,48},{48,56},{56,64},{64,7... | collective-permute-start | bytes 196616 | tf_op jit(solution)/shard_map/ppermute | solution.py:294
  52.0 1.6 %copy-start.4 = (bf16[1024,1024]{1,0:T(8,128)(2,1)S(1)}, bf16[1024,1024]{1,0:T(8,128)(2,1)}, u32[]{:S(2)}) copy-start(bf16[1024,1024]{1,0:T(8,128)(2,1)} %diag_ref.7) | copy-start | bytes 6291460

commit v6 on v5

--- a/solution.py
+++ b/solution.py
@@ -20,6 +20,7 @@
 WIDE = 64
 EVALUATIONS = 3
 CLOSE = 1.6e-5
+CHUNKS = 4
 F32 = jnp.float32
 BF16 = jnp.bfloat16
 
@@ -185,10 +186,79 @@
     on_ref[...] = jnp.where(even, onward, block)
 
 
-def first_kernel(core_ref, low_ref, coupling_ref, over_ref, on_ref):
-    low = low_ref[...]
-    onward = jnp.dot(low, coupling_ref[...], preferred_element_type=F32)
-    send_off(core_ref[0] == 0, low.astype(F32), onward, over_ref, on_ref)
+def chunked(whole_hbm, whole_ref, array_hbm, array_ref, sems):
+    depth = array_ref.shape[0] // CHUNKS
+    chunks = [pl.ds(k * depth, depth) for k in range(CHUNKS)]
+    whole = pltpu.make_async_copy(whole_hbm, whole_ref, sems.at[CHUNKS])
+    whole.start()
+    copies = [
+        pltpu.make_async_copy(array_hbm.at[rows], array_ref.at[rows], sems.at[k])
+        for k, rows in enumerate(chunks)
+    ]
+    for copy in copies:
+        copy.start()
+    whole.wait()
+    return [(copy, slice(k * depth, (k + 1) * depth)) for k, copy in enumerate(copies)]
+
+
+def first_kernel(
+    counts_ref, core_ref, states_hbm, coupling_hbm, low_ref, over_ref, on_ref,
+    states_ref, coupling_ref, sems,
+):
+    copies = chunked(states_hbm, states_ref, coupling_hbm, coupling_ref, sems)
+    live = live_row(counts_ref, states_ref.shape)
+    block = jnp.where(live, states_ref[...].astype(F32), 0.0)
+    low = block.astype(BF16)
+    low_ref[...] = low
+    onward = jnp.zeros_like(block)
+    for copy, rows in copies:
+        copy.wait()
+        onward = onward + jnp.dot(
+            low[:, rows], coupling_ref[rows, :], preferred_element_type=F32
+        )
+    send_off(core_ref[0] == 0, block, onward, over_ref, on_ref)
+
+
+def first_own_kernel(low_any, diag_ref, own_ref, low_ref, sem):
+    copy = pltpu.make_async_copy(low_any, low_ref, sem)
+    copy.start()
+    copy.wait()
+    own_kernel(low_ref, diag_ref, own_ref)
+
+
+def first_step(counts, core, states, coupling):
+    block = states.shape
+    vmem = pl.BlockSpec(memory_space=pltpu.VMEM)
+    smem = pl.BlockSpec(memory_space=pltpu.SMEM)
+    left = pl.BlockSpec(memory_space=pltpu.HBM)
+    return pl.pallas_call(
+        first_kernel,
+        out_shape=tuple(jax.ShapeDtypeStruct(block, dtype) for dtype in (BF16, F32, F32)),
+        in_specs=[smem, smem, left, left],
+        out_specs=(vmem,) * 3,
+        scratch_shapes=[
+            pltpu.VMEM(block, BF16),
+            pltpu.VMEM(coupling.shape, BF16),
+            pltpu.SemaphoreType.DMA((CHUNKS + 1,)),
+        ],
+        compiler_params=pltpu.CompilerParams(vmem_limit_bytes=62 * 2**20),
+        cost_estimate=pl.CostEstimate(flops=2**16, bytes_accessed=2**16, transcendentals=0),
+    )(counts, core, states, coupling)
+
+
+def first_own(low, diag_blocks):
+    return pl.pallas_call(
+        first_own_kernel,
+        out_shape=jax.ShapeDtypeStruct(low.shape, F32),
+        in_specs=[
+            pl.BlockSpec(memory_space=pl.ANY),
+            pl.BlockSpec(memory_space=pltpu.VMEM),
+        ],
+        out_specs=pl.BlockSpec(memory_space=pltpu.VMEM),
+        scratch_shapes=[pltpu.VMEM(low.shape, BF16), pltpu.SemaphoreType.DMA],
+        compiler_params=pltpu.CompilerParams(vmem_limit_bytes=12 * 2**20),
+        cost_estimate=pl.CostEstimate(flops=2**16, bytes_accessed=2**16, transcendentals=0),
+    )(low, diag_blocks)
 
 
 def own_kernel(low_ref, diag_ref, own_ref):
@@ -228,7 +298,7 @@
 
 def last_kernel(
     counts_ref, core_ref, over_ref, both_ref, own_ref, coupling_ref, cur_ref, prev_ref,
-    filtered_ref, copies_ref, onward_ref,
+    filtered_ref, copies_ref,
 ):
     even = core_ref[0] == 0
     block = recur(counts_ref, even, over_ref, both_ref, own_ref, cur_ref, prev_ref, coupling_ref)
@@ -236,11 +306,11 @@
     filtered_ref[...] = low
     for z in range(copies_ref.shape[0]):
         copies_ref[z] = low
-    onward_ref[...] = jnp.dot(low, coupling_ref[...], preferred_element_type=F32).astype(BF16)
-
-
-def diag_kernel(filtered_ref, diag_ref, out_ref):
-    out_ref[...] = jnp.dot(filtered_ref[...], diag_ref[...], preferred_element_type=F32)
+
+
+def product_kernel(left_ref, right_ref, out_ref):
+    out = jnp.dot(left_ref[...], right_ref[...], preferred_element_type=F32)
+    out_ref[...] = out.astype(out_ref.dtype)
 
 
 def terms_kernel(filtered_ref, product_ref, arrived_ref, all_ref, tiles_ref):
@@ -269,31 +339,30 @@
     col = lax.axis_index("col").astype(jnp.int32).reshape(1)
     trade = [(block, F32), (block, F32)]
 
-    live = lax.iota(jnp.int32, rows) < counts[0]
-    low = jnp.where(live[None, :], states, jnp.zeros_like(states))
-    over, on = local_kernel(first_kernel, trade, core, low, coupling, scalars=1)
+    low, over, on = first_step(counts, core, states, coupling)
     history = [low]
     for step in range(DEGREE):
         over = lax.ppermute(over, DOM, across_pairs(domains))
         both = lax.all_gather(on, "core")
         low, both, col = lax.optimization_barrier((low, both, col))
-        (own,) = local_kernel(own_kernel, [(block, F32)], low, diag_blocks)
+        if step == 0:
+            own = first_own(low, diag_blocks)
+        else:
+            (own,) = local_kernel(own_kernel, [(block, F32)], low, diag_blocks)
         args = (counts, core, over, both, own, coupling, *history[:-3:-1])
         if step < DEGREE - 1:
             cur, low, over, on = local_kernel(
                 step_kernel, [(block, F32), (block, BF16)] + trade, *args, scalars=2
             )
             history.append(cur)
-    filtered, copies, onward = local_kernel(
-        last_kernel,
-        [(block, BF16), ((cols,) + block, BF16), (block, BF16)],
-        *args,
-        scalars=2,
-    )
-
+    filtered, copies = local_kernel(
+        last_kernel, [(block, BF16), ((cols,) + block, BF16)], *args, scalars=2
+    )
+
+    (onward,) = local_kernel(product_kernel, [(block, BF16)], filtered, coupling)
     arrived = lax.ppermute(onward, DOM, [(i, i + 1) for i in range(domains - 1)])
     all_states = lax.all_to_all(copies, "col", 0, 0).reshape(cols * local, rows)
-    (product,) = local_kernel(diag_kernel, [(block, F32)], filtered, diag_blocks)
+    (product,) = local_kernel(product_kernel, [(block, F32)], filtered, diag_blocks)
     peers = ALONG_Y * CORES
     (tiles,) = local_kernel(
         terms_kernel, [((peers, 8, 128), F32)], filtered, product, arrived, all_states

time: 130 us -> 131 us (level)
  local copies, waits for them, and re-layouts: 4.77 us -> 2.45 us
  Pallas kernels: 20.7 us -> 23 us
    pallas_call x0 -> x2, Pallas kernels: none -> 3.65 us  [the longest x1 2.5 us: first_step(): pl.pallas_call(first_kernel, out_shape=tuple((jax.ShapeDtypeStruct(block,...]
    unnamed x10 -> x12, local copies, waits for them, and re-layouts: 4.77 us -> 2.45 us
    pallas_call x11 -> x10, Pallas kernels: 8.49 us -> 7.17 us  [local_kernel(): pl.pallas_call(kernel, out_shape=tuple((jax.ShapeDtypeStruct(shape, dtype...]
  transfers between devices with their start and end apart: 5 -> 5, of which waited for: 3 -> 4; matrix products, arithmetic and copies ran while one was open for 0% -> 0% of each run, Pallas kernels for 3% -> 3%
where the time goes in v6:
time: 131 us; the launch traced here: 130 us
  blocking collectives  67.8 us (52%)
  Pallas kernels  23 us (18%)
  starting transfers between devices  21.1 us (16%)
  waiting for transfers between devices  14.1 us (11%)
  local copies, waits for them, and re-layouts  2.45 us (2%)
  between operations  1.41 us (1%)
    all_to_all x1, blocking collectives, body(): parts = lax.all_to_all(tiles, ('y', 'core'), 0, 0)  16.6 us
    all_to_all x1, blocking collectives, body(): shares = lax.all_to_all(copies, ('y', 'col'), 0, 0)  16.3 us
    all_gather x3, blocking collectives, body(): both = lax.all_gather(on, 'core')  15.9 us
    all_to_all x1, blocking collectives, body(): parts = lax.all_to_all(copies, 'x', 0, 0)  13.6 us
    pallas_call x1, Pallas kernels, finish(): pl.pallas_call(finish_kernel, out_shape=(jax.ShapeDtypeStruct((local, row...  12.2 us
    all_to_all x1, waiting for transfers between devices, body(): all_states = lax.all_to_all(copies, 'col', 0, 0).reshape(cols * local, rows)  11.2 us
    ppermute x3, starting transfers between devices, body(): over = lax.ppermute(over, DOM, across_pairs(domains))  9.14 us
    pallas_call x10, Pallas kernels, local_kernel(): pl.pallas_call(kernel, out_shape=tuple((jax.ShapeDtypeStruct(shape, dtype...  7.17 us
  transfers between devices with their start and end apart: 5, of which 4 were waited for; matrix products, arithmetic and copies ran while one was open for 0% of the time, Pallas kernels for 3%

profile of v6, /device:TPU:1, one launch (start us, length us, event | category | flops | bytes accessed | tf_op | source)
XLA Modules:
  0.0 130.0 jit_solution(4407334843924176058)
XLA Ops:
  1.3 2.5 %shard_map.59 = (bf16[32,1024]{1,0:T(8,128)(2,1)}, f32[32,1024]{1,0:T(8,128)}, f32[32,1024]{1,0:T(8,128)}) custom-call(s32[1]{0:T(128)S(6)} %copy.6.counts_ref, s32[1]{0:T(128)} %bitcast.core_ref, bf16[32,1024]{1,0:T(8,128)(2,1)} %states_hbm.1, bf16[1024,1024]{1,0:T(8,128)(2,1)} %right_ref.3), custom_call_target="tpu_custom_call" | custom-call | flops 65536 | bytes 65536 | tf_op jit(solution)/shard_map/pallas_call | solution.py:234
  3.8 0.0 copy-start
  3.8 4.8 %collective-permute-start = (f32[32,1024]{1,0:T(8,128)}, f32[32,1024]{1,0:T(8,128)S(1)}, u32[]{:S(2)}, u32[]{:S(2)}) collective-permute-start(f32[32,1024]{1,0:T(8,128)} %get-tuple-element.24), channel_id=1, source_target_pairs={{8,16},{16,8},{24,32},{32,24},{40,48},{48,40},{56,64},{64,56},{72,... | collective-permute-start | bytes 393224 | tf_op jit(solution)/shard_map/ppermute | solution.py:345
  8.6 12.0 %all-gather = f32[64,1024]{1,0:T(8,128)S(1)} all-gather(f32[32,1024]{1,0:T(8,128)} %get-tuple-element.26), channel_id=2, replica_groups=mesh['x'=8,'y'=8,'core'=2,'col'=8] {'core'}, dimensions={0}, use_global_device_ids=true | all-gather | bytes 393216 | tf_op jit(solution)/shard_map/all_gather | solution.py:346
  20.6 0.0 copy-start.1
  20.6 1.6 %copy-done.1 = bf16[1024,1024]{1,0:T(8,128)(2,1)S(1)} copy-done((bf16[1024,1024]{1,0:T(8,128)(2,1)S(1)}, bf16[1024,1024]{1,0:T(8,128)(2,1)}, u32[]{:S(2)}) %copy-start.1) | copy-done | bytes 2097176
  22.2 0.0 copy-start.4
  22.2 0.8 copy-done.4
  23.0 0.0 copy-start.5
  23.0 1.2 shard_map.60.own_ref
  24.2 0.0 copy-start.2
  24.2 0.0 collective-permute-done.over_ref
  24.2 0.0 copy-done
  24.2 0.0 copy-done.5
  24.2 1.1 shard_map.61
  25.4 1.9 %collective-permute-start.1 = (f32[32,1024]{1,0:T(8,128)S(1)}, f32[32,1024]{1,0:T(8,128)S(1)}, u32[]{:S(2)}, u32[]{:S(2)}) collective-permute-start(f32[32,1024]{1,0:T(8,128)S(1)} %get-tuple-element.29), channel_id=1, source_target_pairs={{8,16},{16,8},{24,32},{32,24},{40,48},{48,40},{56,64},{64,56},{72,... | collective-permute-start | bytes 393224 | tf_op jit(solution)/shard_map/ppermute | solution.py:345
  27.3 2.0 %all-gather.1 = f32[64,1024]{1,0:T(8,128)S(1)} all-gather(f32[32,1024]{1,0:T(8,128)S(1)} %get-tuple-element.31), channel_id=3, replica_groups=mesh['x'=8,'y'=8,'core'=2,'col'=8] {'core'}, dimensions={0}, use_global_device_ids=true | all-gather | bytes 393216 | tf_op jit(solution)/shard_map/all_gather | solution.py:346
  29.3 0.0 copy-done.2
  29.3 1.1 shard_map.62.own_ref
  30.4 1.3 collective-permute-done.1.over_ref
  31.6 1.1 shard_map.63
  32.8 2.4 %collective-permute-start.2 = (f32[32,1024]{1,0:T(8,128)S(1)}, f32[32,1024]{1,0:T(8,128)S(1)}, u32[]{:S(2)}, u32[]{:S(2)}) collective-permute-start(f32[32,1024]{1,0:T(8,128)S(1)} %get-tuple-element.40), channel_id=1, source_target_pairs={{8,16},{16,8},{24,32},{32,24},{40,48},{48,40},{56,64},{64,56},{72,... | collective-permute-start | bytes 393224 | tf_op jit(solution)/shard_map/ppermute | solution.py:345
  35.1 2.0 %all-gather.2 = f32[64,1024]{1,0:T(8,128)S(1)} all-gather(f32[32,1024]{1,0:T(8,128)S(1)} %get-tuple-element.37), channel_id=4, replica_groups=mesh['x'=8,'y'=8,'core'=2,'col'=8] {'core'}, dimensions={0}, use_global_device_ids=true | all-gather | bytes 393216 | tf_op jit(solution)/shard_map/all_gather | solution.py:346
  37.1 1.1 shard_map.64.own_ref
  38.2 0.8 collective-permute-done.2.over_ref
  39.0 1.6 %shard_map.65 = (bf16[32,1024]{1,0:T(8,128)(2,1)S(1)}, bf16[8,32,1024]{2,1,0:T(8,128)(2,1)}) custom-call(s32[1]{0:T(128)S(6)} %copy.6.counts_ref, s32[1]{0:T(128)} %bitcast.core_ref, f32[32,1024]{1,0:T(8,128)S(1)} %collective-permute-done.2.over_ref, f32[2,32,1024]{2,1,0:T(8,128)S(1)} %bitcast.12, f32[32,1024]{1,0:T(8,128)S(1)} %shard_map.64.own_ref, ...), custom_call_target="tpu_custom_call" | custom-call | flops 65536 | bytes 65536 | tf_op jit(solution)/shard_map/pallas_call | solution.py:170
  40.6 7.0 %all-to-all-start = ((bf16[8,32,1024]{2,1,0:T(8,128)(2,1)}), bf16[8,32,1024]{2,1,0:T(8,128)(2,1)S(1)}, u32[]{:S(2)}, u32[]{:S(2)}) async-start(bf16[8,32,1024]{2,1,0:T(8,128)(2,1)} %get-tuple-element.45), calls=%async_computation | async-start | bytes 1048576 | tf_op jit(solution)/shard_map/all_to_all | solution.py:364
  47.6 0.0 copy-start.3
  47.6 0.5 shard_map.67
  48.0 5.0 %collective-permute-start.3 = (bf16[32,1024]{1,0:T(8,128)(2,1)S(1)}, bf16[32,1024]{1,0:T(8,128)(2,1)S(1)}, u32[]{:S(2)}, u32[]{:S(2)}) collective-permute-start(bf16[32,1024]{1,0:T(8,128)(2,1)S(1)} %shard_map.67), channel_id=1, source_target_pairs={{0,8},{8,16},{16,24},{24,32},{32,40},{40,48},{48,56},{56,64},{64,7... | collective-permute-start | bytes 196616 | tf_op jit(solution)/shard_map/ppermute | solution.py:363
  53.1 0.0 copy-done.3
  53.1 0.5 shard_map.66.product_ref
  53.5 0.8 collective-permute-done.3.arrived_ref
  54.4 11.2 %all-to-all-done = bf16[8,32,1024]{2,1,0:T(8,128)(2,1)S(1)} async-done(((bf16[8,32,1024]{2,1,0:T(8,128)(2,1)}), bf16[8,32,1024]{2,1,0:T(8,128)(2,1)S(1)}, u32[]{:S(2)}, u32[]{:S(2)}) %all-to-all-start) | async-done | bytes 524320 | tf_op jit(solution)/shard_map/all_to_all | solution.py:364
  65.6 0.3 shard_map.68
  65.8 16.6 %all_to_all.20.parts_ref = f32[16,8,128]{2,1,0:T(8,128)S(1)} all-to-all(f32[16,8,128]{2,1,0:T(8,128)S(1)} %shard_map.68), channel_id=1, replica_groups=mesh['x'=8,'y'=8,'core'=2,'col'=8] {'y','core'}, dimensions={0} | all-to-all | bytes 131072 | tf_op jit(solution)/shard_map/all_to_all | solution.py:370
  82.5 13.6 %all_to_all.21.parts_ref = f32[8,8,128]{2,1,0:T(8,128)S(1)} all-to-all(f32[8,8,128]{2,1,0:T(8,128)S(1)} %shard_map.69), channel_id=1, replica_groups=mesh['x'=8,'y'=8,'core'=2,'col'=8] {'x'}, dimensions={0} | all-to-all | bytes 65536 | tf_op jit(solution)/shard_map/all_to_all | solution.py:372
  96.2 16.3 %all_to_all.22 = f32[64,8,128]{2,1,0:T(8,128)S(1)} all-to-all(f32[64,8,128]{2,1,0:T(8,128)S(1)} %shard_map.70), channel_id=1, replica_groups=mesh['x'=8,'y'=8,'core'=2,'col'=8] {'y','col'}, dimensions={0} | all-to-all | bytes 524288 | tf_op jit(solution)/shard_map/all_to_all | solution.py:374
  112.5 5.3 %all-gather.3 = f32[128,8,128]{2,1,0:T(8,128)S(1)} all-gather(f32[64,8,128]{2,1,0:T(8,128)S(1)} %all_to_all.22), channel_id=5, replica_groups=mesh['x'=8,'y'=8,'core'=2,'col'=8] {'core'}, dimensions={0}, use_global_device_ids=true | all-gather | bytes 786432 | tf_op jit(solution)/shard_map/all_gather | solution.py:375
  117.8 12.2 %shard_map.71 = (f32[32,1024]{1,0:T(8,128)}, f32[256,256]{1,0:T(8,128)}) custom-call(s32[1]{0:T(128)} %bitcast.2.col_ref, f32[2,8,8,8,128]{4,3,2,1,0:T(8,128)S(1)} %bitcast.9, bf16[256,1024]{1,0:T(8,128)(2,1)S(1)} %bitcast.8), custom_call_target="tpu_custom_call" | custom-call | flops 200000000 | bytes 2097152 | tf_op jit(solution)/shard_map/pallas_call | solution.py:148
  (2 shorter events, 0.0 us)
Async XLA Ops:
  3.8 20.4 %copy-start = (bf16[1024,1024]{1,0:T(8,128)(2,1)S(1)}, bf16[1024,1024]{1,0:T(8,128)(2,1)}, u32[]{:S(2)}) copy-start(bf16[1024,1024]{1,0:T(8,128)(2,1)} %right_ref.3) | copy-start | bytes 6291460
  3.8 20.4 %collective-permute-start = (f32[32,1024]{1,0:T(8,128)}, f32[32,1024]{1,0:T(8,128)S(1)}, u32[]{:S(2)}, u32[]{:S(2)}) collective-permute-start(f32[32,1024]{1,0:T(8,128)} %get-tuple-element.24), channel_id=1, source_target_pairs={{8,16},{16,8},{24,32},{32,24},{40,48},{48,40},{56,64},{64,56},{72,... | collective-permute-start | bytes 393224 | tf_op jit(solution)/shard_map/ppermute | solution.py:345
  20.6 1.6 %copy-start.1 = (bf16[1024,1024]{1,0:T(8,128)(2,1)S(1)}, bf16[1024,1024]{1,0:T(8,128)(2,1)}, u32[]{:S(2)}) copy-start(bf16[1024,1024]{1,0:T(8,128)(2,1)} %right_ref.2) | copy-start | bytes 6291460
  22.2 0.8 copy-start.4
  23.0 1.2 copy-start.5
  24.2 5.1 %copy-start.2 = (bf16[1024,1024]{1,0:T(8,128)(2,1)S(1)}, bf16[1024,1024]{1,0:T(8,128)(2,1)}, u32[]{:S(2)}) copy-start(bf16[1024,1024]{1,0:T(8,128)(2,1)} %right_ref.2) | copy-start | bytes 6291460
  25.4 6.3 %collective-permute-start.1 = (f32[32,1024]{1,0:T(8,128)S(1)}, f32[32,1024]{1,0:T(8,128)S(1)}, u32[]{:S(2)}, u32[]{:S(2)}) collective-permute-start(f32[32,1024]{1,0:T(8,128)S(1)} %get-tuple-element.29), channel_id=1, source_target_pairs={{8,16},{16,8},{24,32},{32,24},{40,48},{48,40},{56,64},{64,56},{72,... | collective-permute-start | bytes 393224 | tf_op jit(solution)/shard_map/ppermute | solution.py:345
  32.8 6.3 %collective-permute-start.2 = (f32[32,1024]{1,0:T(8,128)S(1)}, f32[32,1024]{1,0:T(8,128)S(1)}, u32[]{:S(2)}, u32[]{:S(2)}) collective-permute-start(f32[32,1024]{1,0:T(8,128)S(1)} %get-tuple-element.40), channel_id=1, source_target_pairs={{8,16},{16,8},{24,32},{32,24},{40,48},{48,40},{56,64},{64,56},{72,... | collective-permute-start | bytes 393224 | tf_op jit(solution)/shard_map/ppermute | solution.py:345
  40.6 24.9 %all-to-all-start = ((bf16[8,32,1024]{2,1,0:T(8,128)(2,1)}), bf16[8,32,1024]{2,1,0:T(8,128)(2,1)S(1)}, u32[]{:S(2)}, u32[]{:S(2)}) async-start(bf16[8,32,1024]{2,1,0:T(8,128)(2,1)} %get-tuple-element.45), calls=%async_computation | async-start | bytes 1048576 | tf_op jit(solution)/shard_map/all_to_all | solution.py:364
  47.6 5.5 %copy-start.3 = (bf16[1024,1024]{1,0:T(8,128)(2,1)S(1)}, bf16[1024,1024]{1,0:T(8,128)(2,1)}, u32[]{:S(2)}) copy-start(bf16[1024,1024]{1,0:T(8,128)(2,1)} %right_ref.2) | copy-start | bytes 6291460
  48.0 6.3 %collective-permute-start.3 = (bf16[32,1024]{1,0:T(8,128)(2,1)S(1)}, bf16[32,1024]{1,0:T(8,128)(2,1)S(1)}, u32[]{:S(2)}, u32[]{:S(2)}) collective-permute-start(bf16[32,1024]{1,0:T(8,128)(2,1)S(1)} %shard_map.67), channel_id=1, source_target_pairs={{0,8},{8,16},{16,24},{24,32},{32,40},{40,48},{48,56},{56,64},{64,7... | collective-permute-start | bytes 196616 | tf_op jit(solution)/shard_map/ppermute | solution.py:363

commit v7 on v5

--- a/solution.py
+++ b/solution.py
@@ -176,21 +176,6 @@
     )(*operands)
 
 
-def live_row(counts_ref, shape):
-    return lax.broadcasted_iota(jnp.int32, (1, shape[1]), 1) < counts_ref[0]
-
-
-def send_off(even, block, onward, over_ref, on_ref):
-    over_ref[...] = jnp.where(even, block, onward)
-    on_ref[...] = jnp.where(even, onward, block)
-
-
-def first_kernel(core_ref, low_ref, coupling_ref, over_ref, on_ref):
-    low = low_ref[...]
-    onward = jnp.dot(low, coupling_ref[...], preferred_element_type=F32)
-    send_off(core_ref[0] == 0, low.astype(F32), onward, over_ref, on_ref)
-
-
 def own_kernel(low_ref, diag_ref, own_ref):
     low, diag = low_ref[...], diag_ref[...]
     own = jnp.dot(low, diag, preferred_element_type=F32)
@@ -198,49 +183,32 @@
     own_ref[...] = 0.5 * (own + own_t)
 
 
-def recur(counts_ref, even, over_ref, both_ref, own_ref, cur_ref, prev_ref, coupling_ref):
-    over = over_ref[...]
-    beside = jnp.where(even, both_ref[1], both_ref[0])
-    from_prev = jnp.where(even, over, beside)
-    next_block = jnp.where(even, beside, over).astype(BF16)
-    from_next = lax.dot_general(
-        next_block, coupling_ref[...], TRANSPOSED, preferred_element_type=F32
-    )
-    live = live_row(counts_ref, over.shape)
-    image = jnp.where(live, own_ref[...] + from_prev + from_next, 0.0)
-    shifted = (image - CENTER * cur_ref[...].astype(F32)) / HALF
-    if prev_ref is None:
-        return shifted
-    return 2.0 * shifted - prev_ref[...].astype(F32)
-
-
-def step_kernel(counts_ref, core_ref, over_ref, both_ref, own_ref, coupling_ref, cur_ref, *rest):
-    prev_ref = rest[0] if len(rest) == 5 else None
-    next_ref, low_ref, over_out, on_out = rest[-4:]
-    even = core_ref[0] == 0
-    block = recur(counts_ref, even, over_ref, both_ref, own_ref, cur_ref, prev_ref, coupling_ref)
-    low = block.astype(BF16)
-    next_ref[...] = block
-    low_ref[...] = low
-    onward = jnp.dot(low, coupling_ref[...], preferred_element_type=F32)
-    send_off(even, block, onward, over_out, on_out)
-
-
-def last_kernel(
-    counts_ref, core_ref, over_ref, both_ref, own_ref, coupling_ref, cur_ref, prev_ref,
-    filtered_ref, copies_ref, onward_ref,
-):
-    even = core_ref[0] == 0
-    block = recur(counts_ref, even, over_ref, both_ref, own_ref, cur_ref, prev_ref, coupling_ref)
-    low = block.astype(BF16)
-    filtered_ref[...] = low
-    for z in range(copies_ref.shape[0]):
-        copies_ref[z] = low
-    onward_ref[...] = jnp.dot(low, coupling_ref[...], preferred_element_type=F32).astype(BF16)
-
-
-def diag_kernel(filtered_ref, diag_ref, out_ref):
-    out_ref[...] = jnp.dot(filtered_ref[...], diag_ref[...], preferred_element_type=F32)
+def copies_kernel(array_ref, copies_hbm, sems):
+    copies = [
+        pltpu.make_async_copy(array_ref, copies_hbm.at[i], sems.at[i])
+        for i in range(copies_hbm.shape[0])
+    ]
+    for copy in copies:
+        copy.start()
+    for copy in copies:
+        copy.wait()
+
+
+def copied(array, count):
+    return pl.pallas_call(
+        copies_kernel,
+        out_shape=jax.ShapeDtypeStruct((count,) + array.shape, array.dtype),
+        in_specs=[pl.BlockSpec(memory_space=pltpu.VMEM)],
+        out_specs=pl.BlockSpec(memory_space=pltpu.HBM),
+        scratch_shapes=[pltpu.SemaphoreType.DMA((count,))],
+        compiler_params=pltpu.CompilerParams(vmem_limit_bytes=12 * 2**20),
+        cost_estimate=pl.CostEstimate(flops=0, bytes_accessed=2**16, transcendentals=0),
+    )(array)
+
+
+def product_kernel(left_ref, right_ref, out_ref):
+    out = jnp.dot(left_ref[...], right_ref[...], preferred_element_type=F32)
+    out_ref[...] = out.astype(out_ref.dtype)
 
 
 def terms_kernel(filtered_ref, product_ref, arrived_ref, all_ref, tiles_ref):
@@ -267,33 +235,37 @@
     domains, cols = lax.axis_size(DOM), lax.axis_size("col")
     core = lax.axis_index("core").astype(jnp.int32).reshape(1)
     col = lax.axis_index("col").astype(jnp.int32).reshape(1)
-    trade = [(block, F32), (block, F32)]
-
-    live = lax.iota(jnp.int32, rows) < counts[0]
-    low = jnp.where(live[None, :], states, jnp.zeros_like(states))
-    over, on = local_kernel(first_kernel, trade, core, low, coupling, scalars=1)
-    history = [low]
+
+    live = (lax.iota(jnp.int32, rows) < counts[0])[None, :]
+    low = lax.optimization_barrier(jnp.where(live, states, jnp.zeros_like(states)))
+    even = core[0] == 0
+    history = [low.astype(F32)]
     for step in range(DEGREE):
+        onward = jnp.dot(low, coupling, preferred_element_type=F32)
+        over = jnp.where(even, history[-1], onward)
+        on = jnp.where(even, onward, history[-1])
         over = lax.ppermute(over, DOM, across_pairs(domains))
         both = lax.all_gather(on, "core")
         low, both, col = lax.optimization_barrier((low, both, col))
         (own,) = local_kernel(own_kernel, [(block, F32)], low, diag_blocks)
-        args = (counts, core, over, both, own, coupling, *history[:-3:-1])
-        if step < DEGREE - 1:
-            cur, low, over, on = local_kernel(
-                step_kernel, [(block, F32), (block, BF16)] + trade, *args, scalars=2
-            )
-            history.append(cur)
-    filtered, copies, onward = local_kernel(
-        last_kernel,
-        [(block, BF16), ((cols,) + block, BF16), (block, BF16)],
-        *args,
-        scalars=2,
-    )
-
+        beside = jnp.where(even, both[1], both[0])
+        next_block = jnp.where(even, beside, over).astype(BF16)
+        from_next = lax.dot_general(
+            next_block, coupling, TRANSPOSED, preferred_element_type=F32
+        )
+        image = jnp.where(live, own + jnp.where(even, over, beside) + from_next, 0.0)
+        cur = (image - CENTER * history[-1]) / HALF
+        if step > 0:
+            cur = 2.0 * cur - history[-2]
+        history.append(cur)
+        low = cur.astype(BF16)
+    filtered = lax.optimization_barrier(low)
+    copies = copied(filtered, cols)
+
+    onward = jnp.dot(filtered, coupling, preferred_element_type=F32).astype(BF16)
     arrived = lax.ppermute(onward, DOM, [(i, i + 1) for i in range(domains - 1)])
     all_states = lax.all_to_all(copies, "col", 0, 0).reshape(cols * local, rows)
-    (product,) = local_kernel(diag_kernel, [(block, F32)], filtered, diag_blocks)
+    (product,) = local_kernel(product_kernel, [(block, F32)], filtered, diag_blocks)
     peers = ALONG_Y * CORES
     (tiles,) = local_kernel(
         terms_kernel, [((peers, 8, 128), F32)], filtered, product, arrived, all_states

time: 130 us -> 129 us (level)
  matrix products: 0 us -> 4.12 us
  Pallas kernels: 20.7 us -> 17.1 us
  local copies, waits for them, and re-layouts: 4.77 us -> 1.61 us
    pallas_call x11 -> x7, Pallas kernels: 8.49 us -> 4.01 us  [local_kernel(): pl.pallas_call(kernel, out_shape=tuple((jax.ShapeDtypeStruct(shape, dtype...]
    dot_general x0 -> x7, matrix products: none -> 4.12 us  [the longest x3 2.25 us: body(): lax.dot_general(next_block, coupling, TRANSPOSED, preferred_element_type=...]
    unnamed x10 -> x8, local copies, waits for them, and re-layouts: 4.77 us -> 1.61 us
  transfers between devices with their start and end apart: 5 -> 5, of which waited for: 3 -> 4; matrix products, arithmetic and copies ran while one was open for 0% -> 0% of each run, Pallas kernels for 3% -> 3%
where the time goes in v7:
time: 129 us; the launch traced here: 128 us
  blocking collectives  68 us (53%)
  starting transfers between devices  21.1 us (16%)
  Pallas kernels  17.1 us (13%)
  waiting for transfers between devices  14.2 us (11%)
  matrix products  4.12 us (3%)
  local copies, waits for them, and re-layouts  1.61 us (1%)
  between operations  1.58 us (1%)
    all_to_all x1, blocking collectives, body(): parts = lax.all_to_all(tiles, ('y', 'core'), 0, 0)  16.9 us
    all_to_all x1, blocking collectives, body(): shares = lax.all_to_all(copies, ('y', 'col'), 0, 0)  16.3 us
    all_gather x3, blocking collectives, body(): both = lax.all_gather(on, 'core')  15.7 us
    all_to_all x1, blocking collectives, body(): parts = lax.all_to_all(copies, 'x', 0, 0)  13.8 us
    pallas_call x1, Pallas kernels, finish(): pl.pallas_call(finish_kernel, out_shape=(jax.ShapeDtypeStruct((local, row...  12.2 us
    all_to_all x1, waiting for transfers between devices, body(): all_states = lax.all_to_all(copies, 'col', 0, 0).reshape(cols * local, rows)  11.2 us
    ppermute x3, starting transfers between devices, body(): over = lax.ppermute(over, DOM, across_pairs(domains))  9.14 us
    all_to_all x1, starting transfers between devices, body(): all_states = lax.all_to_all(copies, 'col', 0, 0).reshape(cols * local, rows)  6.99 us
  transfers between devices with their start and end apart: 5, of which 4 were waited for; matrix products, arithmetic and copies ran while one was open for 0% of the time, Pallas kernels for 3%

profile of v7, /device:TPU:1, one launch (start us, length us, event | category | flops | bytes accessed | tf_op | source)
XLA Modules:
  0.0 128.5 jit_solution(8117696817447787890)
XLA Ops:
  0.6 0.0 copy-start
  1.5 0.9 broadcast_select_fusion.2.low_ref
  2.3 0.0 copy-done
  2.3 0.5 convert_select_fusion
  2.8 4.7 %collective-permute-start = (f32[32,1024]{1,0:T(8,128)S(1)}, f32[32,1024]{1,0:T(8,128)S(1)}, u32[]{:S(2)}, u32[]{:S(2)}) collective-permute-start(f32[32,1024]{1,0:T(8,128)S(1)} %get-tuple-element.24), channel_id=1, source_target_pairs={{8,16},{16,8},{24,32},{32,24},{40,48},{48,40},{56,64},{64,56},{72,... | collective-permute-start | bytes 393224 | tf_op jit(solution)/shard_map/ppermute | solution.py:247
  7.5 11.7 %all-gather = f32[64,1024]{1,0:T(8,128)S(1)} all-gather(f32[32,1024]{1,0:T(8,128)S(1)} %get-tuple-element.25), channel_id=2, replica_groups=mesh['x'=8,'y'=8,'core'=2,'col'=8] {'core'}, dimensions={0}, use_global_device_ids=true | all-gather | bytes 393216 | tf_op jit(solution)/shard_map/all_gather | solution.py:248
  19.3 0.0 copy-start.1
  19.3 1.6 %copy-done.1 = bf16[1024,1024]{1,0:T(8,128)(2,1)S(1)} copy-done((bf16[1024,1024]{1,0:T(8,128)(2,1)S(1)}, bf16[1024,1024]{1,0:T(8,128)(2,1)}, u32[]{:S(2)}) %copy-start.1) | copy-done | bytes 2097176
  20.9 1.1 shard_map.59
  21.9 0.0 collective-permute-done
  21.9 0.7 multiply_convert_fusion
  22.7 0.0 copy-start.2
  22.7 0.5 multiply_select_fusion
  23.2 2.1 %collective-permute-start.1 = (f32[32,1024]{1,0:T(8,128)S(1)}, f32[32,1024]{1,0:T(8,128)S(1)}, u32[]{:S(2)}, u32[]{:S(2)}) collective-permute-start(f32[32,1024]{1,0:T(8,128)S(1)} %get-tuple-element.22), channel_id=1, source_target_pairs={{8,16},{16,8},{24,32},{32,24},{40,48},{48,40},{56,64},{64,56},{72,... | collective-permute-start | bytes 393224 | tf_op jit(solution)/shard_map/ppermute | solution.py:247
  25.2 2.0 %all-gather.1 = f32[64,1024]{1,0:T(8,128)S(1)} all-gather(f32[32,1024]{1,0:T(8,128)S(1)} %get-tuple-element.23), channel_id=3, replica_groups=mesh['x'=8,'y'=8,'core'=2,'col'=8] {'core'}, dimensions={0}, use_global_device_ids=true | all-gather | bytes 393216 | tf_op jit(solution)/shard_map/all_gather | solution.py:248
  27.2 0.0 copy-done.2
  27.2 1.1 shard_map.60
  28.3 1.3 collective-permute-done.1
  29.6 0.8 fusion.35
  30.4 0.5 broadcast_select_fusion.1
  30.8 2.4 %collective-permute-start.2 = (f32[32,1024]{1,0:T(8,128)S(1)}, f32[32,1024]{1,0:T(8,128)S(1)}, u32[]{:S(2)}, u32[]{:S(2)}) collective-permute-start(f32[32,1024]{1,0:T(8,128)S(1)} %get-tuple-element.20), channel_id=1, source_target_pairs={{8,16},{16,8},{24,32},{32,24},{40,48},{48,40},{56,64},{64,56},{72,... | collective-permute-start | bytes 393224 | tf_op jit(solution)/shard_map/ppermute | solution.py:247
  33.2 2.0 %all-gather.2 = f32[64,1024]{1,0:T(8,128)S(1)} all-gather(f32[32,1024]{1,0:T(8,128)S(1)} %get-tuple-element.21), channel_id=4, replica_groups=mesh['x'=8,'y'=8,'core'=2,'col'=8] {'core'}, dimensions={0}, use_global_device_ids=true | all-gather | bytes 393216 | tf_op jit(solution)/shard_map/all_gather | solution.py:248
  35.2 1.1 shard_map.61
  36.3 0.8 collective-permute-done.2
  37.1 0.8 fusion.6.left_ref.array_ref.filtered_ref
  37.9 0.9 shard_map.63
  38.8 7.0 %all-to-all-start = ((bf16[8,32,1024]{2,1,0:T(8,128)(2,1)}), bf16[8,32,1024]{2,1,0:T(8,128)(2,1)S(1)}, u32[]{:S(2)}, u32[]{:S(2)}) async-start(bf16[8,32,1024]{2,1,0:T(8,128)(2,1)} %shard_map.63), calls=%async_computation | async-start | bytes 1048576 | tf_op jit(solution)/shard_map/all_to_all | solution.py:267
  45.7 0.0 copy-start.3
  45.8 0.5 convolution_convert_fusion
  46.2 5.0 %collective-permute-start.3 = (bf16[32,1024]{1,0:T(8,128)(2,1)S(1)}, bf16[32,1024]{1,0:T(8,128)(2,1)S(1)}, u32[]{:S(2)}, u32[]{:S(2)}) collective-permute-start(bf16[32,1024]{1,0:T(8,128)(2,1)S(1)} %convolution_convert_fusion), channel_id=1, source_target_pairs={{0,8},{8,16},{16,24},{24,32},{32,40},{40,48},{48,56},{56,64},{64,7... | collective-permute-start | bytes 196616 | tf_op jit(solution)/shard_map/ppermute | solution.py:266
  51.2 0.0 copy-done.3
  51.2 0.5 shard_map.62.product_ref
  51.7 0.8 collective-permute-done.3.arrived_ref
  52.5 11.2 %all-to-all-done = bf16[8,32,1024]{2,1,0:T(8,128)(2,1)S(1)} async-done(((bf16[8,32,1024]{2,1,0:T(8,128)(2,1)}), bf16[8,32,1024]{2,1,0:T(8,128)(2,1)S(1)}, u32[]{:S(2)}, u32[]{:S(2)}) %all-to-all-start) | async-done | bytes 524320 | tf_op jit(solution)/shard_map/all_to_all | solution.py:267
  63.7 0.3 shard_map.64
  64.0 16.9 %all_to_all.20.parts_ref = f32[16,8,128]{2,1,0:T(8,128)S(1)} all-to-all(f32[16,8,128]{2,1,0:T(8,128)S(1)} %shard_map.64), channel_id=1, replica_groups=mesh['x'=8,'y'=8,'core'=2,'col'=8] {'y','core'}, dimensions={0} | all-to-all | bytes 131072 | tf_op jit(solution)/shard_map/all_to_all | solution.py:273
  80.9 13.8 %all_to_all.21.parts_ref = f32[8,8,128]{2,1,0:T(8,128)S(1)} all-to-all(f32[8,8,128]{2,1,0:T(8,128)S(1)} %shard_map.65), channel_id=1, replica_groups=mesh['x'=8,'y'=8,'core'=2,'col'=8] {'x'}, dimensions={0} | all-to-all | bytes 65536 | tf_op jit(solution)/shard_map/all_to_all | solution.py:275
  94.7 16.3 %all_to_all.22 = f32[64,8,128]{2,1,0:T(8,128)S(1)} all-to-all(f32[64,8,128]{2,1,0:T(8,128)S(1)} %shard_map.66), channel_id=1, replica_groups=mesh['x'=8,'y'=8,'core'=2,'col'=8] {'y','col'}, dimensions={0} | all-to-all | bytes 524288 | tf_op jit(solution)/shard_map/all_to_all | solution.py:277
  111.0 5.3 %all-gather.3 = f32[128,8,128]{2,1,0:T(8,128)S(1)} all-gather(f32[64,8,128]{2,1,0:T(8,128)S(1)} %all_to_all.22), channel_id=5, replica_groups=mesh['x'=8,'y'=8,'core'=2,'col'=8] {'core'}, dimensions={0}, use_global_device_ids=true | all-gather | bytes 786432 | tf_op jit(solution)/shard_map/all_gather | solution.py:278
  116.3 12.2 %shard_map.67 = (f32[32,1024]{1,0:T(8,128)}, f32[256,256]{1,0:T(8,128)}) custom-call(s32[1]{0:T(128)} %bitcast.2.col_ref, f32[2,8,8,8,128]{4,3,2,1,0:T(8,128)S(1)} %bitcast.79, bf16[256,1024]{1,0:T(8,128)(2,1)S(1)} %bitcast.78), custom_call_target="tpu_custom_call" | custom-call | flops 200000000 | bytes 2097152 | tf_op jit(solution)/shard_map/pallas_call | solution.py:147
  (3 shorter events, 0.1 us)
Async XLA Ops:
  0.6 1.7 %copy-start = (bf16[1024,1024]{1,0:T(8,128)(2,1)S(1)}, bf16[1024,1024]{1,0:T(8,128)(2,1)}, u32[]{:S(2)}) copy-start(bf16[1024,1024]{1,0:T(8,128)(2,1)} %param.6) | copy-start | bytes 6291460
  2.8 19.1 %collective-permute-start = (f32[32,1024]{1,0:T(8,128)S(1)}, f32[32,1024]{1,0:T(8,128)S(1)}, u32[]{:S(2)}, u32[]{:S(2)}) collective-permute-start(f32[32,1024]{1,0:T(8,128)S(1)} %get-tuple-element.24), channel_id=1, source_target_pairs={{8,16},{16,8},{24,32},{32,24},{40,48},{48,40},{56,64},{64,56},{72,... | collective-permute-start | bytes 393224 | tf_op jit(solution)/shard_map/ppermute | solution.py:247
  19.3 1.6 %copy-start.1 = (bf16[1024,1024]{1,0:T(8,128)(2,1)S(1)}, bf16[1024,1024]{1,0:T(8,128)(2,1)}, u32[]{:S(2)}) copy-start(bf16[1024,1024]{1,0:T(8,128)(2,1)} %right_ref.1) | copy-start | bytes 6291460
  22.7 4.5 %copy-start.2 = (bf16[1024,1024]{1,0:T(8,128)(2,1)S(1)}, bf16[1024,1024]{1,0:T(8,128)(2,1)}, u32[]{:S(2)}) copy-start(bf16[1024,1024]{1,0:T(8,128)(2,1)} %right_ref.1) | copy-start | bytes 6291460
  23.2 6.4 %collective-permute-start.1 = (f32[32,1024]{1,0:T(8,128)S(1)}, f32[32,1024]{1,0:T(8,128)S(1)}, u32[]{:S(2)}, u32[]{:S(2)}) collective-permute-start(f32[32,1024]{1,0:T(8,128)S(1)} %get-tuple-element.22), channel_id=1, source_target_pairs={{8,16},{16,8},{24,32},{32,24},{40,48},{48,40},{56,64},{64,56},{72,... | collective-permute-start | bytes 393224 | tf_op jit(solution)/shard_map/ppermute | solution.py:247
  30.8 6.3 %collective-permute-start.2 = (f32[32,1024]{1,0:T(8,128)S(1)}, f32[32,1024]{1,0:T(8,128)S(1)}, u32[]{:S(2)}, u32[]{:S(2)}) collective-permute-start(f32[32,1024]{1,0:T(8,128)S(1)} %get-tuple-element.20), channel_id=1, source_target_pairs={{8,16},{16,8},{24,32},{32,24},{40,48},{48,40},{56,64},{64,56},{72,... | collective-permute-start | bytes 393224 | tf_op jit(solution)/shard_map/ppermute | solution.py:247
  38.8 25.0 %all-to-all-start = ((bf16[8,32,1024]{2,1,0:T(8,128)(2,1)}), bf16[8,32,1024]{2,1,0:T(8,128)(2,1)S(1)}, u32[]{:S(2)}, u32[]{:S(2)}) async-start(bf16[8,32,1024]{2,1,0:T(8,128)(2,1)} %shard_map.63), calls=%async_computation | async-start | bytes 1048576 | tf_op jit(solution)/shard_map/all_to_all | solution.py:267
  45.7 5.5 %copy-start.3 = (bf16[1024,1024]{1,0:T(8,128)(2,1)S(1)}, bf16[1024,1024]{1,0:T(8,128)(2,1)}, u32[]{:S(2)}) copy-start(bf16[1024,1024]{1,0:T(8,128)(2,1)} %right_ref.1) | copy-start | bytes 6291460
  46.2 6.3 %collective-permute-start.3 = (bf16[32,1024]{1,0:T(8,128)(2,1)S(1)}, bf16[32,1024]{1,0:T(8,128)(2,1)S(1)}, u32[]{:S(2)}, u32[]{:S(2)}) collective-permute-start(bf16[32,1024]{1,0:T(8,128)(2,1)S(1)} %convolution_convert_fusion), channel_id=1, source_target_pairs={{0,8},{8,16},{16,24},{24,32},{32,40},{40,48},{48,56},{56,64},{64,7... | collective-permute-start | bytes 196616 | tf_op jit(solution)/shard_map/ppermute | solution.py:266

commit v8 on v7

--- a/solution.py
+++ b/solution.py
@@ -109,7 +109,10 @@
     return jnp.sum(error * error)
 
 
-def finish_kernel(col_ref, sums_ref, all_ref, basis_ref, reduced_ref, a_ref, q_ref, x_ref, inv_ref):
+def finish_kernel(
+    col_ref, sums_ref, all_ref, basis_ref, reduced_ref,
+    a_ref, q_ref, x_ref, inv_ref, proj_high_ref, proj_low_ref,
+):
     cores, along, cols, eight, lanes = sums_ref.shape
     local = basis_ref.shape[0]
     tiles = cores * along
@@ -121,23 +124,27 @@
         for z in range(cols):
             top = z * local + block * eight
             target[top : top + eight, half * lanes : (half + 1) * lanes] = sums_ref[t % cores, t // cores, z]
+    proj = q_ref[...]
+    proj_high_ref[...], proj_low_ref[...] = halves(0.5 * (proj + proj.T))
+
+    def outputs():
+        proj = proj_high_ref[...], proj_low_ref[...]
+        inverse = halves(inv_ref[...])
+        left = product_of_halves(inverse, proj, PLAIN)
+        reduced_ref[...] = product_of_halves(halves(left), inverse, TRANSPOSED)
+        scale = math.sqrt(ALONG_X * ALONG_Y * CORES * basis_ref.shape[1])
+        mine = scale * inv_ref[pl.ds(pl.multiple_of(col_ref[0] * local, local), local), :]
+        high, low = halves(mine)
+        states = all_ref[...]
+        basis_ref[...] = product(high, states, PLAIN) + product(low, states, PLAIN)
+
     residual = newton_inverse(a_ref[...], inv_ref)
+    outputs()
 
     @pl.when(jnp.logical_not(residual < CLOSE))
     def _():
         cholesky_inverse(a_ref, x_ref, inv_ref)
-
-    proj = q_ref[...]
-    inverse = halves(inv_ref[...])
-    left = product_of_halves(inverse, halves(0.5 * (proj + proj.T)), PLAIN)
-    reduced_ref[...] = product_of_halves(halves(left), inverse, TRANSPOSED)
-    scale = math.sqrt(ALONG_X * ALONG_Y * CORES * basis_ref.shape[1])
-    mine = scale * inv_ref[pl.ds(pl.multiple_of(col_ref[0] * local, local), local), :]
-    high, low = halves(mine)
-    states = all_ref[...]
-    basis_ref[...] = jnp.dot(high, states, preferred_element_type=F32) + jnp.dot(
-        low, states, preferred_element_type=F32
-    )
+        outputs()
 
 
 def finish(col, sums, all_states, local):
@@ -152,7 +159,7 @@
         ),
         in_specs=[pl.BlockSpec(memory_space=pltpu.SMEM), vmem, vmem],
         out_specs=(vmem, vmem),
-        scratch_shapes=[square] * 4,
+        scratch_shapes=[square] * 4 + [pltpu.VMEM((total, total), BF16)] * 2,
         compiler_params=pltpu.CompilerParams(vmem_limit_bytes=32 * 2**20),
         cost_estimate=pl.CostEstimate(flops=2 * 10**8, bytes_accessed=2**21, transcendentals=0),
     )(col, sums, all_states)

time: 129 us -> 129 us (level)
  no operation moved by 1% of the time
where the time goes in v8:
time: 129 us
  blocking collectives  68 us (53%)
  starting transfers between devices  21.1 us (16%)
  Pallas kernels  17.5 us (14%)
  waiting for transfers between devices  14.2 us (11%)
  matrix products  4.12 us (3%)
  local copies, waits for them, and re-layouts  1.61 us (1%)
  between operations  1.58 us (1%)
    all_to_all x1, blocking collectives, body(): parts = lax.all_to_all(tiles, ('y', 'core'), 0, 0)  16.9 us
    all_to_all x1, blocking collectives, body(): shares = lax.all_to_all(copies, ('y', 'col'), 0, 0)  16.3 us
    all_gather x3, blocking collectives, body(): both = lax.all_gather(on, 'core')  15.7 us
    all_to_all x1, blocking collectives, body(): parts = lax.all_to_all(copies, 'x', 0, 0)  13.8 us
    pallas_call x1, Pallas kernels, finish(): pl.pallas_call(finish_kernel, out_shape=(jax.ShapeDtypeStruct((local, row...  12.7 us
    all_to_all x1, waiting for transfers between devices, body(): all_states = lax.all_to_all(copies, 'col', 0, 0).reshape(cols * local, rows)  11.2 us
    ppermute x3, starting transfers between devices, body(): over = lax.ppermute(over, DOM, across_pairs(domains))  9.14 us
    all_to_all x1, starting transfers between devices, body(): all_states = lax.all_to_all(copies, 'col', 0, 0).reshape(cols * local, rows)  6.99 us
  transfers between devices with their start and end apart: 5, of which 4 were waited for; matrix products, arithmetic and copies ran while one was open for 0% of the time, Pallas kernels for 3%

profile of v8, /device:TPU:1, one launch (start us, length us, event | category | flops | bytes accessed | tf_op | source)
XLA Modules:
  0.0 128.9 jit_solution(17072988624798617440)
XLA Ops:
  0.6 0.0 copy-start
  1.5 0.9 broadcast_select_fusion.2.low_ref
  2.3 0.0 copy-done
  2.3 0.5 convert_select_fusion
  2.8 4.7 %collective-permute-start = (f32[32,1024]{1,0:T(8,128)S(1)}, f32[32,1024]{1,0:T(8,128)S(1)}, u32[]{:S(2)}, u32[]{:S(2)}) collective-permute-start(f32[32,1024]{1,0:T(8,128)S(1)} %get-tuple-element.24), channel_id=1, source_target_pairs={{8,16},{16,8},{24,32},{32,24},{40,48},{48,40},{56,64},{64,56},{72,... | collective-permute-start | bytes 393224 | tf_op jit(solution)/shard_map/ppermute | solution.py:254
  7.5 11.7 %all-gather = f32[64,1024]{1,0:T(8,128)S(1)} all-gather(f32[32,1024]{1,0:T(8,128)S(1)} %get-tuple-element.25), channel_id=2, replica_groups=mesh['x'=8,'y'=8,'core'=2,'col'=8] {'core'}, dimensions={0}, use_global_device_ids=true | all-gather | bytes 393216 | tf_op jit(solution)/shard_map/all_gather | solution.py:255
  19.3 0.0 copy-start.1
  19.3 1.6 %copy-done.1 = bf16[1024,1024]{1,0:T(8,128)(2,1)S(1)} copy-done((bf16[1024,1024]{1,0:T(8,128)(2,1)S(1)}, bf16[1024,1024]{1,0:T(8,128)(2,1)}, u32[]{:S(2)}) %copy-start.1) | copy-done | bytes 2097176
  20.9 1.1 shard_map.59
  21.9 0.0 collective-permute-done
  21.9 0.7 multiply_convert_fusion
  22.7 0.0 copy-start.2
  22.7 0.5 multiply_select_fusion
  23.2 2.1 %collective-permute-start.1 = (f32[32,1024]{1,0:T(8,128)S(1)}, f32[32,1024]{1,0:T(8,128)S(1)}, u32[]{:S(2)}, u32[]{:S(2)}) collective-permute-start(f32[32,1024]{1,0:T(8,128)S(1)} %get-tuple-element.22), channel_id=1, source_target_pairs={{8,16},{16,8},{24,32},{32,24},{40,48},{48,40},{56,64},{64,56},{72,... | collective-permute-start | bytes 393224 | tf_op jit(solution)/shard_map/ppermute | solution.py:254
  25.2 2.0 %all-gather.1 = f32[64,1024]{1,0:T(8,128)S(1)} all-gather(f32[32,1024]{1,0:T(8,128)S(1)} %get-tuple-element.23), channel_id=3, replica_groups=mesh['x'=8,'y'=8,'core'=2,'col'=8] {'core'}, dimensions={0}, use_global_device_ids=true | all-gather | bytes 393216 | tf_op jit(solution)/shard_map/all_gather | solution.py:255
  27.2 0.0 copy-done.2
  27.2 1.1 shard_map.60
  28.3 1.3 collective-permute-done.1
  29.6 0.8 fusion.35
  30.4 0.5 broadcast_select_fusion.1
  30.8 2.4 %collective-permute-start.2 = (f32[32,1024]{1,0:T(8,128)S(1)}, f32[32,1024]{1,0:T(8,128)S(1)}, u32[]{:S(2)}, u32[]{:S(2)}) collective-permute-start(f32[32,1024]{1,0:T(8,128)S(1)} %get-tuple-element.20), channel_id=1, source_target_pairs={{8,16},{16,8},{24,32},{32,24},{40,48},{48,40},{56,64},{64,56},{72,... | collective-permute-start | bytes 393224 | tf_op jit(solution)/shard_map/ppermute | solution.py:254
  33.2 2.0 %all-gather.2 = f32[64,1024]{1,0:T(8,128)S(1)} all-gather(f32[32,1024]{1,0:T(8,128)S(1)} %get-tuple-element.21), channel_id=4, replica_groups=mesh['x'=8,'y'=8,'core'=2,'col'=8] {'core'}, dimensions={0}, use_global_device_ids=true | all-gather | bytes 393216 | tf_op jit(solution)/shard_map/all_gather | solution.py:255
  35.2 1.1 shard_map.61
  36.3 0.8 collective-permute-done.2
  37.1 0.8 fusion.6.left_ref.array_ref.filtered_ref
  37.9 0.9 shard_map.63
  38.8 7.0 %all-to-all-start = ((bf16[8,32,1024]{2,1,0:T(8,128)(2,1)}), bf16[8,32,1024]{2,1,0:T(8,128)(2,1)S(1)}, u32[]{:S(2)}, u32[]{:S(2)}) async-start(bf16[8,32,1024]{2,1,0:T(8,128)(2,1)} %shard_map.63), calls=%async_computation | async-start | bytes 1048576 | tf_op jit(solution)/shard_map/all_to_all | solution.py:274
  45.7 0.0 copy-start.3
  45.8 0.5 convolution_convert_fusion
  46.2 5.0 %collective-permute-start.3 = (bf16[32,1024]{1,0:T(8,128)(2,1)S(1)}, bf16[32,1024]{1,0:T(8,128)(2,1)S(1)}, u32[]{:S(2)}, u32[]{:S(2)}) collective-permute-start(bf16[32,1024]{1,0:T(8,128)(2,1)S(1)} %convolution_convert_fusion), channel_id=1, source_target_pairs={{0,8},{8,16},{16,24},{24,32},{32,40},{40,48},{48,56},{56,64},{64,7... | collective-permute-start | bytes 196616 | tf_op jit(solution)/shard_map/ppermute | solution.py:273
  51.2 0.0 copy-done.3
  51.2 0.5 shard_map.62.product_ref
  51.7 0.8 collective-permute-done.3.arrived_ref
  52.5 11.2 %all-to-all-done = bf16[8,32,1024]{2,1,0:T(8,128)(2,1)S(1)} async-done(((bf16[8,32,1024]{2,1,0:T(8,128)(2,1)}), bf16[8,32,1024]{2,1,0:T(8,128)(2,1)S(1)}, u32[]{:S(2)}, u32[]{:S(2)}) %all-to-all-start) | async-done | bytes 524320 | tf_op jit(solution)/shard_map/all_to_all | solution.py:274
  63.7 0.3 shard_map.64
  64.0 16.9 %all_to_all.20.parts_ref = f32[16,8,128]{2,1,0:T(8,128)S(1)} all-to-all(f32[16,8,128]{2,1,0:T(8,128)S(1)} %shard_map.64), channel_id=1, replica_groups=mesh['x'=8,'y'=8,'core'=2,'col'=8] {'y','core'}, dimensions={0} | all-to-all | bytes 131072 | tf_op jit(solution)/shard_map/all_to_all | solution.py:280
  80.9 13.8 %all_to_all.21.parts_ref = f32[8,8,128]{2,1,0:T(8,128)S(1)} all-to-all(f32[8,8,128]{2,1,0:T(8,128)S(1)} %shard_map.65), channel_id=1, replica_groups=mesh['x'=8,'y'=8,'core'=2,'col'=8] {'x'}, dimensions={0} | all-to-all | bytes 65536 | tf_op jit(solution)/shard_map/all_to_all | solution.py:282
  94.7 16.3 %all_to_all.22 = f32[64,8,128]{2,1,0:T(8,128)S(1)} all-to-all(f32[64,8,128]{2,1,0:T(8,128)S(1)} %shard_map.66), channel_id=1, replica_groups=mesh['x'=8,'y'=8,'core'=2,'col'=8] {'y','col'}, dimensions={0} | all-to-all | bytes 524288 | tf_op jit(solution)/shard_map/all_to_all | solution.py:284
  111.0 5.3 %all-gather.3 = f32[128,8,128]{2,1,0:T(8,128)S(1)} all-gather(f32[64,8,128]{2,1,0:T(8,128)S(1)} %all_to_all.22), channel_id=5, replica_groups=mesh['x'=8,'y'=8,'core'=2,'col'=8] {'core'}, dimensions={0}, use_global_device_ids=true | all-gather | bytes 786432 | tf_op jit(solution)/shard_map/all_gather | solution.py:285
  116.3 12.7 %shard_map.67 = (f32[32,1024]{1,0:T(8,128)}, f32[256,256]{1,0:T(8,128)}) custom-call(s32[1]{0:T(128)} %bitcast.2.col_ref, f32[2,8,8,8,128]{4,3,2,1,0:T(8,128)S(1)} %bitcast.79, bf16[256,1024]{1,0:T(8,128)(2,1)S(1)} %bitcast.78), custom_call_target="tpu_custom_call" | custom-call | flops 200000000 | bytes 2097152 | tf_op jit(solution)/shard_map/pallas_call | solution.py:154
  (3 shorter events, 0.1 us)
Async XLA Ops:
  0.6 1.7 %copy-start = (bf16[1024,1024]{1,0:T(8,128)(2,1)S(1)}, bf16[1024,1024]{1,0:T(8,128)(2,1)}, u32[]{:S(2)}) copy-start(bf16[1024,1024]{1,0:T(8,128)(2,1)} %param.6) | copy-start | bytes 6291460
  2.8 19.1 %collective-permute-start = (f32[32,1024]{1,0:T(8,128)S(1)}, f32[32,1024]{1,0:T(8,128)S(1)}, u32[]{:S(2)}, u32[]{:S(2)}) collective-permute-start(f32[32,1024]{1,0:T(8,128)S(1)} %get-tuple-element.24), channel_id=1, source_target_pairs={{8,16},{16,8},{24,32},{32,24},{40,48},{48,40},{56,64},{64,56},{72,... | collective-permute-start | bytes 393224 | tf_op jit(solution)/shard_map/ppermute | solution.py:254
  19.3 1.6 %copy-start.1 = (bf16[1024,1024]{1,0:T(8,128)(2,1)S(1)}, bf16[1024,1024]{1,0:T(8,128)(2,1)}, u32[]{:S(2)}) copy-start(bf16[1024,1024]{1,0:T(8,128)(2,1)} %right_ref.1) | copy-start | bytes 6291460
  22.7 4.5 %copy-start.2 = (bf16[1024,1024]{1,0:T(8,128)(2,1)S(1)}, bf16[1024,1024]{1,0:T(8,128)(2,1)}, u32[]{:S(2)}) copy-start(bf16[1024,1024]{1,0:T(8,128)(2,1)} %right_ref.1) | copy-start | bytes 6291460
  23.2 6.4 %collective-permute-start.1 = (f32[32,1024]{1,0:T(8,128)S(1)}, f32[32,1024]{1,0:T(8,128)S(1)}, u32[]{:S(2)}, u32[]{:S(2)}) collective-permute-start(f32[32,1024]{1,0:T(8,128)S(1)} %get-tuple-element.22), channel_id=1, source_target_pairs={{8,16},{16,8},{24,32},{32,24},{40,48},{48,40},{56,64},{64,56},{72,... | collective-permute-start | bytes 393224 | tf_op jit(solution)/shard_map/ppermute | solution.py:254
  30.8 6.3 %collective-permute-start.2 = (f32[32,1024]{1,0:T(8,128)S(1)}, f32[32,1024]{1,0:T(8,128)S(1)}, u32[]{:S(2)}, u32[]{:S(2)}) collective-permute-start(f32[32,1024]{1,0:T(8,128)S(1)} %get-tuple-element.20), channel_id=1, source_target_pairs={{8,16},{16,8},{24,32},{32,24},{40,48},{48,40},{56,64},{64,56},{72,... | collective-permute-start | bytes 393224 | tf_op jit(solution)/shard_map/ppermute | solution.py:254
  38.8 25.0 %all-to-all-start = ((bf16[8,32,1024]{2,1,0:T(8,128)(2,1)}), bf16[8,32,1024]{2,1,0:T(8,128)(2,1)S(1)}, u32[]{:S(2)}, u32[]{:S(2)}) async-start(bf16[8,32,1024]{2,1,0:T(8,128)(2,1)} %shard_map.63), calls=%async_computation | async-start | bytes 1048576 | tf_op jit(solution)/shard_map/all_to_all | solution.py:274
  45.7 5.5 %copy-start.3 = (bf16[1024,1024]{1,0:T(8,128)(2,1)S(1)}, bf16[1024,1024]{1,0:T(8,128)(2,1)}, u32[]{:S(2)}) copy-start(bf16[1024,1024]{1,0:T(8,128)(2,1)} %right_ref.1) | copy-start | bytes 6291460
  46.2 6.3 %collective-permute-start.3 = (bf16[32,1024]{1,0:T(8,128)(2,1)S(1)}, bf16[32,1024]{1,0:T(8,128)(2,1)S(1)}, u32[]{:S(2)}, u32[]{:S(2)}) collective-permute-start(bf16[32,1024]{1,0:T(8,128)(2,1)S(1)} %convolution_convert_fusion), channel_id=1, source_target_pairs={{0,8},{8,16},{16,24},{24,32},{32,40},{40,48},{48,56},{56,64},{64,7... | collective-permute-start | bytes 196616 | tf_op jit(solution)/shard_map/ppermute | solution.py:273
